TPU v7x, 32 devices: a whole 2x2x4 slice. The times are simulated.
32 devices in a mesh: group: 2 (over y), wide: 4 (over z), narrow: 2 (over x), sub: 2 (over core).
Axes of the slice: x: 2, y: 2, z: 4, core: 2. Of those that a mesh axis runs over, the one named last changes fastest.
Arguments:
- amplitudes: bfloat16 [64, 2048, 2048], P(('group', 'wide'), None, ('narrow', 'sub')), parts along dimension 0, may hold values from -6 to 6
- t_mask: int32 [64, 32, 32], P(('group', 'wide'), None, ('narrow', 'sub')), parts along dimension 0, may hold values 0 or 1
- integrals: bfloat16 [4, 2048, 2048], P('group', 'narrow', 'sub'), parts along dimension 0, may hold values from -0.09375 to 0.09375
- w_mask: int32 [4, 32, 32], P('group', 'narrow', 'sub'), parts along dimension 0, may hold values 0 or 1
- owner_map: int32 [32], replicated, may hold values from 0 to 31, each once
Outputs:
- residual: bfloat16 [32, 2048, 2048], P(('group', 'narrow'), 'wide', 'sub'), parts along dimension 0
There are 2 independent parts, one for each index of `group`. A program takes and returns all parts, laid end to end along the dimension named above; an argument that names none is the same for every part. Nothing has to cross between parts.
Inputs may be any that keep to these rules, and one draw needn't show every extreme that they name: `owner_map`: each virtual tile appears exactly once.
All inputs are finite; a program needn't handle non-finite values. No bound on the sum of `t_mask` or of `w_mask` on one device may be relied on, other than what follows from the above.
Results may differ from a plain program's by a relative error of at most 0.0052.
Values may be sent and summed in bfloat16 or wider, within the bound.
No kernel may reach another device: no remote copies, remote signals or barrier semaphores. Data moves between devices by JAX's collectives and lax.ppermute only.
A program may use at most 320 MiB of HBM per device.

v0:
```python
import jax
import jax.numpy as jnp
from jax import lax
from jax.sharding import PartitionSpec as P


def regroup_rows(amps, owner_map, tile_size):
    pair_count, virt_count, c_count = amps.shape
    ordered = jnp.take(
        amps.reshape(pair_count, virt_count // tile_size, tile_size, c_count), owner_map, axis=1
    )
    ordered = ordered.reshape(pair_count, virt_count, c_count)
    return lax.all_to_all(ordered, "wide", split_axis=1, concat_axis=0, tiled=True)


def join_halves(amps):
    return lax.all_gather(amps, "sub", axis=2, tiled=True)


def shards(amplitudes, t_mask, integrals, w_mask, owner_map):
    tile_count = owner_map.shape[0]
    pair_here, virt_count, c_here = amplitudes.shape
    tile_size = virt_count // tile_count
    t_scale = t_mask.astype(jnp.bfloat16)
    masked_t = (
        amplitudes.reshape(pair_here, tile_count, tile_size, t_mask.shape[2], tile_size)
        * t_scale[:, :, None, :, None]
    )
    masked_t = masked_t.reshape(pair_here, virt_count, c_here)
    k_count, c_rows, b_cols = integrals.shape
    w_scale = w_mask.astype(jnp.bfloat16)
    masked_w = (
        integrals.reshape(k_count, w_mask.shape[1], tile_size, w_mask.shape[2], tile_size)
        * w_scale[:, :, None, :, None]
    )
    masked_w = masked_w.reshape(k_count, c_rows, b_cols)
    regrouped = join_halves(regroup_rows(masked_t, owner_map, tile_size))
    pair_count, row_count, col_count = regrouped.shape
    occ_count = pair_count // k_count
    blocks = regrouped.reshape(occ_count, k_count, row_count, col_count)
    partial_value = jnp.einsum(
        "ikac,kcb->iab", blocks, masked_w, preferred_element_type=jnp.float32
    )
    rounded = partial_value.astype(jnp.bfloat16)
    return (
        lax.psum_scatter(rounded, "narrow", scatter_dimension=0, tiled=True)
        .astype(jnp.float32)
        .astype(jnp.bfloat16)
    )


def solution(mesh):
    in_specs = (
        P(("group", "wide"), None, ("narrow", "sub")),
        P(("group", "wide"), None, ("narrow", "sub")),
        P("group", "narrow", "sub"),
        P("group", "narrow", "sub"),
        P(),
    )
    out_specs = P(("group", "narrow"), "wide", "sub")
    return jax.shard_map(shards, mesh=mesh, in_specs=in_specs, out_specs=out_specs, check_vma=False)
```

profile of v0, /device:TPU:8, one launch (start us, length us, event | category | flops | bytes accessed | tf_op | source)
XLA Modules:
  0.0 768.5 jit_solution(4964758062591659845)
XLA Ops:
  6.5 0.7 compare_select_fusion
  7.2 0.7 compare_and_fusion
  7.9 0.8 convert_element_type.11
  8.6 0.1 copy.11
  8.7 0.3 mul.24
  9.1 0.3 mul.25
  9.4 13.8 %broadcast_multiply_fusion = bf16[8,32,64,512]{3,2,1,0:T(8,128)(2,1)} fusion(bf16[8,32,64,512]{3,2,1,0:T(8,128)(2,1)} %bitcast.23, bf16[8,32,512]{2,1,0:T(8,128)(2,1)S(1)} %mul.25), kind=kLoop, calls=%fused_computation.3 | loop fusion | flops 8388608 | bytes 33816576 | tf_op jit(solution)/shard_map/mul | solution.py:26
  23.2 13.1 %gather_fusion = bf16[32,8,64,512]{3,2,1,0:T(8,128)(2,1)} fusion(bf16[8,32,64,512]{3,2,1,0:T(8,128)(2,1)} %broadcast_multiply_fusion, s32[1024]{0:T(1024)S(1)} %pad_clamp_fusion), kind=kCustom, calls=%fused_computation | custom fusion | bytes 33554560 | tf_op jit(solution)/shard_map/jit(_take)/gather | solution.py:9
  36.2 14.0 %copy.12 = bf16[8,32,64,512]{3,2,1,0:T(8,128)(2,1)} copy(bf16[8,32,64,512]{3,2,0,1:T(8,128)(2,1)} %bitcast.21) | data formatting | bytes 33554432 | tf_op jit(solution)/shard_map/jit(_take)/gather | solution.py:9
  50.2 0.1 broadcast_in_dim.18
  50.3 0.1 broadcast_in_dim.19
  50.4 8.7 %bitcast_select_fusion = bf16[8,2048,512]{2,1,0:T(8,128)(2,1)S(1)} fusion(bf16[8,32,64,512]{3,2,1,0:T(8,128)(2,1)} %copy.12, pred[2048]{0:T(1024)(128)(4,1)S(1)} %broadcast_in_dim.19), kind=kLoop, calls=%fused_computation.2 | loop fusion | flops 8388608 | bytes 33556480 | tf_op jit(solution)/shard_map/jit(_take)/select_n | solution.py:9
  59.1 38.0 %copy.13 = bf16[8,2048,512]{2,0,1:T(8,128)(2,1)S(1)} copy(bf16[8,2048,512]{2,1,0:T(8,128)(2,1)S(1)} %bitcast_select_fusion) | data formatting | bytes 33554432 | tf_op jit(solution)/shard_map/jit(_take)/select_n | solution.py:9
  97.1 366.1 %all_to_all.18 = bf16[8,2048,512]{2,0,1:T(8,128)(2,1)S(1)} all-to-all(bf16[8,2048,512]{2,0,1:T(8,128)(2,1)S(1)} %copy.13), channel_id=1, replica_groups=mesh['group'=2,'wide'=4,'narrow'=2,'sub'=2] {'wide'}, dimensions={1} | all-to-all | bytes 33554432 | tf_op jit(solution)/shard_map/all_to_all | solution.py:13
  463.2 11.8 %copy.15 = bf16[4,8,512,512]{3,2,1,0:T(8,128)(2,1)} copy(bf16[4,8,512,512]{3,1,2,0:T(8,128)(2,1)S(1)} %bitcast.22) | data formatting | bytes 33554432 | tf_op jit(solution)/shard_map/all_to_all | solution.py:13
  475.0 0.0 all-gather.2.cloned.1.call-update
  475.0 0.2 reduce-scatter.2.cloned.1.call-start
  475.3 0.5 copy-done
  475.7 4.5 mul.28
  480.3 12.9 %mul.29 = bf16[2,1024,1024]{2,1,0:T(8,128)(2,1)} reshape(bf16[2,16,64,16,64]{4,3,2,1,0:T(8,128)(2,1)} %mul.28) | data formatting | bytes 8388608 | tf_op jit(solution)/shard_map/mul | solution.py:33
  493.2 34.9 %all-gather.2.cloned.1.call-done = bf16[32,512,1024]{2,1,0:T(8,128)(2,1)} async-done(((bf16[32,512,512]{2,1,0:T(8,128)(2,1)}), bf16[32,512,1024]{2,1,0:T(8,128)(2,1)}) %all-gather.2.cloned.1.call-update) | async-done | bytes 33554448 | tf_op jit(solution)/shard_map/all_gather | solution.py:17
  528.1 43.4 %bitcast_convert_fusion = bf16[16,512,1024]{2,1,0:T(8,128)(2,1)} fusion(bf16[16,2,512,1024]{3,2,1,0:T(8,128)(2,1)} %bitcast.24, bf16[2,1024,1024]{2,1,0:T(8,128)(2,1)} %param.7, bf16[2,1024,1024]{2,1,0:T(8,128)(2,1)} %mul.29), kind=kOutput, calls=%fused_computation.1 | convolution fusion | flops 34370224128 | bytes 58720256 | tf_op jit(solution)/shard_map/ikac,kcb->iab/dot_general | solution.py:41
  571.5 0.0 reduce-scatter.2.cloned.1.call-update
  571.5 190.2 %reduce-scatter.2.cloned.1.call-done = bf16[8,512,1024]{2,1,0:T(8,128)(2,1)} async-done(((bf16[16,512,1024]{2,1,0:T(8,128)(2,1)}), bf16[8,512,1024]{2,1,0:T(8,128)(2,1)}) %reduce-scatter.2.cloned.1.call-update) | async-done | bytes 8388624 | tf_op jit(solution)/shard_map/reduce_scatter | solution.py:46
  (4 shorter events, 0.0 us)
Async XLA Ops:
  6.5 521.6 %all-gather.2.cloned.1.call-start = ((), (), s32[]{:S(2)}) async-start(), calls=%async_computation.2 | async-start | bytes 50331648 | tf_op jit(solution)/shard_map/all_gather | solution.py:17
  475.0 0.7 copy-start
  475.0 286.7 %reduce-scatter.2.cloned.1.call-start = ((), (), s32[]{:S(2)}) async-start(), calls=%async_computation.3 | async-start | bytes 25165824 | tf_op jit(solution)/shard_map/reduce_scatter | solution.py:46
Sparse Core Ops, SparseCore 0:
  475.1 52.9 all-gather.1
  571.6 190.0 reduce-scatter.1
where the time goes:
time: 771 us; the launch traced here: 769 us
  blocking collectives  366 us (47%)
  waiting for transfers between devices  225 us (29%)
  local copies, waits for them, and re-layouts  95.7 us (12%)
  matrix products  43.4 us (6%)
  other arithmetic  24.6 us (3%)
  between operations  13.4 us (2%)
    all_to_all x1, blocking collectives, regroup_rows(): lax.all_to_all(ordered, 'wide', split_axis=1, concat_axis=0, tiled=True)  366 us
    reduce_scatter x1, waiting for transfers between devices, shards(): lax.psum_scatter(rounded, 'narrow', scatter_dimension=0, tiled=True)  190 us
    dot_general x1, matrix products, shards(): jnp.einsum('ikac,kcb->iab', blocks, masked_w, preferred_element_type=jnp....  43.4 us
    select_n x1, local copies, waits for them, and re-layouts, regroup_rows(): jnp.take(amps.reshape(pair_count, virt_count // tile_size, tile_size, c_c...  38 us
    all_gather x1, waiting for transfers between devices, join_halves(): return lax.all_gather(amps, 'sub', axis=2, tiled=True)  34.9 us
    gather x2, local copies, waits for them, and re-layouts, regroup_rows(): jnp.take(amps.reshape(pair_count, virt_count // tile_size, tile_size, c_c...  27.1 us
    mul x2, local copies, waits for them, and re-layouts, shards(): integrals.reshape(k_count, w_mask.shape[1], tile_size, w_mask.shape[2], t...  17.5 us
  transfers between devices with their start and end apart: 2, of which 2 were waited for; matrix products, arithmetic and copies ran while one was open for 2% of the time, Pallas kernels for 0%

commit v1 on v0

--- a/solution.py
+++ b/solution.py
@@ -1,7 +1,217 @@
 import jax
 import jax.numpy as jnp
 from jax import lax
+from jax.experimental import pallas as pl
+from jax.experimental.pallas import tpu as pltpu
 from jax.sharding import PartitionSpec as P
+
+BF16 = jnp.bfloat16
+F32 = jnp.float32
+
+SUM_HOME = [(0, 2), (0, 3), (1, 2)]
+SUM_AWAY = [(1, 3), (2, 2), (2, 3)]
+SUM_LAST = [(3, 2), (3, 3)]
+NEAR = [(0, 1), (1, 1), (2, 1), (3, 1)]
+OWN = [(0, 0), (1, 0), (2, 0), (3, 0)]
+
+
+def add(left, right):
+    return (left.astype(F32) + right.astype(F32)).astype(BF16)
+
+
+def order_tiles(meta, owner_map, amps, t_scale, tile_size):
+    block_count = meta.shape[1]
+    pair_count, virt_count, c_here = amps.shape
+    tile_count = owner_map.shape[0]
+    tiles = tile_count // 4
+    k_count = 2
+
+    def tile_of(j, g, meta, owner):
+        return owner[meta[1, g] * tiles + j]
+
+    def kernel(meta, owner, scale_ref, *refs):
+        out_ref = refs[-1]
+        g = pl.program_id(0)
+        for j in range(tiles):
+            tile = tile_of(j, g, meta, owner)
+            for k in range(k_count):
+                scale = scale_ref[meta[0, g] * k_count + k, pl.ds(tile, 1), :]
+                part = refs[j][k].astype(F32) * scale
+                out_ref[0, k, pl.ds(j * tile_size, tile_size), :] = part.astype(BF16)
+
+    in_specs = [pl.BlockSpec(t_scale.shape, lambda g, meta, owner: (0, 0, 0))]
+    for j in range(tiles):
+        in_specs.append(
+            pl.BlockSpec(
+                (k_count, tile_size, c_here),
+                lambda g, meta, owner, j=j: (meta[0, g], tile_of(j, g, meta, owner), 0),
+            )
+        )
+    rows = tiles * tile_size
+    return pl.pallas_call(
+        kernel,
+        out_shape=jax.ShapeDtypeStruct((block_count, k_count, rows, c_here), BF16),
+        grid_spec=pltpu.PrefetchScalarGridSpec(
+            num_scalar_prefetch=2,
+            grid=(block_count,),
+            in_specs=in_specs,
+            out_specs=pl.BlockSpec(
+                (1, k_count, rows, c_here), lambda g, meta, owner: (g, 0, 0, 0)
+            ),
+        ),
+        compiler_params=pltpu.CompilerParams(vmem_limit_bytes=32 * 2**20),
+        cost_estimate=pl.CostEstimate(
+            flops=0, bytes_accessed=4 * block_count * k_count * rows * c_here, transcendentals=0
+        ),
+        name="order_tiles",
+    )(meta, owner_map, t_scale, *([amps] * tiles))
+
+
+def mask_integrals(core, integrals, w_scale, tile_size):
+    k_count, c_rows, b_cols = integrals.shape
+    half = c_rows // 2
+    tiles = half // tile_size
+
+    def kernel(core, scale_ref, in_ref, out_ref):
+        for j in range(tiles):
+            rows = pl.ds(j * tile_size, tile_size)
+            scale = scale_ref[0, 0, pl.ds(j, 1), :]
+            out_ref[0, 0, rows, :] = (in_ref[0, 0, rows, :].astype(F32) * scale).astype(BF16)
+
+    return pl.pallas_call(
+        kernel,
+        out_shape=jax.ShapeDtypeStruct((k_count, 2, half, b_cols), BF16),
+        grid_spec=pltpu.PrefetchScalarGridSpec(
+            num_scalar_prefetch=1,
+            grid=(k_count, 2),
+            in_specs=[
+                pl.BlockSpec((1, 1, tiles, b_cols), lambda k, h, core: (k, (h + core[0]) % 2, 0, 0)),
+                pl.BlockSpec((1, 1, half, b_cols), lambda k, h, core: (k, (h + core[0]) % 2, 0, 0)),
+            ],
+            out_specs=pl.BlockSpec((1, 1, half, b_cols), lambda k, h, core: (k, h, 0, 0)),
+        ),
+        compiler_params=pltpu.CompilerParams(vmem_limit_bytes=32 * 2**20),
+        name="mask_integrals",
+    )(
+        core,
+        w_scale.reshape(k_count, 2, tiles, b_cols),
+        integrals.reshape(k_count, 2, half, b_cols),
+    )
+
+
+def contract(mine, theirs, weights, index):
+    _, k_count, rows, half = mine.shape
+    b_cols = weights.shape[3]
+    steps = 2
+
+    def kernel(mine_ref, theirs_ref, weights_ref, out_ref):
+        total = None
+        for k in range(k_count):
+            for h, ref in enumerate((mine_ref, theirs_ref)):
+                term = jnp.dot(ref[0, k], weights_ref[k, h], preferred_element_type=F32)
+                total = term if total is None else total + term
+        out_ref[...] = total.astype(BF16)
+
+    block = pl.BlockSpec((1, k_count, rows // steps, half), lambda r: (index, 0, r, 0))
+    return pl.pallas_call(
+        kernel,
+        out_shape=jax.ShapeDtypeStruct((rows, b_cols), BF16),
+        grid=(steps,),
+        in_specs=[block, block, pl.BlockSpec(weights.shape, lambda r: (0, 0, 0, 0))],
+        out_specs=pl.BlockSpec((rows // steps, b_cols), lambda r: (r, 0)),
+        compiler_params=pltpu.CompilerParams(vmem_limit_bytes=40 * 2**20),
+        cost_estimate=pl.CostEstimate(
+            flops=4 * k_count * rows * half * b_cols,
+            bytes_accessed=2 * (weights.size + 2 * k_count * rows * half + rows * b_cols),
+            transcendentals=0,
+        ),
+        name="contract",
+    )(mine, theirs, weights)
+
+
+def plane_shards(amplitudes, t_mask, integrals, w_mask, owner_map):
+    tile_size = integrals.shape[1] // w_mask.shape[1]
+    at_wide = lax.axis_index("wide")
+    home = lax.axis_index("narrow") == at_wide // 2
+    core = lax.axis_index("sub")
+    both = ("wide", "narrow")
+
+    def device(w, at_home):
+        return w * 2 + (w // 2 if at_home else 1 - w // 2)
+
+    def move(x, pairs):
+        return lax.ppermute(x, both, pairs)
+
+    inward = [(device(w, False), device(w, True)) for w in range(4)]
+    outward = [(device(w, True), device(w, False)) for w in range(4)]
+
+    def along(home_distance, away_distance):
+        pairs = []
+        for w in range(4):
+            if home_distance is not None:
+                pairs.append((device(w, True), device(w, True) % 2 + 2 * (w ^ home_distance)))
+            if away_distance is not None:
+                pairs.append((device(w, False), device(w, False) % 2 + 2 * (w ^ away_distance)))
+        return pairs
+
+    t_scale = jnp.repeat(t_mask.astype(F32), tile_size, axis=2)
+    w_scale = jnp.repeat(w_mask.astype(F32), tile_size, axis=2)
+    weights = mask_integrals(core.reshape(1), integrals, w_scale, tile_size)
+
+    def partial_sums(home_blocks, away_blocks):
+        home_meta = jnp.array(home_blocks, jnp.int32).T
+        away_meta = jnp.array(away_blocks, jnp.int32).T
+        meta = jnp.where(home, home_meta, away_meta)
+        meta = jnp.stack([meta[0], meta[1] ^ at_wide])
+        mine = order_tiles(meta, owner_map, amplitudes, t_scale, tile_size)
+        theirs = lax.ppermute(mine, "sub", [(0, 1), (1, 0)])
+        return [contract(mine, theirs, weights, g) for g in range(len(home_blocks))]
+
+    give, keep, last = [], [], []
+    give_0, last_0 = partial_sums([SUM_AWAY[0], SUM_LAST[0]], [SUM_HOME[0], SUM_LAST[0]])
+    keep_0, give_1, keep_1 = partial_sums(
+        [SUM_HOME[0], SUM_AWAY[1], SUM_HOME[1]], [SUM_AWAY[0], SUM_HOME[1], SUM_AWAY[1]]
+    )
+    last_1, give_2, keep_2 = partial_sums(
+        [SUM_LAST[1], SUM_AWAY[2], SUM_HOME[2]], [SUM_LAST[1], SUM_HOME[2], SUM_AWAY[2]]
+    )
+    near = partial_sums(NEAR, NEAR)
+    own = partial_sums(OWN, OWN)
+
+    rows, b_cols = own[0].shape
+    out = jnp.zeros((8, rows, b_cols), BF16)
+
+    def place(out, value, home_block, away_block):
+        def slot(block):
+            return ((at_wide ^ block[1]) % 2) * 4 + block[0]
+
+        where = jnp.where(home, slot(home_block), slot(away_block))
+        return lax.dynamic_update_slice(out, value[None], (where, 0, 0))
+
+    last_far = []
+    for block, value in zip(SUM_LAST, (last_0, last_1)):
+        arrived = move(value, along(block[1], block[1]))
+        last_far.append((arrived, move(arrived, outward)))
+    far = []
+    for index, (given, kept) in enumerate(zip((give_0, give_1, give_2), (keep_0, keep_1, keep_2))):
+        total = add(kept, move(given, inward + outward))
+        arrived = move(total, along(SUM_HOME[index][1], SUM_AWAY[index][1]))
+        far.append((arrived, move(arrived, outward)))
+    near_far = []
+    for value in near:
+        total = add(value, move(value, inward))
+        near_far.append(move(total, along(1, None)))
+    own_sums = [add(value, move(value, inward)) for value in own]
+
+    out = place(out, jnp.where(home, near_far[0], far[0][0]), NEAR[0], SUM_HOME[0])
+    out = place(out, jnp.where(home, near_far[1], far[1][0]), NEAR[1], SUM_HOME[1])
+    out = place(out, jnp.where(home, near_far[2], far[2][0]), NEAR[2], SUM_HOME[2])
+    out = place(out, jnp.where(home, near_far[3], far[0][1]), NEAR[3], SUM_AWAY[0])
+    out = place(out, jnp.where(home, own_sums[0], far[1][1]), OWN[0], SUM_AWAY[1])
+    out = place(out, jnp.where(home, own_sums[1], far[2][1]), OWN[1], SUM_AWAY[2])
+    out = place(out, jnp.where(home, own_sums[2], add(*last_far[0])), OWN[2], SUM_LAST[0])
+    out = place(out, jnp.where(home, own_sums[3], add(*last_far[1])), OWN[3], SUM_LAST[1])
+    return out
 
 
 def regroup_rows(amps, owner_map, tile_size):
@@ -58,4 +268,6 @@
         P(),
     )
     out_specs = P(("group", "narrow"), "wide", "sub")
-    return jax.shard_map(shards, mesh=mesh, in_specs=in_specs, out_specs=out_specs, check_vma=False)
+    planes = (mesh.shape["wide"], mesh.shape["narrow"], mesh.shape["sub"]) == (4, 2, 2)
+    body = plane_shards if planes else shards
+    return jax.shard_map(body, mesh=mesh, in_specs=in_specs, out_specs=out_specs, check_vma=False)

time: 771 us -> 431 us (0.56)
  blocking collectives: 366 us -> 0 us
  Pallas kernels: 0 us -> 79 us
  local copies, waits for them, and re-layouts: 95.7 us -> 25.9 us
  starting transfers between devices: 0.22 us -> 44.2 us
  matrix products: 43.4 us -> 0 us
  waiting for transfers between devices: 225 us -> 253 us
  between operations: 13.4 us -> 0.7 us
    all_to_all x1 -> x0, blocking collectives: 366 us -> none  [regroup_rows(): lax.all_to_all(ordered, 'wide', split_axis=1, concat_axis=0, tiled=True)]
    ppermute x0 -> x30, waiting for transfers between devices: none -> 253 us  [the longest x25 253 us: move(): return lax.ppermute(x, both, pairs)]
    reduce_scatter x1 -> x0, waiting for transfers between devices: 190 us -> none  [shards(): lax.psum_scatter(rounded, 'narrow', scatter_dimension=0, tiled=True)]
    pallas_call x0 -> x22, Pallas kernels: none -> 79 us  [the longest x16 62.8 us: contract(): pl.pallas_call(kernel, out_shape=jax.ShapeDtypeStruct((rows, b_cols), BF1...]
    ppermute x0 -> x30, starting transfers between devices: none -> 44.2 us  [the longest x25 43.1 us: move(): return lax.ppermute(x, both, pairs)]
    dot_general x1 -> x0, matrix products: 43.4 us -> none  [shards(): jnp.einsum('ikac,kcb->iab', blocks, masked_w, preferred_element_type=jnp....]
    select_n x1 -> x0, local copies, waits for them, and re-layouts: 38 us -> none  [regroup_rows(): jnp.take(amps.reshape(pair_count, virt_count // tile_size, tile_size, c_c...]
    all_gather x1 -> x0, waiting for transfers between devices: 34.9 us -> none  [join_halves(): return lax.all_gather(amps, 'sub', axis=2, tiled=True)]
  transfers between devices with their start and end apart: 2 -> 30, of which waited for: 2 -> 15; matrix products, arithmetic and copies ran while one was open for 2% -> 5% of each run, Pallas kernels for 0% -> 18%
where the time goes in v1:
time: 431 us; the launch traced here: 426 us
  waiting for transfers between devices  253 us (59%)
  Pallas kernels  79 us (18%)
  starting transfers between devices  44.2 us (10%)
  local copies, waits for them, and re-layouts  25.9 us (6%)
  other arithmetic  23.8 us (6%)
    ppermute x25, waiting for transfers between devices, move(): return lax.ppermute(x, both, pairs)  253 us
    pallas_call x16, Pallas kernels, contract(): pl.pallas_call(kernel, out_shape=jax.ShapeDtypeStruct((rows, b_cols), BF1...  62.8 us
    ppermute x25, starting transfers between devices, move(): return lax.ppermute(x, both, pairs)  43.1 us
    unnamed x46, local copies, waits for them, and re-layouts  23.9 us
    pallas_call x5, Pallas kernels, order_tiles(): pl.pallas_call(kernel, out_shape=jax.ShapeDtypeStruct((block_count, k_cou...  15.4 us
    dynamic_update_slice x8, other arithmetic, place(): return lax.dynamic_update_slice(out, value[None], (where, 0, 0))  13.5 us
    convert_element_type x7, other arithmetic, add(): return (left.astype(F32) + right.astype(F32)).astype(BF16)  9.41 us
  transfers between devices with their start and end apart: 30, of which 15 were waited for; matrix products, arithmetic and copies ran while one was open for 5% of the time, Pallas kernels for 18%

profile of v1, /device:TPU:8, one launch (start us, length us, event | category | flops | bytes accessed | tf_op | source)
XLA Modules:
  0.0 426.4 jit_solution(16724461619698133945)
XLA Ops:
  1.7 5.8 %copy-done = bf16[8,2048,512]{2,1,0:T(8,128)(2,1)S(1)} copy-done((bf16[8,2048,512]{2,1,0:T(8,128)(2,1)S(1)}, bf16[8,2048,512]{2,1,0:T(8,128)(2,1)}, u32[]{:S(2)}) %copy-start) | copy-done | bytes 16777240
  14.4 5.8 %copy-done.1 = bf16[8,2048,512]{2,1,0:T(8,128)(2,1)S(1)} copy-done((bf16[8,2048,512]{2,1,0:T(8,128)(2,1)S(1)}, bf16[8,2048,512]{2,1,0:T(8,128)(2,1)}, u32[]{:S(2)}) %copy-start.1) | copy-done | bytes 16777240
  21.2 3.8 order_tiles.5.mine_ref
  25.1 5.8 %copy-done.2 = bf16[8,2048,512]{2,1,0:T(8,128)(2,1)S(1)} copy-done((bf16[8,2048,512]{2,1,0:T(8,128)(2,1)S(1)}, bf16[8,2048,512]{2,1,0:T(8,128)(2,1)}, u32[]{:S(2)}) %copy-start.2) | copy-done | bytes 16777240
  33.8 3.9 order_tiles.9.mine_ref
  41.0 5.3 %contract.18 = bf16[512,1024]{1,0:T(8,128)(2,1)} custom-call(bf16[2,2,512,512]{3,2,1,0:T(8,128)(2,1)} %order_tiles.7.mine_ref, bf16[2,2,512,512]{3,2,1,0:T(8,128)(2,1)} %collective-permute-done.4.theirs_ref, bf16[2,2,512,1024]{3,2,1,0:T(8,128)(2,1)S(1)} %mask_integrals.1.weights_ref), custom_call_target="tpu_custom_call" | custom-call | flops 2147483648 | bytes 7340032 | tf_op jit(solution)/shard_map/contract/pallas_call | solution.py:116
  60.8 4.4 %contract.31 = bf16[512,1024]{1,0:T(8,128)(2,1)} custom-call(bf16[3,2,512,512]{3,2,1,0:T(8,128)(2,1)S(1)} %order_tiles.8.mine_ref, bf16[3,2,512,512]{3,2,1,0:T(8,128)(2,1)} %collective-permute-done.13.theirs_ref, bf16[2,2,512,1024]{3,2,1,0:T(8,128)(2,1)S(1)} %copy-done.4), custom_call_target="tpu_custom_call" | custom-call | flops 2147483648 | bytes 7340032 | tf_op jit(solution)/shard_map/contract/pallas_call | solution.py:116
  65.2 4.4 %contract.24 = bf16[512,1024]{1,0:T(8,128)(2,1)} custom-call(bf16[3,2,512,512]{3,2,1,0:T(8,128)(2,1)S(1)} %order_tiles.8.mine_ref, bf16[3,2,512,512]{3,2,1,0:T(8,128)(2,1)} %collective-permute-done.13.theirs_ref, bf16[2,2,512,1024]{3,2,1,0:T(8,128)(2,1)S(1)} %copy-done.4), custom_call_target="tpu_custom_call" | custom-call | flops 2147483648 | bytes 7340032 | tf_op jit(solution)/shard_map/contract/pallas_call | solution.py:116
  80.1 14.9 %collective-permute-done.9 = bf16[512,1024]{1,0:T(8,128)(2,1)S(1)} collective-permute-done((bf16[512,1024]{1,0:T(8,128)(2,1)S(1)}, bf16[512,1024]{1,0:T(8,128)(2,1)S(1)}, u32[]{:S(2)}, u32[]{:S(2)}) %collective-permute-start.9) | collective-permute-done | bytes 1048608 | tf_op jit(solution)/shard_map/ppermute | solution.py:143
  97.6 3.9 contract.20
  101.5 3.8 contract.16
  105.8 40.8 %collective-permute-done.25 = bf16[512,1024]{1,0:T(8,128)(2,1)} collective-permute-done((bf16[512,1024]{1,0:T(8,128)(2,1)S(1)}, bf16[512,1024]{1,0:T(8,128)(2,1)}, u32[]{:S(2)}, u32[]{:S(2)}) %collective-permute-start.25) | collective-permute-done | bytes 1048608 | tf_op jit(solution)/shard_map/ppermute | solution.py:143
  153.1 39.1 %collective-permute-done.6 = bf16[512,1024]{1,0:T(8,128)(2,1)} collective-permute-done((bf16[512,1024]{1,0:T(8,128)(2,1)S(1)}, bf16[512,1024]{1,0:T(8,128)(2,1)}, u32[]{:S(2)}, u32[]{:S(2)}) %collective-permute-start.6) | collective-permute-done | bytes 1048608 | tf_op jit(solution)/shard_map/ppermute | solution.py:143
  195.0 42.1 %collective-permute-done.28 = bf16[512,1024]{1,0:T(8,128)(2,1)} collective-permute-done((bf16[512,1024]{1,0:T(8,128)(2,1)}, bf16[512,1024]{1,0:T(8,128)(2,1)}, u32[]{:S(2)}, u32[]{:S(2)}) %collective-permute-start.28) | collective-permute-done | bytes 1048608 | tf_op jit(solution)/shard_map/ppermute | solution.py:143
  254.7 4.2 collective-permute-done.10
  260.2 5.6 %collective-permute-start.18 = (bf16[512,1024]{1,0:T(8,128)(2,1)}, bf16[512,1024]{1,0:T(8,128)(2,1)}, u32[]{:S(2)}, u32[]{:S(2)}) collective-permute-start(bf16[512,1024]{1,0:T(8,128)(2,1)} %collective-permute-done.6), channel_id=1, source_target_pairs={{0,2},{4,6},{10,8},{14,12},{1,3},{5,7},{11,9},{15,13},{16,18},{20,... | collective-permute-start | bytes 3145736 | tf_op jit(solution)/shard_map/ppermute | solution.py:143
  267.4 14.0 %collective-permute-done.15 = bf16[512,1024]{1,0:T(8,128)(2,1)} collective-permute-done((bf16[512,1024]{1,0:T(8,128)(2,1)}, bf16[512,1024]{1,0:T(8,128)(2,1)}, u32[]{:S(2)}, u32[]{:S(2)}) %collective-permute-start.15) | collective-permute-done | bytes 1048608 | tf_op jit(solution)/shard_map/ppermute | solution.py:143
  291.0 3.9 collective-permute-start.8
  297.6 12.4 %collective-permute-done.16 = bf16[512,1024]{1,0:T(8,128)(2,1)S(1)} collective-permute-done((bf16[512,1024]{1,0:T(8,128)(2,1)S(1)}, bf16[512,1024]{1,0:T(8,128)(2,1)S(1)}, u32[]{:S(2)}, u32[]{:S(2)}) %collective-permute-start.16) | collective-permute-done | bytes 1048608 | tf_op jit(solution)/shard_map/ppermute | solution.py:143
  312.4 20.1 %collective-permute-done.20 = bf16[512,1024]{1,0:T(8,128)(2,1)S(1)} collective-permute-done((bf16[512,1024]{1,0:T(8,128)(2,1)S(1)}, bf16[512,1024]{1,0:T(8,128)(2,1)S(1)}, u32[]{:S(2)}, u32[]{:S(2)}) %collective-permute-start.20) | collective-permute-done | bytes 1048608 | tf_op jit(solution)/shard_map/ppermute | solution.py:143
  345.5 7.8 %collective-permute-done.22 = bf16[512,1024]{1,0:T(8,128)(2,1)S(1)} collective-permute-done((bf16[512,1024]{1,0:T(8,128)(2,1)S(1)}, bf16[512,1024]{1,0:T(8,128)(2,1)S(1)}, u32[]{:S(2)}, u32[]{:S(2)}) %collective-permute-start.22) | collective-permute-done | bytes 1048608 | tf_op jit(solution)/shard_map/ppermute | solution.py:143
  360.9 16.3 %collective-permute-done.17 = bf16[512,1024]{1,0:T(8,128)(2,1)} collective-permute-done((bf16[512,1024]{1,0:T(8,128)(2,1)S(1)}, bf16[512,1024]{1,0:T(8,128)(2,1)}, u32[]{:S(2)}, u32[]{:S(2)}) %collective-permute-start.17) | collective-permute-done | bytes 1048608 | tf_op jit(solution)/shard_map/ppermute | solution.py:143
  383.0 21.6 %collective-permute-done.26 = bf16[512,1024]{1,0:T(8,128)(2,1)S(1)} collective-permute-done((bf16[512,1024]{1,0:T(8,128)(2,1)}, bf16[512,1024]{1,0:T(8,128)(2,1)S(1)}, u32[]{:S(2)}, u32[]{:S(2)}) %collective-permute-start.26) | collective-permute-done | bytes 1048608 | tf_op jit(solution)/shard_map/ppermute | solution.py:143
  406.8 16.5 %collective-permute-done.29 = bf16[512,1024]{1,0:T(8,128)(2,1)S(1)} collective-permute-done((bf16[512,1024]{1,0:T(8,128)(2,1)}, bf16[512,1024]{1,0:T(8,128)(2,1)S(1)}, u32[]{:S(2)}, u32[]{:S(2)}) %collective-permute-start.29) | collective-permute-done | bytes 1048608 | tf_op jit(solution)/shard_map/ppermute | solution.py:143
  (136 shorter events, 119.4 us)
Async XLA Ops:
  10.9 42.9 %collective-permute-start.3 = (bf16[3,2,512,512]{3,2,1,0:T(8,128)(2,1)}, bf16[3,2,512,512]{3,2,1,0:T(8,128)(2,1)}, u32[]{:S(2)}, u32[]{:S(2)}) collective-permute-start(bf16[3,2,512,512]{3,2,1,0:T(8,128)(2,1)} %order_tiles.6.mine_ref), channel_id=1, source_target_pairs={{0,1},{1,0},{2,3},{3,2},{4,5},{5,4},{6,7},{7,6},{8,9},{9,8},{10,11... | collective-permute-start | bytes 9437192 | tf_op jit(solution)/shard_map/ppermute | solution.py:167
  13.8 46.4 %collective-permute-start.13 = (bf16[3,2,512,512]{3,2,1,0:T(8,128)(2,1)S(1)}, bf16[3,2,512,512]{3,2,1,0:T(8,128)(2,1)}, u32[]{:S(2)}, u32[]{:S(2)}) collective-permute-start(bf16[3,2,512,512]{3,2,1,0:T(8,128)(2,1)S(1)} %order_tiles.8.mine_ref), channel_id=1, source_target_pairs={{0,1},{1,0},{2,3},{3,2},{4,5},{5,4},{6,7},{7,6},{8,9},{9,8},{10,11... | collective-permute-start | bytes 9437192 | tf_op jit(solution)/shard_map/ppermute | solution.py:167
  25.0 72.6 %collective-permute-start = (bf16[4,2,512,512]{3,2,1,0:T(8,128)(2,1)}, bf16[4,2,512,512]{3,2,1,0:T(8,128)(2,1)}, u32[]{:S(2)}, u32[]{:S(2)}) collective-permute-start(bf16[4,2,512,512]{3,2,1,0:T(8,128)(2,1)} %order_tiles.5.mine_ref), channel_id=1, source_target_pairs={{0,1},{1,0},{2,3},{3,2},{4,5},{5,4},{6,7},{7,6},{8,9},{9,8},{10,11... | collective-permute-start | bytes 12582920 | tf_op jit(solution)/shard_map/ppermute | solution.py:167
  37.7 208.2 %collective-permute-start.19 = (bf16[4,2,512,512]{3,2,1,0:T(8,128)(2,1)}, bf16[4,2,512,512]{3,2,1,0:T(8,128)(2,1)}, u32[]{:S(2)}, u32[]{:S(2)}) collective-permute-start(bf16[4,2,512,512]{3,2,1,0:T(8,128)(2,1)} %order_tiles.9.mine_ref), channel_id=1, source_target_pairs={{0,1},{1,0},{2,3},{3,2},{4,5},{5,4},{6,7},{7,6},{8,9},{9,8},{10,11... | collective-permute-start | bytes 12582920 | tf_op jit(solution)/shard_map/ppermute | solution.py:167
  53.8 92.8 %collective-permute-start.25 = (bf16[512,1024]{1,0:T(8,128)(2,1)S(1)}, bf16[512,1024]{1,0:T(8,128)(2,1)}, u32[]{:S(2)}, u32[]{:S(2)}) collective-permute-start(bf16[512,1024]{1,0:T(8,128)(2,1)S(1)} %contract.29), channel_id=1, source_target_pairs={{0,8},{2,10},{4,12},{6,14},{10,2},{8,0},{14,6},{12,4},{1,9},{3,11}... | collective-permute-start | bytes 3145736 | tf_op jit(solution)/shard_map/ppermute | solution.py:143
  73.2 73.5 %collective-permute-start.14 = (bf16[512,1024]{1,0:T(8,128)(2,1)}, bf16[512,1024]{1,0:T(8,128)(2,1)S(1)}, u32[]{:S(2)}, u32[]{:S(2)}) collective-permute-start(bf16[512,1024]{1,0:T(8,128)(2,1)} %contract.24), channel_id=1, source_target_pairs={{2,0},{6,4},{8,10},{12,14},{0,2},{4,6},{10,8},{14,12},{3,1},{7,5},... | collective-permute-start | bytes 3145736 | tf_op jit(solution)/shard_map/ppermute | solution.py:143
  95.0 97.2 %collective-permute-start.6 = (bf16[512,1024]{1,0:T(8,128)(2,1)S(1)}, bf16[512,1024]{1,0:T(8,128)(2,1)}, u32[]{:S(2)}, u32[]{:S(2)}) collective-permute-start(bf16[512,1024]{1,0:T(8,128)(2,1)S(1)} %add_convert_fusion.11), channel_id=1, source_target_pairs={{0,8},{2,14},{4,12},{6,10},{10,2},{8,4},{14,6},{12,0},{1,9},{3,15}... | collective-permute-start | bytes 3145736 | tf_op jit(solution)/shard_map/ppermute | solution.py:143
  97.6 139.5 %collective-permute-start.28 = (bf16[512,1024]{1,0:T(8,128)(2,1)}, bf16[512,1024]{1,0:T(8,128)(2,1)}, u32[]{:S(2)}, u32[]{:S(2)}) collective-permute-start(bf16[512,1024]{1,0:T(8,128)(2,1)} %contract.31), channel_id=1, source_target_pairs={{0,12},{2,14},{4,8},{6,10},{10,6},{8,4},{14,2},{12,0},{1,13},{3,15... | collective-permute-start | bytes 3145736 | tf_op jit(solution)/shard_map/ppermute | solution.py:143
  146.6 112.4 %collective-permute-start.10 = (bf16[512,1024]{1,0:T(8,128)(2,1)S(1)}, bf16[512,1024]{1,0:T(8,128)(2,1)}, u32[]{:S(2)}, u32[]{:S(2)}) collective-permute-start(bf16[512,1024]{1,0:T(8,128)(2,1)S(1)} %add_convert_fusion.9), channel_id=1, source_target_pairs={{0,12},{2,10},{4,8},{6,14},{10,6},{8,0},{14,2},{12,4},{1,13},{3,11... | collective-permute-start | bytes 3145736 | tf_op jit(solution)/shard_map/ppermute | solution.py:143
  146.7 113.5 %collective-permute-start.1 = (bf16[512,1024]{1,0:T(8,128)(2,1)S(1)}, bf16[512,1024]{1,0:T(8,128)(2,1)}, u32[]{:S(2)}, u32[]{:S(2)}) collective-permute-start(bf16[512,1024]{1,0:T(8,128)(2,1)S(1)} %contract.16), channel_id=1, source_target_pairs={{2,0},{6,4},{8,10},{12,14},{3,1},{7,5},{9,11},{13,15},{18,16},{22,... | collective-permute-start | bytes 3145736 | tf_op jit(solution)/shard_map/ppermute | solution.py:143
  192.2 89.3 %collective-permute-start.15 = (bf16[512,1024]{1,0:T(8,128)(2,1)}, bf16[512,1024]{1,0:T(8,128)(2,1)}, u32[]{:S(2)}, u32[]{:S(2)}) collective-permute-start(bf16[512,1024]{1,0:T(8,128)(2,1)} %add_convert_fusion.7), channel_id=1, source_target_pairs={{0,8},{2,14},{4,12},{6,10},{10,2},{8,4},{14,6},{12,0},{1,9},{3,15}... | collective-permute-start | bytes 3145736 | tf_op jit(solution)/shard_map/ppermute | solution.py:143
  237.1 45.6 %collective-permute-start.7 = (bf16[512,1024]{1,0:T(8,128)(2,1)S(1)}, bf16[512,1024]{1,0:T(8,128)(2,1)}, u32[]{:S(2)}, u32[]{:S(2)}) collective-permute-start(bf16[512,1024]{1,0:T(8,128)(2,1)S(1)} %contract.19), channel_id=1, source_target_pairs={{2,0},{6,4},{8,10},{12,14},{3,1},{7,5},{9,11},{13,15},{18,16},{22,... | collective-permute-start | bytes 3145736 | tf_op jit(solution)/shard_map/ppermute | solution.py:143
  245.9 45.1 %collective-permute-start.11 = (bf16[512,1024]{1,0:T(8,128)(2,1)S(1)}, bf16[512,1024]{1,0:T(8,128)(2,1)S(1)}, u32[]{:S(2)}, u32[]{:S(2)}) collective-permute-start(bf16[512,1024]{1,0:T(8,128)(2,1)S(1)} %contract.22), channel_id=1, source_target_pairs={{2,0},{6,4},{8,10},{12,14},{3,1},{7,5},{9,11},{13,15},{18,16},{22,... | collective-permute-start | bytes 3145736 | tf_op jit(solution)/shard_map/ppermute | solution.py:143
  258.9 51.1 %collective-permute-start.16 = (bf16[512,1024]{1,0:T(8,128)(2,1)S(1)}, bf16[512,1024]{1,0:T(8,128)(2,1)S(1)}, u32[]{:S(2)}, u32[]{:S(2)}) collective-permute-start(bf16[512,1024]{1,0:T(8,128)(2,1)S(1)} %contract.25), channel_id=1, source_target_pairs={{2,0},{6,4},{8,10},{12,14},{3,1},{7,5},{9,11},{13,15},{18,16},{22,... | collective-permute-start | bytes 3145736 | tf_op jit(solution)/shard_map/ppermute | solution.py:143
  281.4 51.1 %collective-permute-start.20 = (bf16[512,1024]{1,0:T(8,128)(2,1)S(1)}, bf16[512,1024]{1,0:T(8,128)(2,1)S(1)}, u32[]{:S(2)}, u32[]{:S(2)}) collective-permute-start(bf16[512,1024]{1,0:T(8,128)(2,1)S(1)} %contract.26), channel_id=1, source_target_pairs={{2,0},{6,4},{8,10},{12,14},{3,1},{7,5},{9,11},{13,15},{18,16},{22,... | collective-permute-start | bytes 3145736 | tf_op jit(solution)/shard_map/ppermute | solution.py:143
  282.7 51.7 %collective-permute-start.2 = (bf16[512,1024]{1,0:T(8,128)(2,1)S(1)}, bf16[512,1024]{1,0:T(8,128)(2,1)}, u32[]{:S(2)}, u32[]{:S(2)}) collective-permute-start(bf16[512,1024]{1,0:T(8,128)(2,1)S(1)} %add_convert_fusion.12), channel_id=1, source_target_pairs={{0,4},{4,0},{10,14},{14,10},{1,5},{5,1},{11,15},{15,11},{16,20},{2... | collective-permute-start | bytes 3145736 | tf_op jit(solution)/shard_map/ppermute | solution.py:143
  291.0 51.5 %collective-permute-start.8 = (bf16[512,1024]{1,0:T(8,128)(2,1)}, bf16[512,1024]{1,0:T(8,128)(2,1)}, u32[]{:S(2)}, u32[]{:S(2)}) collective-permute-start(bf16[512,1024]{1,0:T(8,128)(2,1)} %add_convert_fusion.10), channel_id=1, source_target_pairs={{0,4},{4,0},{10,14},{14,10},{1,5},{5,1},{11,15},{15,11},{16,20},{2... | collective-permute-start | bytes 3145736 | tf_op jit(solution)/shard_map/ppermute | solution.py:143
  296.3 57.1 %collective-permute-start.22 = (bf16[512,1024]{1,0:T(8,128)(2,1)S(1)}, bf16[512,1024]{1,0:T(8,128)(2,1)S(1)}, u32[]{:S(2)}, u32[]{:S(2)}) collective-permute-start(bf16[512,1024]{1,0:T(8,128)(2,1)S(1)} %contract.27), channel_id=1, source_target_pairs={{2,0},{6,4},{8,10},{12,14},{3,1},{7,5},{9,11},{13,15},{18,16},{22,... | collective-permute-start | bytes 3145736 | tf_op jit(solution)/shard_map/ppermute | solution.py:143
  310.1 45.6 %collective-permute-start.12 = (bf16[512,1024]{1,0:T(8,128)(2,1)}, bf16[512,1024]{1,0:T(8,128)(2,1)}, u32[]{:S(2)}, u32[]{:S(2)}) collective-permute-start(bf16[512,1024]{1,0:T(8,128)(2,1)} %add_convert_fusion.8), channel_id=1, source_target_pairs={{0,4},{4,0},{10,14},{14,10},{1,5},{5,1},{11,15},{15,11},{16,20},{2... | collective-permute-start | bytes 3145736 | tf_op jit(solution)/shard_map/ppermute | solution.py:143
  332.5 44.7 %collective-permute-start.17 = (bf16[512,1024]{1,0:T(8,128)(2,1)S(1)}, bf16[512,1024]{1,0:T(8,128)(2,1)}, u32[]{:S(2)}, u32[]{:S(2)}) collective-permute-start(bf16[512,1024]{1,0:T(8,128)(2,1)S(1)} %add_convert_fusion.6), channel_id=1, source_target_pairs={{0,4},{4,0},{10,14},{14,10},{1,5},{5,1},{11,15},{15,11},{16,20},{2... | collective-permute-start | bytes 3145736 | tf_op jit(solution)/shard_map/ppermute | solution.py:143
  353.4 51.2 %collective-permute-start.26 = (bf16[512,1024]{1,0:T(8,128)(2,1)}, bf16[512,1024]{1,0:T(8,128)(2,1)S(1)}, u32[]{:S(2)}, u32[]{:S(2)}) collective-permute-start(bf16[512,1024]{1,0:T(8,128)(2,1)} %collective-permute-done.25), channel_id=1, source_target_pairs={{0,2},{4,6},{10,8},{14,12},{1,3},{5,7},{11,9},{15,13},{16,18},{20,... | collective-permute-start | bytes 3145736 | tf_op jit(solution)/shard_map/ppermute | solution.py:143
  355.7 48.9 %collective-permute-start.24 = (bf16[512,1024]{1,0:T(8,128)(2,1)S(1)}, bf16[512,1024]{1,0:T(8,128)(2,1)S(1)}, u32[]{:S(2)}, u32[]{:S(2)}) collective-permute-start(bf16[512,1024]{1,0:T(8,128)(2,1)S(1)} %contract.28), channel_id=1, source_target_pairs={{2,0},{6,4},{8,10},{12,14},{3,1},{7,5},{9,11},{13,15},{18,16},{22,... | collective-permute-start | bytes 3145736 | tf_op jit(solution)/shard_map/ppermute | solution.py:143
  359.7 63.6 %collective-permute-start.27 = (bf16[512,1024]{1,0:T(8,128)(2,1)S(1)}, bf16[512,1024]{1,0:T(8,128)(2,1)S(1)}, u32[]{:S(2)}, u32[]{:S(2)}) collective-permute-start(bf16[512,1024]{1,0:T(8,128)(2,1)S(1)} %contract.30), channel_id=1, source_target_pairs={{2,0},{6,4},{8,10},{12,14},{3,1},{7,5},{9,11},{13,15},{18,16},{22,... | collective-permute-start | bytes 3145736 | tf_op jit(solution)/shard_map/ppermute | solution.py:143
  377.3 46.0 %collective-permute-start.29 = (bf16[512,1024]{1,0:T(8,128)(2,1)}, bf16[512,1024]{1,0:T(8,128)(2,1)S(1)}, u32[]{:S(2)}, u32[]{:S(2)}) collective-permute-start(bf16[512,1024]{1,0:T(8,128)(2,1)} %collective-permute-done.28), channel_id=1, source_target_pairs={{0,2},{4,6},{10,8},{14,12},{1,3},{5,7},{11,9},{15,13},{16,18},{20,... | collective-permute-start | bytes 3145736 | tf_op jit(solution)/shard_map/ppermute | solution.py:143
  (29 other events, 261.6 us)

commit v2 on v0

--- a/solution.py
+++ b/solution.py
@@ -1,7 +1,335 @@
 import jax
 import jax.numpy as jnp
 from jax import lax
+from jax.experimental import pallas as pl
+from jax.experimental.pallas import tpu as pltpu
 from jax.sharding import PartitionSpec as P
+
+BF16 = jnp.bfloat16
+F32 = jnp.float32
+MIB = 2**20
+
+SUM_HOME = [(0, 2), (1, 3), (2, 2)]
+SUM_AWAY = [(0, 3), (1, 2), (2, 3), (3, 2)]
+SUM_LAST = [(3, 3)]
+NEAR = [(0, 1), (1, 1), (2, 1), (3, 1)]
+OWN = [(0, 0), (1, 0), (2, 0), (3, 0)]
+HOME_SLOTS = [
+    SUM_LAST[0], SUM_AWAY[0], SUM_AWAY[1], SUM_HOME[0], SUM_AWAY[2], SUM_HOME[1], SUM_HOME[2], SUM_AWAY[3], *NEAR, *OWN
+]
+AWAY_SLOTS = [
+    SUM_LAST[0], SUM_HOME[0], SUM_HOME[1], SUM_AWAY[0], SUM_HOME[2], SUM_AWAY[1], SUM_AWAY[2], SUM_AWAY[3], *NEAR, *OWN
+]
+
+ANY = pl.BlockSpec(memory_space=pl.ANY)
+
+
+COST = pl.CostEstimate(flops=10**12, bytes_accessed=10**9, transcendentals=0)
+
+
+class Chain:
+    def __init__(self, first):
+        self.before = first
+
+    def call(self, kernel, name, operands, out_shape, grid, in_specs, out_specs, prefetch=(), aliases=None):
+        skip = len(prefetch) + len(operands)
+
+        def body(*refs):
+            kernel(*refs[:skip], *refs[skip + 1:])
+
+        result = pl.pallas_call(
+            body,
+            out_shape=out_shape,
+            grid_spec=pltpu.PrefetchScalarGridSpec(
+                num_scalar_prefetch=len(prefetch),
+                grid=grid,
+                in_specs=[*in_specs, ANY],
+                out_specs=out_specs,
+            ),
+            input_output_aliases=aliases or {},
+            compiler_params=pltpu.CompilerParams(vmem_limit_bytes=64 * MIB),
+            cost_estimate=COST,
+            name=name,
+        )(*prefetch, *operands, self.before)
+        self.before = result
+        return result
+
+    def order_tiles(self, meta, owner_map, amps, t_scale, tile_size, first, count):
+        c_here = amps.shape[2]
+        tiles = owner_map.shape[0] // 4
+        rows = tiles * tile_size
+        k_count = 2
+
+        def tile_of(j, g, meta, owner):
+            return owner[meta[1, first + g] * tiles + j]
+
+        def kernel(meta, owner, scale_ref, *refs):
+            out_ref = refs[-1]
+            g = pl.program_id(0)
+            for j in range(tiles):
+                tile = tile_of(j, g, meta, owner)
+                for k in range(k_count):
+                    scale = scale_ref[meta[0, first + g] * k_count + k, pl.ds(tile, 1), :]
+                    part = refs[j][k].astype(F32) * scale
+                    out_ref[0, k, pl.ds(j * tile_size, tile_size), :] = part.astype(BF16)
+
+        in_specs = [pl.BlockSpec(t_scale.shape, lambda g, meta, owner: (0, 0, 0))]
+        for j in range(tiles):
+            in_specs.append(
+                pl.BlockSpec(
+                    (k_count, tile_size, c_here),
+                    lambda g, meta, owner, j=j: (meta[0, first + g], tile_of(j, g, meta, owner), 0),
+                )
+            )
+        return self.call(
+            kernel,
+            "order_tiles",
+            (t_scale, *([amps] * tiles)),
+            jax.ShapeDtypeStruct((count, k_count, rows, c_here), BF16),
+            (count,),
+            in_specs,
+            pl.BlockSpec((1, k_count, rows, c_here), lambda g, meta, owner: (g, 0, 0, 0)),
+            prefetch=(meta, owner_map),
+        )
+
+    def mask_integrals(self, core, integrals, w_scale, tile_size):
+        k_count, c_rows, b_cols = integrals.shape
+        half = c_rows // 2
+        tiles = half // tile_size
+
+        def kernel(core, scale_ref, in_ref, out_ref):
+            for j in range(tiles):
+                rows = pl.ds(j * tile_size, tile_size)
+                scale = scale_ref[0, 0, pl.ds(j, 1), :]
+                out_ref[0, 0, rows, :] = (in_ref[0, 0, rows, :].astype(F32) * scale).astype(BF16)
+
+        def source(k, h, core):
+            return (k, (h + core[0]) % 2, 0, 0)
+
+        return self.call(
+            kernel,
+            "mask_integrals",
+            (
+                w_scale.reshape(k_count, 2, tiles, b_cols),
+                integrals.reshape(k_count, 2, half, b_cols),
+            ),
+            jax.ShapeDtypeStruct((k_count, 2, half, b_cols), BF16),
+            (k_count, 2),
+            [
+                pl.BlockSpec((1, 1, tiles, b_cols), source),
+                pl.BlockSpec((1, 1, half, b_cols), source),
+            ],
+            pl.BlockSpec((1, 1, half, b_cols), lambda k, h, core: (k, h, 0, 0)),
+            prefetch=(core,),
+        )
+
+    def contract(self, tiles, weights, first, count=1):
+        mine, theirs = tiles
+        _, k_count, rows, half = mine.shape
+        b_cols = weights.shape[3]
+        steps = 2
+
+        def kernel(mine_ref, theirs_ref, weights_ref, out_ref):
+            total = None
+            for k in range(k_count):
+                for h, ref in enumerate((mine_ref, theirs_ref)):
+                    term = jnp.dot(ref[0, k], weights_ref[k, h], preferred_element_type=F32)
+                    total = term if total is None else total + term
+            out_ref[0] = total.astype(BF16)
+
+        block = pl.BlockSpec((1, k_count, rows // steps, half), lambda g, r: (first + g, 0, r, 0))
+        return self.call(
+            kernel,
+            "contract",
+            (mine, theirs, weights),
+            jax.ShapeDtypeStruct((count, rows, b_cols), BF16),
+            (count, steps),
+            [block, block, pl.BlockSpec(weights.shape, lambda g, r: (0, 0, 0, 0))],
+            pl.BlockSpec((1, rows // steps, b_cols), lambda g, r: (g, r, 0)),
+        )
+
+    def add(self, left, right):
+        count, rows, b_cols = left.shape
+        steps = 2
+
+        def kernel(left_ref, right_ref, out_ref):
+            out_ref[...] = (left_ref[...].astype(F32) + right_ref[...].astype(F32)).astype(BF16)
+
+        block = pl.BlockSpec((1, rows // steps, b_cols), lambda g, r: (g, r, 0))
+        return self.call(
+            kernel,
+            "add",
+            (left, right),
+            jax.ShapeDtypeStruct(left.shape, BF16),
+            (count, steps),
+            [block, block],
+            block,
+        )
+
+    def hand_on(self, value):
+        return self.call(
+            lambda *refs: None,
+            "hand_on",
+            (value,),
+            jax.ShapeDtypeStruct(value.shape, value.dtype),
+            (1,),
+            [ANY],
+            ANY,
+            aliases={0: 0},
+        )
+
+    def place(self, out, where, home_terms, away_terms):
+        terms = (*home_terms, *away_terms)
+        _, rows, b_cols = terms[0][0].shape
+        steps = 2
+        block_count = 8
+
+        def total(refs):
+            if len(refs) == 1:
+                return refs[0][...]
+            return (refs[0][...].astype(F32) + refs[1][...].astype(F32)).astype(BF16)
+
+        def kernel(where, *refs):
+            out_ref = refs[-1]
+            split = len(home_terms)
+
+            @pl.when(where[0] == 1)
+            def _():
+                out_ref[...] = total(refs[:split])
+
+            @pl.when(where[0] == 0)
+            def _():
+                out_ref[...] = total(refs[split:len(terms)])
+
+        def block(index):
+            return pl.BlockSpec((1, rows // steps, b_cols), lambda r, where: (index, r, 0))
+
+        held = () if out is None else (out,)
+        return self.call(
+            kernel,
+            "place",
+            (*[array for array, _ in terms], *held),
+            jax.ShapeDtypeStruct((block_count, rows, b_cols), BF16),
+            (steps,),
+            [block(index) for _, index in terms] + [ANY] * len(held),
+            pl.BlockSpec((1, rows // steps, b_cols), lambda r, where: (where[1], r, 0)),
+            prefetch=(where,),
+            aliases={1 + len(terms): 0} if held else None,
+        )
+
+
+def plane_shards(amplitudes, t_mask, integrals, w_mask, owner_map):
+    tile_size = integrals.shape[1] // w_mask.shape[1]
+    at_wide = lax.axis_index("wide")
+    home = lax.axis_index("narrow") == at_wide // 2
+    core = lax.axis_index("sub").reshape(1)
+    both = ("wide", "narrow")
+
+    def device(w, at_home):
+        return w * 2 + (w // 2 if at_home else 1 - w // 2)
+
+    def move(x, pairs):
+        return lax.ppermute(x, both, pairs)
+
+    inward = [(device(w, False), device(w, True)) for w in range(4)]
+    outward = [(device(w, True), device(w, False)) for w in range(4)]
+
+    def along(home_distance, away_distance):
+        pairs = []
+        for w in range(4):
+            for at_home, distance in ((True, home_distance), (False, away_distance)):
+                if distance is not None:
+                    here = device(w, at_home)
+                    pairs.append((here, here % 2 + 2 * (w ^ distance)))
+        return pairs
+
+    home_meta = jnp.array(HOME_SLOTS, jnp.int32).T
+    away_meta = jnp.array(AWAY_SLOTS, jnp.int32).T
+    meta = jnp.where(home, home_meta, away_meta)
+    meta = jnp.stack([meta[0], meta[1] ^ at_wide])
+    t_scale = jnp.repeat(t_mask.astype(F32), tile_size, axis=2)
+    w_scale = jnp.repeat(w_mask.astype(F32), tile_size, axis=2)
+
+    chain = Chain(meta)
+
+    def ordered(first, count):
+        mine = chain.order_tiles(meta, owner_map, amplitudes, t_scale, tile_size, first, count)
+        return mine, lax.ppermute(mine, "sub", [(0, 1), (1, 0)])
+
+    def where(home_block, away_block):
+        def slot(block):
+            return ((at_wide ^ block[1]) % 2) * 4 + block[0]
+
+        return jnp.stack([home.astype(jnp.int32), jnp.where(home, slot(home_block), slot(away_block))])
+
+    swap = inward + outward
+
+    def contract(tiles, first, count=1):
+        return chain.contract(tiles, weights, first, count)
+
+    tiles_last = ordered(0, 1)
+    tiles_first = ordered(1, 1)
+    weights = chain.mask_integrals(core, integrals, w_scale, tile_size)
+    tiles_a = ordered(2, 3)
+    last_far = move(contract(tiles_last, 0), along(SUM_LAST[0][1], SUM_LAST[0][1]))
+    given_0 = move(contract(tiles_first, 0), swap)
+    given_1 = move(contract(tiles_a, 0), swap)
+    tiles_b = ordered(5, 3)
+    kept_0 = contract(tiles_a, 1)
+    kept_1 = contract(tiles_b, 0)
+    tiles_c = ordered(8, 8)
+    far_0 = move(chain.add(kept_0, given_0), along(SUM_HOME[0][1], SUM_AWAY[0][1]))
+    given_2 = move(contract(tiles_a, 2), swap)
+    kept_2 = contract(tiles_b, 1)
+    far_1 = move(chain.add(kept_1, given_1), along(SUM_HOME[1][1], SUM_AWAY[1][1]))
+    last_far = chain.hand_on(last_far)
+    near_a = contract(tiles_c, 0, 2)
+    near_a_in = move(near_a, inward)
+    extra = contract(tiles_b, 2)
+    extra_out = move(extra, outward)
+
+    total_2 = chain.add(kept_2, given_2)
+    last_far = chain.hand_on(last_far)
+    last_over = move(last_far, outward)
+
+    total_3 = chain.add(extra, extra_out)
+    far_0 = chain.hand_on(far_0)
+    far_2 = move(chain.hand_on(total_2), along(SUM_HOME[2][1], SUM_AWAY[2][1]))
+    near_b = contract(tiles_c, 2, 2)
+    near_b_in = move(near_b, inward)
+
+    last_over = chain.hand_on(last_over)
+    far_0 = chain.hand_on(far_0)
+    over_0 = move(far_0, outward)
+    near_a_far = move(chain.add(near_a, near_a_in), along(1, None))
+
+    over_0 = chain.hand_on(over_0)
+    far_1 = chain.hand_on(far_1)
+    over_1 = move(far_1, outward)
+    own_a = contract(tiles_c, 4, 3)
+    own_a_in = move(own_a, inward)
+
+    near_b_far = move(chain.add(near_b, near_b_in), along(1, None))
+    over_1 = chain.hand_on(over_1)
+    far_3 = move(chain.hand_on(total_3), along(None, SUM_AWAY[3][1]))
+
+    far_2 = chain.hand_on(far_2)
+    over_2 = move(far_2, outward)
+    out = chain.place(None, where(NEAR[0], SUM_LAST[0]), [(near_a_far, 0)], [(last_far, 0), (last_over, 0)])
+    out = chain.place(out, where(NEAR[1], SUM_HOME[0]), [(near_a_far, 1)], [(far_0, 0)])
+    own_b = contract(tiles_c, 7)
+    own_b_in = move(own_b, inward)
+
+    over_2 = chain.hand_on(over_2)
+    far_3 = chain.hand_on(far_3)
+    over_3 = move(far_3, outward)
+    out = chain.place(out, where(NEAR[2], SUM_HOME[1]), [(near_b_far, 0)], [(far_1, 0)])
+    out = chain.place(out, where(NEAR[3], SUM_AWAY[0]), [(near_b_far, 1)], [(over_0, 0)])
+    out = chain.place(out, where(OWN[0], SUM_AWAY[1]), [(own_a, 0), (own_a_in, 0)], [(over_1, 0)])
+    out = chain.place(out, where(OWN[1], SUM_HOME[2]), [(own_a, 1), (own_a_in, 1)], [(far_2, 0)])
+    out = chain.place(out, where(OWN[2], SUM_AWAY[2]), [(own_a, 2), (own_a_in, 2)], [(over_2, 0)])
+    out = chain.place(out, where(OWN[3], SUM_AWAY[3]), [(own_b, 0), (own_b_in, 0)], [(over_3, 0)])
+    return out
 
 
 def regroup_rows(amps, owner_map, tile_size):
@@ -58,4 +386,6 @@
         P(),
     )
     out_specs = P(("group", "narrow"), "wide", "sub")
-    return jax.shard_map(shards, mesh=mesh, in_specs=in_specs, out_specs=out_specs, check_vma=False)
+    planes = (mesh.shape["wide"], mesh.shape["narrow"], mesh.shape["sub"]) == (4, 2, 2)
+    body = plane_shards if planes else shards
+    return jax.shard_map(body, mesh=mesh, in_specs=in_specs, out_specs=out_specs, check_vma=False)

time: 771 us -> 370 us (0.48)
  blocking collectives: 366 us -> 0 us
  Pallas kernels: 0 us -> 159 us
  waiting for transfers between devices: 225 us -> 90.9 us
  starting transfers between devices: 0.22 us -> 58.5 us
  local copies, waits for them, and re-layouts: 95.7 us -> 48.6 us
  matrix products: 43.4 us -> 0 us
  other arithmetic: 24.6 us -> 7.15 us
  between operations: 13.4 us -> 0.29 us
    all_to_all x1 -> x0, blocking collectives: 366 us -> none  [regroup_rows(): lax.all_to_all(ordered, 'wide', split_axis=1, concat_axis=0, tiled=True)]
    reduce_scatter x1 -> x0, waiting for transfers between devices: 190 us -> none  [shards(): lax.psum_scatter(rounded, 'narrow', scatter_dimension=0, tiled=True)]
    pallas_call x0 -> x45, Pallas kernels: none -> 159 us  [call(): pl.pallas_call(body, out_shape=out_shape, grid_spec=pltpu.PrefetchScalarG...]
    ppermute x0 -> x25, waiting for transfers between devices: none -> 90.9 us  [the longest x20 90.7 us: move(): return lax.ppermute(x, both, pairs)]
    ppermute x0 -> x25, starting transfers between devices: none -> 58.5 us  [the longest x20 57.6 us: move(): return lax.ppermute(x, both, pairs)]
    unnamed x2 -> x6, local copies, waits for them, and re-layouts: 0.46 us -> 46.2 us
    dot_general x1 -> x0, matrix products: 43.4 us -> none  [shards(): jnp.einsum('ikac,kcb->iab', blocks, masked_w, preferred_element_type=jnp....]
    select_n x1 -> x0, local copies, waits for them, and re-layouts: 38 us -> none  [regroup_rows(): jnp.take(amps.reshape(pair_count, virt_count // tile_size, tile_size, c_c...]
  transfers between devices with their start and end apart: 2 -> 25, of which waited for: 2 -> 9; matrix products, arithmetic and copies ran while one was open for 2% -> 14% of each run, Pallas kernels for 0% -> 42%
where the time goes in v2:
time: 370 us; the launch traced here: 364 us
  Pallas kernels  159 us (43%)
  waiting for transfers between devices  90.9 us (25%)
  starting transfers between devices  58.5 us (16%)
  local copies, waits for them, and re-layouts  48.6 us (13%)
  other arithmetic  7.15 us (2%)
    pallas_call x45, Pallas kernels, call(): pl.pallas_call(body, out_shape=out_shape, grid_spec=pltpu.PrefetchScalarG...  159 us
    ppermute x20, waiting for transfers between devices, move(): return lax.ppermute(x, both, pairs)  90.7 us
    ppermute x20, starting transfers between devices, move(): return lax.ppermute(x, both, pairs)  57.6 us
    unnamed x6, local copies, waits for them, and re-layouts  46.2 us
  transfers between devices with their start and end apart: 25, of which 9 were waited for; matrix products, arithmetic and copies ran while one was open for 14% of the time, Pallas kernels for 42%

profile of v2, /device:TPU:8, one launch (start us, length us, event | category | flops | bytes accessed | tf_op | source)
XLA Modules:
  0.0 364.5 jit_solution(7679562305675749037)
XLA Ops:
  27.4 5.9 %contract.12.refs_3_ = bf16[1,512,1024]{2,1,0:T(8,128)(2,1)} custom-call(bf16[1,2,512,512]{3,2,1,0:T(8,128)(2,1)} %order_tiles.5.refs_11_.refs_0_, bf16[1,2,512,512]{3,2,1,0:T(8,128)(2,1)} %collective-permute-done.2.refs_1_, bf16[2,2,512,1024]{3,2,1,0:T(8,128)(2,1)} %mask_integrals.1.refs_11_.refs_2_, bf16[3,2,512,512]{3,2,1,0:T(8,128)(2,1)} %order_tiles.7.refs_3_.refs_0_), custom_call_target="tpu_custom_call" | custom-call | flops 999999995904 | bytes 1000000000 | tf_op jit(solution)/shard_map/contract/pallas_call | solution.py:40
  34.8 5.9 %contract.13.refs_3_ = bf16[1,512,1024]{2,1,0:T(8,128)(2,1)} custom-call(bf16[1,2,512,512]{3,2,1,0:T(8,128)(2,1)} %order_tiles.6.refs_3_.refs_0_, bf16[1,2,512,512]{3,2,1,0:T(8,128)(2,1)} %collective-permute-done.1.refs_1_, bf16[2,2,512,1024]{3,2,1,0:T(8,128)(2,1)} %mask_integrals.1.refs_11_.refs_2_, bf16[1,512,1024]{2,1,0:T(8,128)(2,1)} %contract.12.refs_3_), custom_call_target="tpu_custom_call" | custom-call | flops 999999995904 | bytes 1000000000 | tf_op jit(solution)/shard_map/contract/pallas_call | solution.py:40
  54.3 5.9 %contract.15.refs_3_.refs_0_ = bf16[1,512,1024]{2,1,0:T(8,128)(2,1)} custom-call(bf16[3,2,512,512]{3,2,1,0:T(8,128)(2,1)} %order_tiles.7.refs_3_.refs_0_, bf16[3,2,512,512]{3,2,1,0:T(8,128)(2,1)} %collective-permute-done.refs_1_, bf16[2,2,512,1024]{3,2,1,0:T(8,128)(2,1)} %mask_integrals.1.refs_11_.refs_2_, bf16[3,2,512,512]{3,2,1,0:T(8,128)(2,1)} %order_tiles.8.refs_3_.refs_0_), custom_call_target="tpu_custom_call" | custom-call | flops 999999995904 | bytes 1000000000 | tf_op jit(solution)/shard_map/contract/pallas_call | solution.py:40
  66.2 10.4 %order_tiles.9.refs_2_.refs_0_ = bf16[8,2,512,512]{3,2,1,0:T(8,128)(2,1)} custom-call(s32[2,16]{1,0:T(2,128)} %pad_add_fusion.refs_0_.refs_11_, s32[32]{0:T(128)} %refs_1_.9, f32[8,32,512]{2,1,0:T(8,128)} %reshape.9.refs_2_, bf16[8,2048,512]{2,1,0:T(8,128)(2,1)} %refs_10_.9, bf16[8,2048,512]{2,1,0:T(8,128)(2,1)} %refs_10_.9, bf16[8,2048,512]{2,1,0:T(8,128)(2,1)} %refs_10_.9, ...), custom_call_target="tpu_custom_call" | custom-call | flops 999999995904 | bytes 1000000000 | tf_op jit(solution)/shard_map/order_tiles/pallas_call | solution.py:40
  80.4 5.8 %contract.17.refs_3_ = bf16[1,512,1024]{2,1,0:T(8,128)(2,1)} custom-call(bf16[3,2,512,512]{3,2,1,0:T(8,128)(2,1)} %order_tiles.7.refs_3_.refs_0_, bf16[3,2,512,512]{3,2,1,0:T(8,128)(2,1)} %collective-permute-done.refs_1_, bf16[2,2,512,1024]{3,2,1,0:T(8,128)(2,1)} %mask_integrals.1.refs_11_.refs_2_, bf16[1,512,1024]{2,1,0:T(8,128)(2,1)} %add.102.refs_3_), custom_call_target="tpu_custom_call" | custom-call | flops 999999995904 | bytes 1000000000 | tf_op jit(solution)/shard_map/contract/pallas_call | solution.py:40
  87.2 5.9 %contract.18.refs_2_.refs_0_ = bf16[1,512,1024]{2,1,0:T(8,128)(2,1)} custom-call(bf16[3,2,512,512]{3,2,1,0:T(8,128)(2,1)} %order_tiles.8.refs_3_.refs_0_, bf16[3,2,512,512]{3,2,1,0:T(8,128)(2,1)} %collective-permute-done.3.refs_1_, bf16[2,2,512,1024]{3,2,1,0:T(8,128)(2,1)} %mask_integrals.1.refs_11_.refs_2_, bf16[1,512,1024]{2,1,0:T(8,128)(2,1)} %contract.17.refs_3_), custom_call_target="tpu_custom_call" | custom-call | flops 999999995904 | bytes 1000000000 | tf_op jit(solution)/shard_map/contract/pallas_call | solution.py:40
  99.0 8.6 %contract.19.refs_3_.refs_0_ = bf16[2,512,1024]{2,1,0:T(8,128)(2,1)} custom-call(bf16[8,2,512,512]{3,2,1,0:T(8,128)(2,1)} %order_tiles.9.refs_2_.refs_0_, bf16[8,2,512,512]{3,2,1,0:T(8,128)(2,1)} %collective-permute-done.4.refs_1_, bf16[2,2,512,1024]{3,2,1,0:T(8,128)(2,1)} %mask_integrals.1.refs_11_.refs_2_, bf16[1,512,1024]{2,1,0:T(8,128)(2,1)} %hand_on.13.refs_3_.refs_0_), custom_call_target="tpu_custom_call" | custom-call | flops 999999995904 | bytes 1000000000 | tf_op jit(solution)/shard_map/contract/pallas_call | solution.py:40
  109.0 5.9 %contract.20.refs_2_.refs_0_ = bf16[1,512,1024]{2,1,0:T(8,128)(2,1)} custom-call(bf16[3,2,512,512]{3,2,1,0:T(8,128)(2,1)} %order_tiles.8.refs_3_.refs_0_, bf16[3,2,512,512]{3,2,1,0:T(8,128)(2,1)} %collective-permute-done.3.refs_1_, bf16[2,2,512,1024]{3,2,1,0:T(8,128)(2,1)} %mask_integrals.1.refs_11_.refs_2_, bf16[2,512,1024]{2,1,0:T(8,128)(2,1)} %contract.19.refs_3_.refs_0_), custom_call_target="tpu_custom_call" | custom-call | flops 999999995904 | bytes 1000000000 | tf_op jit(solution)/shard_map/contract/pallas_call | solution.py:40
  114.9 6.7 %collective-permute-start.10 = (bf16[1,512,1024]{2,1,0:T(8,128)(2,1)}, bf16[1,512,1024]{2,1,0:T(8,128)(2,1)}, u32[]{:S(2)}, u32[]{:S(2)}) collective-permute-start(bf16[1,512,1024]{2,1,0:T(8,128)(2,1)} %contract.20.refs_2_.refs_0_), channel_id=1, source_target_pairs={{0,2},{4,6},{10,8},{14,12},{1,3},{5,7},{11,9},{15,13},{16,18},{20,... | collective-permute-start | bytes 3145736 | tf_op jit(solution)/shard_map/ppermute | solution.py:232
  126.4 18.2 %collective-permute-done.10.refs_1_ = bf16[1,512,1024]{2,1,0:T(8,128)(2,1)} collective-permute-done((bf16[1,512,1024]{2,1,0:T(8,128)(2,1)}, bf16[1,512,1024]{2,1,0:T(8,128)(2,1)}, u32[]{:S(2)}, u32[]{:S(2)}) %collective-permute-start.10) | collective-permute-done | bytes 1048608 | tf_op jit(solution)/shard_map/ppermute | solution.py:232
  152.6 8.5 %contract.21.refs_1_.refs_0_ = bf16[2,512,1024]{2,1,0:T(8,128)(2,1)} custom-call(bf16[8,2,512,512]{3,2,1,0:T(8,128)(2,1)} %order_tiles.9.refs_2_.refs_0_, bf16[8,2,512,512]{3,2,1,0:T(8,128)(2,1)} %collective-permute-done.4.refs_1_, bf16[2,2,512,1024]{3,2,1,0:T(8,128)(2,1)} %mask_integrals.1.refs_11_.refs_2_, bf16[1,512,1024]{2,1,0:T(8,128)(2,1)} %hand_on.16.refs_3_), custom_call_target="tpu_custom_call" | custom-call | flops 999999995904 | bytes 1000000000 | tf_op jit(solution)/shard_map/contract/pallas_call | solution.py:40
  177.9 12.5 %collective-permute-done.16.refs_0_ = bf16[1,512,1024]{2,1,0:T(8,128)(2,1)} collective-permute-done((bf16[1,512,1024]{2,1,0:T(8,128)(2,1)}, bf16[1,512,1024]{2,1,0:T(8,128)(2,1)}, u32[]{:S(2)}, u32[]{:S(2)}) %collective-permute-start.16) | collective-permute-done | bytes 1048608 | tf_op jit(solution)/shard_map/ppermute | solution.py:232
  194.2 6.0 %collective-permute-start.17 = (bf16[1,512,1024]{2,1,0:T(8,128)(2,1)}, bf16[1,512,1024]{2,1,0:T(8,128)(2,1)}, u32[]{:S(2)}, u32[]{:S(2)}) collective-permute-start(bf16[1,512,1024]{2,1,0:T(8,128)(2,1)} %hand_on.20.refs_3_.refs_2_), channel_id=1, source_target_pairs={{0,2},{4,6},{10,8},{14,12},{1,3},{5,7},{11,9},{15,13},{16,18},{20,... | collective-permute-start | bytes 3145736 | tf_op jit(solution)/shard_map/ppermute | solution.py:232
  200.2 11.2 %contract.22.refs_2_.refs_1_ = bf16[3,512,1024]{2,1,0:T(8,128)(2,1)} custom-call(bf16[8,2,512,512]{3,2,1,0:T(8,128)(2,1)} %order_tiles.9.refs_2_.refs_0_, bf16[8,2,512,512]{3,2,1,0:T(8,128)(2,1)} %collective-permute-done.4.refs_1_, bf16[2,2,512,1024]{3,2,1,0:T(8,128)(2,1)} %mask_integrals.1.refs_11_.refs_2_, bf16[1,512,1024]{2,1,0:T(8,128)(2,1)} %hand_on.20.refs_3_.refs_2_), custom_call_target="tpu_custom_call" | custom-call | flops 999999995904 | bytes 1000000000 | tf_op jit(solution)/shard_map/contract/pallas_call | solution.py:40
  223.3 6.3 %collective-permute-start.21 = (bf16[1,512,1024]{2,1,0:T(8,128)(2,1)}, bf16[1,512,1024]{2,1,0:T(8,128)(2,1)}, u32[]{:S(2)}, u32[]{:S(2)}) collective-permute-start(bf16[1,512,1024]{2,1,0:T(8,128)(2,1)} %hand_on.23.refs_4_.refs_3_), channel_id=1, source_target_pairs={{0,2},{4,6},{10,8},{14,12},{1,3},{5,7},{11,9},{15,13},{16,18},{20,... | collective-permute-start | bytes 3145736 | tf_op jit(solution)/shard_map/ppermute | solution.py:232
  229.6 11.4 %collective-permute-done.13.refs_1_ = bf16[2,512,1024]{2,1,0:T(8,128)(2,1)} collective-permute-done((bf16[2,512,1024]{2,1,0:T(8,128)(2,1)}, bf16[2,512,1024]{2,1,0:T(8,128)(2,1)}, u32[]{:S(2)}, u32[]{:S(2)}) %collective-permute-start.13) | collective-permute-done | bytes 2097184 | tf_op jit(solution)/shard_map/ppermute | solution.py:232
  244.4 7.6 %copy.40.refs_3_ = bf16[8,512,1024]{2,1,0:T(8,128)(2,1)} copy(bf16[8,512,1024]{2,1,0:T(8,128)(2,1)} %place.8.refs_4_) | data formatting | bytes 16777216
  262.2 8.4 %collective-permute-start.22 = (bf16[1,512,1024]{2,1,0:T(8,128)(2,1)}, bf16[1,512,1024]{2,1,0:T(8,128)(2,1)}, u32[]{:S(2)}, u32[]{:S(2)}) collective-permute-start(bf16[1,512,1024]{2,1,0:T(8,128)(2,1)} %hand_on.25.refs_4_), channel_id=1, source_target_pairs={{0,2},{4,6},{10,8},{14,12},{1,3},{5,7},{11,9},{15,13},{16,18},{20,... | collective-permute-start | bytes 3145736 | tf_op jit(solution)/shard_map/ppermute | solution.py:232
  270.6 35.5 %collective-permute-done.24.refs_1_ = bf16[2,512,1024]{2,1,0:T(8,128)(2,1)} collective-permute-done((bf16[2,512,1024]{2,1,0:T(8,128)(2,1)}, bf16[2,512,1024]{2,1,0:T(8,128)(2,1)}, u32[]{:S(2)}, u32[]{:S(2)}) %collective-permute-start.24) | collective-permute-done | bytes 2097184 | tf_op jit(solution)/shard_map/ppermute | solution.py:232
  309.2 7.8 %copy.44.refs_3_ = bf16[8,512,1024]{2,1,0:T(8,128)(2,1)} copy(bf16[8,512,1024]{2,1,0:T(8,128)(2,1)} %place.10.refs_4_) | data formatting | bytes 16777216
  319.9 7.6 %copy.45.refs_4_ = bf16[8,512,1024]{2,1,0:T(8,128)(2,1)} copy(bf16[8,512,1024]{2,1,0:T(8,128)(2,1)} %place.11.refs_5_) | data formatting | bytes 16777216
  331.0 7.8 %copy.46.refs_4_ = bf16[8,512,1024]{2,1,0:T(8,128)(2,1)} copy(bf16[8,512,1024]{2,1,0:T(8,128)(2,1)} %place.12.refs_5_) | data formatting | bytes 16777216
  342.2 7.6 %copy.47.refs_4_ = bf16[8,512,1024]{2,1,0:T(8,128)(2,1)} copy(bf16[8,512,1024]{2,1,0:T(8,128)(2,1)} %place.13.refs_5_) | data formatting | bytes 16777216
  353.3 7.8 %copy.48.refs_4_ = bf16[8,512,1024]{2,1,0:T(8,128)(2,1)} copy(bf16[8,512,1024]{2,1,0:T(8,128)(2,1)} %place.14.refs_5_) | data formatting | bytes 16777216
  (94 shorter events, 139.1 us)
Async XLA Ops:
  6.7 20.6 %collective-permute-start.2 = (bf16[1,2,512,512]{3,2,1,0:T(8,128)(2,1)}, bf16[1,2,512,512]{3,2,1,0:T(8,128)(2,1)}, u32[]{:S(2)}, u32[]{:S(2)}) collective-permute-start(bf16[1,2,512,512]{3,2,1,0:T(8,128)(2,1)} %order_tiles.5.refs_11_.refs_0_), channel_id=1, source_target_pairs={{0,1},{1,0},{2,3},{3,2},{4,5},{5,4},{6,7},{7,6},{8,9},{9,8},{10,11... | collective-permute-start | bytes 3145736 | tf_op jit(solution)/shard_map/ppermute | solution.py:257
  10.0 24.8 %collective-permute-start.1 = (bf16[1,2,512,512]{3,2,1,0:T(8,128)(2,1)}, bf16[1,2,512,512]{3,2,1,0:T(8,128)(2,1)}, u32[]{:S(2)}, u32[]{:S(2)}) collective-permute-start(bf16[1,2,512,512]{3,2,1,0:T(8,128)(2,1)} %order_tiles.6.refs_3_.refs_0_), channel_id=1, source_target_pairs={{0,1},{1,0},{2,3},{3,2},{4,5},{5,4},{6,7},{7,6},{8,9},{9,8},{10,11... | collective-permute-start | bytes 3145736 | tf_op jit(solution)/shard_map/ppermute | solution.py:257
  22.8 19.4 %collective-permute-start = (bf16[3,2,512,512]{3,2,1,0:T(8,128)(2,1)}, bf16[3,2,512,512]{3,2,1,0:T(8,128)(2,1)}, u32[]{:S(2)}, u32[]{:S(2)}) collective-permute-start(bf16[3,2,512,512]{3,2,1,0:T(8,128)(2,1)} %order_tiles.7.refs_3_.refs_0_), channel_id=1, source_target_pairs={{0,1},{1,0},{2,3},{3,2},{4,5},{5,4},{6,7},{7,6},{8,9},{9,8},{10,11... | collective-permute-start | bytes 9437192 | tf_op jit(solution)/shard_map/ppermute | solution.py:257
  33.2 65.7 %collective-permute-start.5 = (bf16[1,512,1024]{2,1,0:T(8,128)(2,1)}, bf16[1,512,1024]{2,1,0:T(8,128)(2,1)}, u32[]{:S(2)}, u32[]{:S(2)}) collective-permute-start(bf16[1,512,1024]{2,1,0:T(8,128)(2,1)} %contract.12.refs_3_), channel_id=1, source_target_pairs={{0,12},{2,14},{4,8},{6,10},{10,6},{8,4},{14,2},{12,0},{1,13},{3,15... | collective-permute-start | bytes 3145736 | tf_op jit(solution)/shard_map/ppermute | solution.py:232
  40.7 36.2 %collective-permute-start.7 = (bf16[1,512,1024]{2,1,0:T(8,128)(2,1)}, bf16[1,512,1024]{2,1,0:T(8,128)(2,1)}, u32[]{:S(2)}, u32[]{:S(2)}) collective-permute-start(bf16[1,512,1024]{2,1,0:T(8,128)(2,1)} %contract.13.refs_3_), channel_id=1, source_target_pairs={{2,0},{6,4},{8,10},{12,14},{0,2},{4,6},{10,8},{14,12},{3,1},{7,5},... | collective-permute-start | bytes 3145736 | tf_op jit(solution)/shard_map/ppermute | solution.py:232
  53.8 39.2 %collective-permute-start.6 = (bf16[1,512,1024]{2,1,0:T(8,128)(2,1)}, bf16[1,512,1024]{2,1,0:T(8,128)(2,1)}, u32[]{:S(2)}, u32[]{:S(2)}) collective-permute-start(bf16[1,512,1024]{2,1,0:T(8,128)(2,1)} %contract.14.refs_11_), channel_id=1, source_target_pairs={{2,0},{6,4},{8,10},{12,14},{0,2},{4,6},{10,8},{14,12},{3,1},{7,5},... | collective-permute-start | bytes 3145736 | tf_op jit(solution)/shard_map/ppermute | solution.py:232
  76.6 22.4 %collective-permute-start.4 = (bf16[8,2,512,512]{3,2,1,0:T(8,128)(2,1)}, bf16[8,2,512,512]{3,2,1,0:T(8,128)(2,1)}, u32[]{:S(2)}, u32[]{:S(2)}) collective-permute-start(bf16[8,2,512,512]{3,2,1,0:T(8,128)(2,1)} %order_tiles.9.refs_2_.refs_0_), channel_id=1, source_target_pairs={{0,1},{1,0},{2,3},{3,2},{4,5},{5,4},{6,7},{7,6},{8,9},{9,8},{10,11... | collective-permute-start | bytes 25165832 | tf_op jit(solution)/shard_map/ppermute | solution.py:257
  79.4 71.3 %collective-permute-start.9 = (bf16[1,512,1024]{2,1,0:T(8,128)(2,1)}, bf16[1,512,1024]{2,1,0:T(8,128)(2,1)}, u32[]{:S(2)}, u32[]{:S(2)}) collective-permute-start(bf16[1,512,1024]{2,1,0:T(8,128)(2,1)} %add.102.refs_3_), channel_id=1, source_target_pairs={{0,8},{2,14},{4,12},{6,10},{10,2},{8,4},{14,6},{12,0},{1,9},{3,15}... | collective-permute-start | bytes 3145736 | tf_op jit(solution)/shard_map/ppermute | solution.py:232
  86.3 35.3 %collective-permute-start.11 = (bf16[1,512,1024]{2,1,0:T(8,128)(2,1)}, bf16[1,512,1024]{2,1,0:T(8,128)(2,1)}, u32[]{:S(2)}, u32[]{:S(2)}) collective-permute-start(bf16[1,512,1024]{2,1,0:T(8,128)(2,1)} %contract.17.refs_3_), channel_id=1, source_target_pairs={{2,0},{6,4},{8,10},{12,14},{0,2},{4,6},{10,8},{14,12},{3,1},{7,5},... | collective-permute-start | bytes 3145736 | tf_op jit(solution)/shard_map/ppermute | solution.py:232
  95.5 98.7 %collective-permute-start.15 = (bf16[1,512,1024]{2,1,0:T(8,128)(2,1)}, bf16[1,512,1024]{2,1,0:T(8,128)(2,1)}, u32[]{:S(2)}, u32[]{:S(2)}) collective-permute-start(bf16[1,512,1024]{2,1,0:T(8,128)(2,1)} %add.103.refs_1_), channel_id=1, source_target_pairs={{0,12},{2,10},{4,8},{6,14},{10,6},{8,0},{14,2},{12,4},{1,13},{3,11... | collective-permute-start | bytes 3145736 | tf_op jit(solution)/shard_map/ppermute | solution.py:232
  107.5 62.9 %collective-permute-start.8 = (bf16[2,512,1024]{2,1,0:T(8,128)(2,1)}, bf16[2,512,1024]{2,1,0:T(8,128)(2,1)}, u32[]{:S(2)}, u32[]{:S(2)}) collective-permute-start(bf16[2,512,1024]{2,1,0:T(8,128)(2,1)} %contract.19.refs_3_.refs_0_), channel_id=1, source_target_pairs={{2,0},{6,4},{8,10},{12,14},{3,1},{7,5},{9,11},{13,15},{18,16},{22,... | collective-permute-start | bytes 6291464 | tf_op jit(solution)/shard_map/ppermute | solution.py:232
  114.9 29.6 %collective-permute-start.10 = (bf16[1,512,1024]{2,1,0:T(8,128)(2,1)}, bf16[1,512,1024]{2,1,0:T(8,128)(2,1)}, u32[]{:S(2)}, u32[]{:S(2)}) collective-permute-start(bf16[1,512,1024]{2,1,0:T(8,128)(2,1)} %contract.20.refs_2_.refs_0_), channel_id=1, source_target_pairs={{0,2},{4,6},{10,8},{14,12},{1,3},{5,7},{11,9},{15,13},{16,18},{20,... | collective-permute-start | bytes 3145736 | tf_op jit(solution)/shard_map/ppermute | solution.py:232
  124.1 40.9 %collective-permute-start.12 = (bf16[1,512,1024]{2,1,0:T(8,128)(2,1)}, bf16[1,512,1024]{2,1,0:T(8,128)(2,1)}, u32[]{:S(2)}, u32[]{:S(2)}) collective-permute-start(bf16[1,512,1024]{2,1,0:T(8,128)(2,1)} %hand_on.14.refs_2_), channel_id=1, source_target_pairs={{0,2},{4,6},{10,8},{14,12},{1,3},{5,7},{11,9},{15,13},{16,18},{20,... | collective-permute-start | bytes 3145736 | tf_op jit(solution)/shard_map/ppermute | solution.py:232
  150.7 72.6 %collective-permute-start.14 = (bf16[1,512,1024]{2,1,0:T(8,128)(2,1)}, bf16[1,512,1024]{2,1,0:T(8,128)(2,1)}, u32[]{:S(2)}, u32[]{:S(2)}) collective-permute-start(bf16[1,512,1024]{2,1,0:T(8,128)(2,1)} %hand_on.16.refs_3_), channel_id=1, source_target_pairs={{0,8},{2,14},{4,12},{6,10},{10,2},{8,4},{14,6},{12,0},{1,9},{3,15}... | collective-permute-start | bytes 3145736 | tf_op jit(solution)/shard_map/ppermute | solution.py:232
  161.1 51.5 %collective-permute-start.18 = (bf16[2,512,1024]{2,1,0:T(8,128)(2,1)}, bf16[2,512,1024]{2,1,0:T(8,128)(2,1)}, u32[]{:S(2)}, u32[]{:S(2)}) collective-permute-start(bf16[2,512,1024]{2,1,0:T(8,128)(2,1)} %contract.21.refs_1_.refs_0_), channel_id=1, source_target_pairs={{2,0},{6,4},{8,10},{12,14},{3,1},{7,5},{9,11},{13,15},{18,16},{22,... | collective-permute-start | bytes 6291464 | tf_op jit(solution)/shard_map/ppermute | solution.py:232
  165.0 25.3 %collective-permute-start.16 = (bf16[1,512,1024]{2,1,0:T(8,128)(2,1)}, bf16[1,512,1024]{2,1,0:T(8,128)(2,1)}, u32[]{:S(2)}, u32[]{:S(2)}) collective-permute-start(bf16[1,512,1024]{2,1,0:T(8,128)(2,1)} %hand_on.18.refs_2_), channel_id=1, source_target_pairs={{0,2},{4,6},{10,8},{14,12},{1,3},{5,7},{11,9},{15,13},{16,18},{20,... | collective-permute-start | bytes 3145736 | tf_op jit(solution)/shard_map/ppermute | solution.py:232
  174.8 66.2 %collective-permute-start.13 = (bf16[2,512,1024]{2,1,0:T(8,128)(2,1)}, bf16[2,512,1024]{2,1,0:T(8,128)(2,1)}, u32[]{:S(2)}, u32[]{:S(2)}) collective-permute-start(bf16[2,512,1024]{2,1,0:T(8,128)(2,1)} %add.106.refs_1_), channel_id=1, source_target_pairs={{0,4},{4,0},{10,14},{14,10},{1,5},{5,1},{11,15},{15,11},{16,20},{2... | collective-permute-start | bytes 6291464 | tf_op jit(solution)/shard_map/ppermute | solution.py:232
  194.2 27.8 %collective-permute-start.17 = (bf16[1,512,1024]{2,1,0:T(8,128)(2,1)}, bf16[1,512,1024]{2,1,0:T(8,128)(2,1)}, u32[]{:S(2)}, u32[]{:S(2)}) collective-permute-start(bf16[1,512,1024]{2,1,0:T(8,128)(2,1)} %hand_on.20.refs_3_.refs_2_), channel_id=1, source_target_pairs={{0,2},{4,6},{10,8},{14,12},{1,3},{5,7},{11,9},{15,13},{16,18},{20,... | collective-permute-start | bytes 3145736 | tf_op jit(solution)/shard_map/ppermute | solution.py:232
  211.4 116.2 %collective-permute-start.23 = (bf16[3,512,1024]{2,1,0:T(8,128)(2,1)}, bf16[3,512,1024]{2,1,0:T(8,128)(2,1)}, u32[]{:S(2)}, u32[]{:S(2)}) collective-permute-start(bf16[3,512,1024]{2,1,0:T(8,128)(2,1)} %contract.22.refs_2_.refs_1_), channel_id=1, source_target_pairs={{2,0},{6,4},{8,10},{12,14},{3,1},{7,5},{9,11},{13,15},{18,16},{22,... | collective-permute-start | bytes 9437192 | tf_op jit(solution)/shard_map/ppermute | solution.py:232
  217.0 89.1 %collective-permute-start.24 = (bf16[2,512,1024]{2,1,0:T(8,128)(2,1)}, bf16[2,512,1024]{2,1,0:T(8,128)(2,1)}, u32[]{:S(2)}, u32[]{:S(2)}) collective-permute-start(bf16[2,512,1024]{2,1,0:T(8,128)(2,1)} %add.107.refs_1_), channel_id=1, source_target_pairs={{0,4},{4,0},{10,14},{14,10},{1,5},{5,1},{11,15},{15,11},{16,20},{2... | collective-permute-start | bytes 6291464 | tf_op jit(solution)/shard_map/ppermute | solution.py:232
  222.0 40.2 %collective-permute-start.20 = (bf16[1,512,1024]{2,1,0:T(8,128)(2,1)}, bf16[1,512,1024]{2,1,0:T(8,128)(2,1)}, u32[]{:S(2)}, u32[]{:S(2)}) collective-permute-start(bf16[1,512,1024]{2,1,0:T(8,128)(2,1)} %hand_on.22.refs_1_), channel_id=1, source_target_pairs={{2,10},{6,14},{8,0},{12,4},{3,11},{7,15},{9,1},{13,5},{18,26},{22,... | collective-permute-start | bytes 3145736 | tf_op jit(solution)/shard_map/ppermute | solution.py:232
  223.3 38.9 %collective-permute-start.21 = (bf16[1,512,1024]{2,1,0:T(8,128)(2,1)}, bf16[1,512,1024]{2,1,0:T(8,128)(2,1)}, u32[]{:S(2)}, u32[]{:S(2)}) collective-permute-start(bf16[1,512,1024]{2,1,0:T(8,128)(2,1)} %hand_on.23.refs_4_.refs_3_), channel_id=1, source_target_pairs={{0,2},{4,6},{10,8},{14,12},{1,3},{5,7},{11,9},{15,13},{16,18},{20,... | collective-permute-start | bytes 3145736 | tf_op jit(solution)/shard_map/ppermute | solution.py:232
  260.9 100.2 %collective-permute-start.19 = (bf16[1,512,1024]{2,1,0:T(8,128)(2,1)}, bf16[1,512,1024]{2,1,0:T(8,128)(2,1)}, u32[]{:S(2)}, u32[]{:S(2)}) collective-permute-start(bf16[1,512,1024]{2,1,0:T(8,128)(2,1)} %contract.23.refs_1_), channel_id=1, source_target_pairs={{2,0},{6,4},{8,10},{12,14},{3,1},{7,5},{9,11},{13,15},{18,16},{22,... | collective-permute-start | bytes 3145736 | tf_op jit(solution)/shard_map/ppermute | solution.py:232
  262.2 98.8 %collective-permute-start.22 = (bf16[1,512,1024]{2,1,0:T(8,128)(2,1)}, bf16[1,512,1024]{2,1,0:T(8,128)(2,1)}, u32[]{:S(2)}, u32[]{:S(2)}) collective-permute-start(bf16[1,512,1024]{2,1,0:T(8,128)(2,1)} %hand_on.25.refs_4_), channel_id=1, source_target_pairs={{0,2},{4,6},{10,8},{14,12},{1,3},{5,7},{11,9},{15,13},{16,18},{20,... | collective-permute-start | bytes 3145736 | tf_op jit(solution)/shard_map/ppermute | solution.py:232
  (1 other events, 6.0 us)

commit v3 on v0

--- a/solution.py
+++ b/solution.py
@@ -1,7 +1,431 @@
 import jax
 import jax.numpy as jnp
 from jax import lax
+from jax.experimental import pallas as pl
+from jax.experimental.pallas import tpu as pltpu
 from jax.sharding import PartitionSpec as P
+
+BF16 = jnp.bfloat16
+F32 = jnp.float32
+MIB = 2**20
+
+SUM_HOME = [(0, 2), (1, 3), (2, 2)]
+SUM_AWAY = [(0, 3), (1, 2), (2, 3), (3, 2)]
+SUM_LAST = (3, 3)
+NEAR = [(0, 1), (1, 1), (2, 1), (3, 1)]
+OWN = [(0, 0), (1, 0), (2, 0), (3, 0)]
+
+ANY = pl.BlockSpec(memory_space=pl.ANY)
+COST = pl.CostEstimate(flops=10**12, bytes_accessed=10**9, transcendentals=0)
+
+
+def pick(values, index):
+    chosen = values[0]
+    for at, value in enumerate(values[1:], 1):
+        chosen = jnp.where(index == at, value, chosen)
+    return chosen
+
+
+def widen(mask, tile_size, tile_dim):
+    tiles = mask.shape[tile_dim]
+    shape = (tiles, tiles * tile_size)
+    column = lax.broadcasted_iota(jnp.int32, shape, 1)
+    first = lax.broadcasted_iota(jnp.int32, shape, 0) * tile_size
+    spread = (column >= first) & (column < first + tile_size)
+    return lax.dot_general(
+        mask.astype(F32), spread.astype(F32), (((tile_dim,), (0,)), ((), ())), preferred_element_type=F32
+    )
+
+
+class Chain:
+    def __init__(self):
+        self.before = None
+
+    def call(
+        self, kernel, name, operands, out_shape, grid, in_specs, out_specs, prefetch=(), aliases=None, scratch=()
+    ):
+        skip = len(prefetch) + len(operands)
+        before = self.before
+        known = before is None or any(before is operand for operand in operands)
+        after = () if known else (before,)
+
+        def body(*refs):
+            kernel(*refs[:skip], *refs[skip + len(after):])
+
+        result = pl.pallas_call(
+            body,
+            out_shape=out_shape,
+            grid_spec=pltpu.PrefetchScalarGridSpec(
+                num_scalar_prefetch=len(prefetch),
+                grid=grid,
+                in_specs=[*in_specs, *[ANY] * len(after)],
+                out_specs=out_specs,
+                scratch_shapes=scratch,
+            ),
+            input_output_aliases=aliases or {},
+            compiler_params=pltpu.CompilerParams(vmem_limit_bytes=64 * MIB),
+            cost_estimate=COST,
+            name=name,
+        )(*prefetch, *operands, *after)
+        self.before = result[0] if isinstance(result, (list, tuple)) else result
+        return result
+
+    def order_tiles(self, role, owner_map, amps, t_mask, tile_size, blocks):
+        c_here = amps.shape[2]
+        tiles = owner_map.shape[0] // 4
+        rows = tiles * tile_size
+        k_count = 2
+
+        def choose(role, g, part):
+            home, away = ([pair[at][part] for pair in blocks] for at in (0, 1))
+            return pick([h if h == a else jnp.where(role[0] == 1, h, a) for h, a in zip(home, away)], g)
+
+        def tile_of(j, g, role, owner):
+            return owner[(role[1] ^ choose(role, g, 1)) * tiles + j]
+
+        def kernel(role, owner, mask_ref, *refs):
+            out_ref, wide_ref = refs[-2:]
+            g = pl.program_id(0)
+            for k in range(k_count):
+                wide_ref[k] = widen(mask_ref[k], tile_size, 0)
+            for j in range(tiles):
+                tile = tile_of(j, g, role, owner)
+                for k in range(k_count):
+                    scale = wide_ref[k, pl.ds(tile, 1), :].astype(BF16)
+                    out_ref[0, pl.ds(j * tile_size, tile_size), pl.ds(k * c_here, c_here)] = refs[j][k] * scale
+
+        def pair(g, role, owner):
+            return (choose(role, g, 0), 0, 0)
+
+        in_specs = [pl.BlockSpec((k_count, *t_mask.shape[1:]), pair)]
+        for j in range(tiles):
+            in_specs.append(
+                pl.BlockSpec(
+                    (k_count, tile_size, c_here),
+                    lambda g, role, owner, j=j: (choose(role, g, 0), tile_of(j, g, role, owner), 0),
+                )
+            )
+        return self.call(
+            kernel,
+            "order_tiles",
+            (t_mask, *([amps] * tiles)),
+            jax.ShapeDtypeStruct((len(blocks), rows, k_count * c_here), BF16),
+            (len(blocks),),
+            in_specs,
+            pl.BlockSpec((1, rows, k_count * c_here), lambda g, role, owner: (g, 0, 0)),
+            prefetch=(role, owner_map),
+            scratch=[pltpu.VMEM((k_count, t_mask.shape[2], c_here), F32)],
+        )
+
+    def contract_first(self, role, tiles, integrals, w_mask, tile_size):
+        mine, theirs = tiles
+        k_count, c_rows, b_cols = integrals.shape
+        count, rows, _ = mine.shape
+        half = c_rows // 2
+        half_tiles = half // tile_size
+
+        def kernel(role, mask_ref, in_ref, mine_ref, theirs_ref, *refs):
+            *out_refs, weights_ref, wide_ref, total_ref = refs
+            h, k = pl.program_id(0), pl.program_id(1)
+            wide_ref[...] = widen(mask_ref[0], tile_size, 1)
+            for j in range(half_tiles):
+                at = pl.ds(j * tile_size, tile_size)
+                scale = wide_ref[pl.ds((h ^ role[2]) * half_tiles + j, 1), :].astype(BF16)
+                weights_ref[0, at, :] = in_ref[0, at, :] * scale
+
+            def term(ref, block):
+                return jnp.dot(ref[block], weights_ref[0], preferred_element_type=F32)
+
+            for block in range(count):
+
+                @pl.when((h == 0) & (k == 0))
+                def _(block=block):
+                    total_ref[block] = term(mine_ref, block)
+
+                @pl.when((h == 0) & (k > 0))
+                def _(block=block):
+                    total_ref[block] += term(mine_ref, block)
+
+                @pl.when((h == 1) & (k < k_count - 1))
+                def _(block=block):
+                    total_ref[block] += term(theirs_ref, block)
+
+                @pl.when((h == 1) & (k == k_count - 1))
+                def _(block=block):
+                    out_refs[block][0] = (total_ref[block] + term(theirs_ref, block)).astype(BF16)
+
+        block = pl.BlockSpec((count, rows, half), lambda h, k, role: (0, 0, k))
+        return self.call(
+            kernel,
+            "contract_first",
+            (w_mask, integrals, mine, theirs),
+            [
+                *[jax.ShapeDtypeStruct((1, rows, b_cols), BF16)] * count,
+                jax.ShapeDtypeStruct((2, k_count * half, b_cols), BF16),
+            ],
+            (2, k_count),
+            [
+                pl.BlockSpec((1, *w_mask.shape[1:]), lambda h, k, role: (k, 0, 0)),
+                pl.BlockSpec((1, half, b_cols), lambda h, k, role: (k, h ^ role[2], 0)),
+                block,
+                block,
+            ],
+            [
+                *[pl.BlockSpec((1, rows, b_cols), lambda h, k, role: (0, 0, 0))] * count,
+                pl.BlockSpec((1, half, b_cols), lambda h, k, role: (h, k, 0)),
+            ],
+            prefetch=(role,),
+            scratch=[pltpu.VMEM((w_mask.shape[1], b_cols), F32), pltpu.VMEM((count, rows, b_cols), F32)],
+        )
+
+    def contract_apart(self, tiles, weights, first, count):
+        mine, theirs = tiles
+        _, rows, depth = mine.shape
+        b_cols = weights.shape[2]
+        steps = 2
+
+        def kernel(mine_ref, theirs_ref, weights_ref, *out_refs):
+            g = pl.program_id(0)
+            total = jnp.dot(mine_ref[0], weights_ref[0], preferred_element_type=F32)
+            total += jnp.dot(theirs_ref[0], weights_ref[1], preferred_element_type=F32)
+            for at in range(count):
+
+                @pl.when(g == at)
+                def _(out_ref=out_refs[at]):
+                    out_ref[0] = total.astype(BF16)
+
+        block = pl.BlockSpec((1, rows // steps, depth), lambda g, r: (first + g, r, 0))
+
+        def out_block(at):
+            return pl.BlockSpec(
+                (1, rows // steps, b_cols),
+                lambda g, r: (0, jnp.where(g < at, 0, jnp.where(g > at, steps - 1, r)), 0),
+            )
+
+        return self.call(
+            kernel,
+            "contract_apart",
+            (mine, theirs, weights),
+            [jax.ShapeDtypeStruct((1, rows, b_cols), BF16)] * count,
+            (count, steps),
+            [block, block, pl.BlockSpec(weights.shape, lambda g, r: (0, 0, 0))],
+            [out_block(at) for at in range(count)],
+        )
+
+    def contract(self, role, tiles, weights, first, count=1):
+        mine, theirs = tiles
+        _, rows, depth = mine.shape
+        b_cols = weights.shape[2]
+        steps = 2
+
+        def kernel(role, mine_ref, theirs_ref, weights_ref, out_ref):
+            total = jnp.dot(mine_ref[0], weights_ref[0], preferred_element_type=F32)
+            total += jnp.dot(theirs_ref[0], weights_ref[1], preferred_element_type=F32)
+            out_ref[0] = total.astype(BF16)
+
+        block = pl.BlockSpec((1, rows // steps, depth), lambda g, r, role: (first + g, r, 0))
+        return self.call(
+            kernel,
+            "contract",
+            (mine, theirs, weights),
+            jax.ShapeDtypeStruct((count, rows, b_cols), BF16),
+            (count, steps),
+            [block, block, pl.BlockSpec(weights.shape, lambda g, r, role: (0, 0, 0))],
+            pl.BlockSpec((1, rows // steps, b_cols), lambda g, r, role: (g, r, 0)),
+            prefetch=(role,),
+        )
+
+    def add(self, sums):
+        steps = 2
+        count = len(sums)
+        _, rows, b_cols = sums[0][0][0].shape
+
+        def kernel(*refs):
+            out_ref = refs[-1]
+            g = pl.program_id(0)
+            for at in range(count):
+
+                @pl.when(g == at)
+                def _(left=refs[2 * at], right=refs[2 * at + 1]):
+                    out_ref[...] = (left[...].astype(F32) + right[...].astype(F32)).astype(BF16)
+
+        def block(at, index):
+            return pl.BlockSpec(
+                (1, rows // steps, b_cols),
+                lambda g, r: (index, jnp.where(g < at, 0, jnp.where(g > at, steps - 1, r)), 0),
+            )
+
+        return self.call(
+            kernel,
+            "add",
+            tuple(array for both in sums for array, _ in both),
+            jax.ShapeDtypeStruct((count, rows, b_cols), BF16),
+            (count, steps),
+            [block(at, index) for at, both in enumerate(sums) for _, index in both],
+            pl.BlockSpec((1, rows // steps, b_cols), lambda g, r: (g, r, 0)),
+        )
+
+    def hand_on(self, value):
+        return self.call(
+            lambda *refs: None,
+            "hand_on",
+            (value,),
+            jax.ShapeDtypeStruct(value.shape, value.dtype),
+            (1,),
+            [ANY],
+            ANY,
+            aliases={0: 0},
+        )
+
+    def place(self, role, out, home_terms, away_terms, blocks=None, block_count=8):
+        terms = (*home_terms, *away_terms)
+        _, rows, b_cols = terms[0][0].shape
+        steps = 2
+        orbitals = block_count // 2
+
+        def total(refs):
+            if len(refs) == 1:
+                return refs[0][...]
+            return (refs[0][...].astype(F32) + refs[1][...].astype(F32)).astype(BF16)
+
+        def kernel(role, *refs):
+            out_ref = refs[-1]
+            split = len(home_terms)
+
+            @pl.when(role[0] == 1)
+            def _():
+                out_ref[...] = total(refs[:split])
+
+            @pl.when(role[0] == 0)
+            def _():
+                out_ref[...] = total(refs[split:len(terms)])
+
+        def block(index):
+            return pl.BlockSpec((1, rows // steps, b_cols), lambda r, role: (index, r, 0))
+
+        def slot(role):
+            if blocks is None:
+                return 0
+            orbital, distance = (jnp.where(role[0] == 1, *pair) for pair in zip(*blocks))
+            return ((role[1] ^ distance) % 2) * orbitals + orbital
+
+        held = () if out is None else (out,)
+        return self.call(
+            kernel,
+            "place",
+            (*[array for array, _ in terms], *held),
+            jax.ShapeDtypeStruct((block_count, rows, b_cols), BF16),
+            (steps,),
+            [block(index) for _, index in terms] + [ANY] * len(held),
+            pl.BlockSpec((1, rows // steps, b_cols), lambda r, role: (slot(role), r, 0)),
+            prefetch=(role,),
+            aliases={1 + len(terms): 0} if held else None,
+        )
+
+
+def plane_shards(amplitudes, t_mask, integrals, w_mask, owner_map):
+    tile_size = integrals.shape[1] // w_mask.shape[1]
+    at_wide = lax.axis_index("wide")
+    home = (lax.axis_index("narrow") == at_wide // 2).astype(jnp.int32)
+    role = jnp.stack([home, at_wide, lax.axis_index("sub")])
+    masks = jnp.swapaxes(t_mask, 1, 2)
+    both = ("wide", "narrow")
+
+    def device(w, at_home):
+        return w * 2 + (w // 2 if at_home else 1 - w // 2)
+
+    def move(x, pairs):
+        return lax.ppermute(x, both, pairs)
+
+    inward = [(device(w, False), device(w, True)) for w in range(4)]
+    outward = [(device(w, True), device(w, False)) for w in range(4)]
+
+    def far(home_distance=None, away_distance=None):
+        pairs = []
+        for w in range(4):
+            keeper = device(w, True) % 2
+            for at_home, distance in ((True, home_distance), (False, away_distance)):
+                if distance is not None:
+                    pairs.append((device(w, at_home), keeper + 2 * (w ^ distance)))
+        return pairs
+
+    near = [(device(w, True), device(w, True) % 2 + 2 * (w ^ 1)) for w in range(4)]
+    chain = Chain()
+
+    def ordered(blocks):
+        mine = chain.order_tiles(role, owner_map, amplitudes, masks, tile_size, blocks)
+        return mine, lax.ppermute(mine, "sub", [(0, 1), (1, 0)])
+
+    def contract(tiles, first, count=1):
+        return chain.contract(role, tiles, weights, first, count)
+
+    def add(left, right):
+        return chain.add([(left, right)])
+
+    def same(block):
+        return (block, block)
+
+    def place(out, home_block, away_block, home_terms, away_terms):
+        return chain.place(role, out, home_terms, away_terms, (home_block, away_block))
+
+    swap = inward + outward
+    give = [(away, home) for home, away in zip(NEAR, SUM_AWAY)]
+    keep = list(zip(NEAR, SUM_AWAY))
+
+    tiles_a = ordered([give[0], same(SUM_LAST)])
+    tiles_b = ordered([same(SUM_HOME[0]), keep[0]])
+    tiles_c = ordered([give[1], same(SUM_HOME[1]), keep[1], give[2]])
+    give_0, last, weights = chain.contract_first(role, tiles_a, integrals, w_mask, tile_size)
+    got_0 = move(give_0, swap)
+    last_away = move(last, far(None, SUM_LAST[1]))
+    home_0, keep_0 = chain.contract_apart(tiles_b, weights, 0, 2)
+    home_0_in = move(home_0, inward)
+    give_1, home_1 = chain.contract_apart(tiles_c, weights, 0, 2)
+    last_home = move(last, far(SUM_LAST[1], None))
+
+    round_0 = move(add((keep_0, 0), (got_0, 0)), near + far(None, SUM_AWAY[0][1]))
+    got_1 = move(chain.hand_on(give_1), swap)
+    keep_1, give_2 = chain.contract_apart(tiles_c, weights, 2, 2)
+    tiles_d = ordered([same(SUM_HOME[2]), keep[2], give[3], keep[3], *[same(block) for block in OWN]])
+    far_0 = move(add((home_0, 0), (home_0_in, 0)), far(SUM_HOME[0][1], None))
+    home_1 = chain.hand_on(home_1)
+    home_1_in = move(home_1, inward)
+    last_away = chain.hand_on(last_away)
+    last_home = chain.hand_on(last_home)
+
+    round_1 = move(add((keep_1, 0), (got_1, 0)), near + far(None, SUM_AWAY[1][1]))
+    got_2 = move(chain.hand_on(give_2), swap)
+    home_2, keep_2 = chain.contract_apart(tiles_d, weights, 0, 2)
+    round_0 = chain.hand_on(round_0)
+    far_0 = chain.hand_on(far_0)
+    far_1 = move(add((home_1, 0), (home_1_in, 0)), far(SUM_HOME[1][1], None))
+    home_2 = chain.hand_on(home_2)
+    home_2_in = move(home_2, inward)
+    give_3, keep_3 = chain.contract_apart(tiles_d, weights, 2, 2)
+
+    round_2 = move(add((keep_2, 0), (got_2, 0)), near + far(None, SUM_AWAY[2][1]))
+    got_3 = move(chain.hand_on(give_3), swap)
+    own_012 = contract(tiles_d, 4, 3)
+    own_3 = contract(tiles_d, 7)
+    round_1 = chain.hand_on(round_1)
+    far_1 = chain.hand_on(far_1)
+    far_2 = move(add((home_2, 0), (home_2_in, 0)), far(SUM_HOME[2][1], None))
+    own_012 = chain.hand_on(own_012)
+    own_012_in = move(own_012, inward)
+    out = place(None, NEAR[0], SUM_AWAY[0], [(round_0, 0)], [(round_0, 0)])
+    out = place(out, NEAR[1], SUM_AWAY[1], [(round_1, 0)], [(round_1, 0)])
+
+    round_3 = move(add((keep_3, 0), (got_3, 0)), near + far(None, SUM_AWAY[3][1]))
+    own_3 = chain.hand_on(own_3)
+    own_3_in = move(own_3, inward)
+    out = place(out, NEAR[2], SUM_AWAY[2], [(round_2, 0)], [(round_2, 0)])
+    far_2 = chain.hand_on(far_2)
+    out = place(out, OWN[0], SUM_LAST, [(own_012, 0), (own_012_in, 0)], [(last_away, 0), (last_home, 0)])
+    out = place(out, OWN[1], SUM_HOME[0], [(own_012, 1), (own_012_in, 1)], [(far_0, 0)])
+    out = place(out, OWN[2], SUM_HOME[1], [(own_012, 2), (own_012_in, 2)], [(far_1, 0)])
+    out = place(out, NEAR[3], SUM_AWAY[3], [(round_3, 0)], [(round_3, 0)])
+    out = place(out, OWN[3], SUM_HOME[2], [(own_3, 0), (own_3_in, 0)], [(far_2, 0)])
+    return out
 
 
 def regroup_rows(amps, owner_map, tile_size):
@@ -58,4 +482,6 @@
         P(),
     )
     out_specs = P(("group", "narrow"), "wide", "sub")
-    return jax.shard_map(shards, mesh=mesh, in_specs=in_specs, out_specs=out_specs, check_vma=False)
+    planes = (mesh.shape["wide"], mesh.shape["narrow"], mesh.shape["sub"]) == (4, 2, 2)
+    body = plane_shards if planes else shards
+    return jax.shard_map(body, mesh=mesh, in_specs=in_specs, out_specs=out_specs, check_vma=False)

time: 771 us -> 317 us (0.41)
  blocking collectives: 366 us -> 0 us
  Pallas kernels: 0 us -> 143 us
  waiting for transfers between devices: 225 us -> 101 us
  local copies, waits for them, and re-layouts: 95.7 us -> 0 us
  starting transfers between devices: 0.22 us -> 68.2 us
  matrix products: 43.4 us -> 0 us
  other arithmetic: 24.6 us -> 0.67 us
  between operations: 13.4 us -> 0.15 us
    all_to_all x1 -> x0, blocking collectives: 366 us -> none  [regroup_rows(): lax.all_to_all(ordered, 'wide', split_axis=1, concat_axis=0, tiled=True)]
    reduce_scatter x1 -> x0, waiting for transfers between devices: 190 us -> none  [shards(): lax.psum_scatter(rounded, 'narrow', scatter_dimension=0, tiled=True)]
    pallas_call x0 -> x41, Pallas kernels: none -> 143 us  [call(): pl.pallas_call(body, out_shape=out_shape, grid_spec=pltpu.PrefetchScalarG...]
    ppermute x0 -> x22, waiting for transfers between devices: none -> 101 us  [the longest x18 101 us: move(): return lax.ppermute(x, both, pairs)]
    ppermute x0 -> x22, starting transfers between devices: none -> 68.2 us  [the longest x18 67.7 us: move(): return lax.ppermute(x, both, pairs)]
    dot_general x1 -> x0, matrix products: 43.4 us -> none  [shards(): jnp.einsum('ikac,kcb->iab', blocks, masked_w, preferred_element_type=jnp....]
    select_n x1 -> x0, local copies, waits for them, and re-layouts: 38 us -> none  [regroup_rows(): jnp.take(amps.reshape(pair_count, virt_count // tile_size, tile_size, c_c...]
    all_gather x1 -> x0, waiting for transfers between devices: 34.9 us -> none  [join_halves(): return lax.all_gather(amps, 'sub', axis=2, tiled=True)]
  transfers between devices with their start and end apart: 2 -> 22, of which waited for: 2 -> 6; matrix products, arithmetic and copies ran while one was open for 2% -> 0% of each run, Pallas kernels for 0% -> 44%
where the time goes in v3:
time: 317 us; the launch traced here: 313 us
  Pallas kernels  143 us (45%)
  waiting for transfers between devices  101 us (32%)
  starting transfers between devices  68.2 us (22%)
    pallas_call x41, Pallas kernels, call(): pl.pallas_call(body, out_shape=out_shape, grid_spec=pltpu.PrefetchScalarG...  143 us
    ppermute x18, waiting for transfers between devices, move(): return lax.ppermute(x, both, pairs)  101 us
    ppermute x18, starting transfers between devices, move(): return lax.ppermute(x, both, pairs)  67.7 us
  transfers between devices with their start and end apart: 22, of which 6 were waited for; matrix products, arithmetic and copies ran while one was open for 0% of the time, Pallas kernels for 44%

profile of v3, /device:TPU:8, one launch (start us, length us, event | category | flops | bytes accessed | tf_op | source)
XLA Modules:
  0.0 313.1 jit_solution(13359409897552834114)
XLA Ops:
  0.7 3.8 %order_tiles.4.refs_11_.refs_3_ = bf16[2,512,1024]{2,1,0:T(8,128)(2,1)} custom-call(s32[3]{0:T(128)} %pad_add_fusion.refs_0_, s32[32]{0:T(128)} %refs_1_.9, s32[8,8,32]{2,1,0:T(8,128)} %bitcast.4, bf16[8,2048,512]{2,1,0:T(8,128)(2,1)} %refs_10_.7, bf16[8,2048,512]{2,1,0:T(8,128)(2,1)} %refs_10_.7, bf16[8,2048,512]{2,1,0:T(8,128)(2,1)} %refs_10_.7, ...), custom_call_target="tpu_custom_call" | custom-call | flops 999999995904 | bytes 1000000000 | tf_op jit(solution)/shard_map/order_tiles/pallas_call | solution.py:55
  4.4 3.8 %order_tiles.5.refs_11_.refs_0_ = bf16[2,512,1024]{2,1,0:T(8,128)(2,1)} custom-call(s32[3]{0:T(128)} %pad_add_fusion.refs_0_, s32[32]{0:T(128)} %refs_1_.9, s32[8,8,32]{2,1,0:T(8,128)} %bitcast.5, bf16[8,2048,512]{2,1,0:T(8,128)(2,1)} %refs_10_.7, bf16[8,2048,512]{2,1,0:T(8,128)(2,1)} %refs_10_.7, bf16[8,2048,512]{2,1,0:T(8,128)(2,1)} %refs_10_.7, ...), custom_call_target="tpu_custom_call" | custom-call | flops 999999995904 | bytes 1000000000 | tf_op jit(solution)/shard_map/order_tiles/pallas_call | solution.py:55
  8.7 6.1 %order_tiles.6.refs_5_.refs_0_ = bf16[4,512,1024]{2,1,0:T(8,128)(2,1)} custom-call(s32[3]{0:T(128)} %pad_add_fusion.refs_0_, s32[32]{0:T(128)} %refs_1_.9, s32[8,8,32]{2,1,0:T(8,128)} %bitcast.6, bf16[8,2048,512]{2,1,0:T(8,128)(2,1)} %refs_10_.7, bf16[8,2048,512]{2,1,0:T(8,128)(2,1)} %refs_10_.7, bf16[8,2048,512]{2,1,0:T(8,128)(2,1)} %refs_10_.7, ...), custom_call_target="tpu_custom_call" | custom-call | flops 999999995904 | bytes 1000000000 | tf_op jit(solution)/shard_map/order_tiles/pallas_call | solution.py:55
  14.8 11.8 %contract_first.1 = (bf16[1,512,1024]{2,1,0:T(8,128)(2,1)}, bf16[1,512,1024]{2,1,0:T(8,128)(2,1)}, bf16[2,1024,1024]{2,1,0:T(8,128)(2,1)}) custom-call(s32[3]{0:T(128)} %pad_add_fusion.refs_0_, s32[2,16,16]{2,1,0:T(8,128)} %refs_1_.8, bf16[2,1024,1024]{2,1,0:T(8,128)(2,1)} %refs_2_.1, bf16[2,512,1024]{2,1,0:T(8,128)(2,1)} %order_tiles.4.refs_11_.refs_3_, ...), custom_call_target="tpu_custom_call" | custom-call | flops 999999995904 | bytes 1000000000 | tf_op jit(solution)/shard_map/contract_first/pallas_call | solution.py:55
  28.3 6.2 %collective-permute-start.6 = (bf16[1,512,1024]{2,1,0:T(8,128)(2,1)}, bf16[1,512,1024]{2,1,0:T(8,128)(2,1)}, u32[]{:S(2)}, u32[]{:S(2)}) collective-permute-start(bf16[1,512,1024]{2,1,0:T(8,128)(2,1)} %get-tuple-element.25), channel_id=1, source_target_pairs={{0,12},{4,8},{10,6},{14,2},{1,13},{5,9},{11,7},{15,3},{16,28},{20,... | collective-permute-start | bytes 3145736 | tf_op jit(solution)/shard_map/ppermute | solution.py:338
  34.4 8.9 %contract_apart.5 = (bf16[1,512,1024]{2,1,0:T(8,128)(2,1)}, bf16[1,512,1024]{2,1,0:T(8,128)(2,1)}) custom-call(bf16[2,512,1024]{2,1,0:T(8,128)(2,1)} %order_tiles.5.refs_11_.refs_0_, bf16[2,512,1024]{2,1,0:T(8,128)(2,1)} %collective-permute-done.2.refs_1_, bf16[2,1024,1024]{2,1,0:T(8,128)(2,1)} %get-tuple-element.18.refs_2_.refs_3_, ...), custom_call_target="tpu_custom_call" | custom-call | flops 999999995904 | bytes 1000000000 | tf_op jit(solution)/shard_map/contract_apart/pallas_call | solution.py:55
  44.6 8.9 %contract_apart.6 = (bf16[1,512,1024]{2,1,0:T(8,128)(2,1)}, bf16[1,512,1024]{2,1,0:T(8,128)(2,1)}) custom-call(bf16[4,512,1024]{2,1,0:T(8,128)(2,1)} %order_tiles.6.refs_5_.refs_0_, bf16[4,512,1024]{2,1,0:T(8,128)(2,1)} %collective-permute-done.refs_1_, bf16[2,1024,1024]{2,1,0:T(8,128)(2,1)} %get-tuple-element.18.refs_2_.refs_3_, ...), custom_call_target="tpu_custom_call" | custom-call | flops 999999995904 | bytes 1000000000 | tf_op jit(solution)/shard_map/contract_apart/pallas_call | solution.py:55
  53.5 25.6 %collective-permute-done.3.refs_1_ = bf16[1,512,1024]{2,1,0:T(8,128)(2,1)} collective-permute-done((bf16[1,512,1024]{2,1,0:T(8,128)(2,1)}, bf16[1,512,1024]{2,1,0:T(8,128)(2,1)}, u32[]{:S(2)}, u32[]{:S(2)}) %collective-permute-start.3) | collective-permute-done | bytes 1048608 | tf_op jit(solution)/shard_map/ppermute | solution.py:338
  84.4 8.9 %contract_apart.7 = (bf16[1,512,1024]{2,1,0:T(8,128)(2,1)}, bf16[1,512,1024]{2,1,0:T(8,128)(2,1)}) custom-call(bf16[4,512,1024]{2,1,0:T(8,128)(2,1)} %order_tiles.6.refs_5_.refs_0_, bf16[4,512,1024]{2,1,0:T(8,128)(2,1)} %collective-permute-done.refs_1_, bf16[2,1024,1024]{2,1,0:T(8,128)(2,1)} %get-tuple-element.18.refs_2_.refs_3_, ...), custom_call_target="tpu_custom_call" | custom-call | flops 999999995904 | bytes 1000000000 | tf_op jit(solution)/shard_map/contract_apart/pallas_call | solution.py:55
  93.3 10.8 %order_tiles.7.refs_2_.refs_0_.refs_1_ = bf16[8,512,1024]{2,1,0:T(8,128)(2,1)} custom-call(s32[3]{0:T(128)} %pad_add_fusion.refs_0_, s32[32]{0:T(128)} %refs_1_.9, s32[8,8,32]{2,1,0:T(8,128)} %bitcast.7, bf16[8,2048,512]{2,1,0:T(8,128)(2,1)} %refs_10_.7, bf16[8,2048,512]{2,1,0:T(8,128)(2,1)} %refs_10_.7, bf16[8,2048,512]{2,1,0:T(8,128)(2,1)} %refs_10_.7, ...), custom_call_target="tpu_custom_call" | custom-call | flops 999999995904 | bytes 1000000000 | tf_op jit(solution)/shard_map/order_tiles/pallas_call | solution.py:55
  106.7 4.3 %collective-permute-start.10 = (bf16[1,512,1024]{2,1,0:T(8,128)(2,1)}, bf16[1,512,1024]{2,1,0:T(8,128)(2,1)}, u32[]{:S(2)}, u32[]{:S(2)}) collective-permute-start(bf16[1,512,1024]{2,1,0:T(8,128)(2,1)} %add.13.refs_1_), channel_id=1, source_target_pairs={{0,8},{4,12},{10,2},{14,6},{1,9},{5,13},{11,3},{15,7},{16,24},{20,... | collective-permute-start | bytes 3145736 | tf_op jit(solution)/shard_map/ppermute | solution.py:338
  114.8 19.9 %collective-permute-start.14 = (bf16[1,512,1024]{2,1,0:T(8,128)(2,1)}, bf16[1,512,1024]{2,1,0:T(8,128)(2,1)}, u32[]{:S(2)}, u32[]{:S(2)}) collective-permute-start(bf16[1,512,1024]{2,1,0:T(8,128)(2,1)} %add.14.refs_1_), channel_id=1, source_target_pairs={{0,4},{4,0},{10,14},{14,10},{2,8},{6,12},{8,2},{12,6},{1,5},{5,1},... | collective-permute-start | bytes 3145736 | tf_op jit(solution)/shard_map/ppermute | solution.py:338
  137.3 8.9 %contract_apart.8 = (bf16[1,512,1024]{2,1,0:T(8,128)(2,1)}, bf16[1,512,1024]{2,1,0:T(8,128)(2,1)}) custom-call(bf16[8,512,1024]{2,1,0:T(8,128)(2,1)} %order_tiles.7.refs_2_.refs_0_.refs_1_, bf16[8,512,1024]{2,1,0:T(8,128)(2,1)} %collective-permute-done.4.refs_1_.refs_2_, bf16[2,1024,1024]{2,1,0:T(8,128)(2,1)} %get-tuple-element.18.refs_2_.refs_3_, ...), custom_call_target="tpu_custom_call" | custom-call | flops 999999995904 | bytes 1000000000 | tf_op jit(solution)/shard_map/contract_apart/pallas_call | solution.py:55
  146.2 9.6 %collective-permute-done.10.refs_0_ = bf16[1,512,1024]{2,1,0:T(8,128)(2,1)} collective-permute-done((bf16[1,512,1024]{2,1,0:T(8,128)(2,1)}, bf16[1,512,1024]{2,1,0:T(8,128)(2,1)}, u32[]{:S(2)}, u32[]{:S(2)}) %collective-permute-start.10) | collective-permute-done | bytes 1048608 | tf_op jit(solution)/shard_map/ppermute | solution.py:338
  162.2 9.0 %contract_apart.9 = (bf16[1,512,1024]{2,1,0:T(8,128)(2,1)}, bf16[1,512,1024]{2,1,0:T(8,128)(2,1)}) custom-call(bf16[8,512,1024]{2,1,0:T(8,128)(2,1)} %order_tiles.7.refs_2_.refs_0_.refs_1_, bf16[8,512,1024]{2,1,0:T(8,128)(2,1)} %collective-permute-done.4.refs_1_.refs_2_, bf16[2,1024,1024]{2,1,0:T(8,128)(2,1)} %get-tuple-element.18.refs_2_.refs_3_, ...), custom_call_target="tpu_custom_call" | custom-call | flops 999999995904 | bytes 1000000000 | tf_op jit(solution)/shard_map/contract_apart/pallas_call | solution.py:55
  171.1 8.7 %collective-permute-done.12.refs_1_ = bf16[1,512,1024]{2,1,0:T(8,128)(2,1)} collective-permute-done((bf16[1,512,1024]{2,1,0:T(8,128)(2,1)}, bf16[1,512,1024]{2,1,0:T(8,128)(2,1)}, u32[]{:S(2)}, u32[]{:S(2)}) %collective-permute-start.12) | collective-permute-done | bytes 1048608 | tf_op jit(solution)/shard_map/ppermute | solution.py:338
  188.2 11.9 %contract.2.refs_4_.refs_0_ = bf16[3,512,1024]{2,1,0:T(8,128)(2,1)} custom-call(s32[3]{0:T(128)} %pad_add_fusion.refs_0_, bf16[8,512,1024]{2,1,0:T(8,128)(2,1)} %order_tiles.7.refs_2_.refs_0_.refs_1_, bf16[8,512,1024]{2,1,0:T(8,128)(2,1)} %collective-permute-done.4.refs_1_.refs_2_, bf16[2,1024,1024]{2,1,0:T(8,128)(2,1)} %get-tuple-element.18.refs_2_.refs_3_, ...), custom_call_target="tpu_custom_call" | custom-call | flops 999999995904 | bytes 1000000000 | tf_op jit(solution)/shard_map/contract/pallas_call | solution.py:55
  200.1 6.5 %contract.3.refs_1_.refs_0_ = bf16[1,512,1024]{2,1,0:T(8,128)(2,1)} custom-call(s32[3]{0:T(128)} %pad_add_fusion.refs_0_, bf16[8,512,1024]{2,1,0:T(8,128)(2,1)} %order_tiles.7.refs_2_.refs_0_.refs_1_, bf16[8,512,1024]{2,1,0:T(8,128)(2,1)} %collective-permute-done.4.refs_1_.refs_2_, bf16[2,1024,1024]{2,1,0:T(8,128)(2,1)} %get-tuple-element.18.refs_2_.refs_3_, ...), custom_call_target="tpu_custom_call" | custom-call | flops 999999995904 | bytes 1000000000 | tf_op jit(solution)/shard_map/contract/pallas_call | solution.py:55
  209.1 4.0 %collective-permute-start.18 = (bf16[1,512,1024]{2,1,0:T(8,128)(2,1)}, bf16[1,512,1024]{2,1,0:T(8,128)(2,1)}, u32[]{:S(2)}, u32[]{:S(2)}) collective-permute-start(bf16[1,512,1024]{2,1,0:T(8,128)(2,1)} %add.17.refs_1_), channel_id=1, source_target_pairs={{0,8},{4,12},{10,2},{14,6},{1,9},{5,13},{11,3},{15,7},{16,24},{20,... | collective-permute-start | bytes 3145736 | tf_op jit(solution)/shard_map/ppermute | solution.py:338
  223.3 11.2 %collective-permute-start.20 = (bf16[1,512,1024]{2,1,0:T(8,128)(2,1)}, bf16[1,512,1024]{2,1,0:T(8,128)(2,1)}, u32[]{:S(2)}, u32[]{:S(2)}) collective-permute-start(bf16[1,512,1024]{2,1,0:T(8,128)(2,1)} %add.18.refs_1_), channel_id=1, source_target_pairs={{0,4},{4,0},{10,14},{14,10},{2,8},{6,12},{8,2},{12,6},{1,5},{5,1},... | collective-permute-start | bytes 3145736 | tf_op jit(solution)/shard_map/ppermute | solution.py:338
  239.1 17.3 %collective-permute-done.18.refs_0_ = bf16[1,512,1024]{2,1,0:T(8,128)(2,1)} collective-permute-done((bf16[1,512,1024]{2,1,0:T(8,128)(2,1)}, bf16[1,512,1024]{2,1,0:T(8,128)(2,1)}, u32[]{:S(2)}, u32[]{:S(2)}) %collective-permute-start.18) | collective-permute-done | bytes 1048608 | tf_op jit(solution)/shard_map/ppermute | solution.py:338
  256.4 33.2 %collective-permute-done.21.refs_2_ = bf16[3,512,1024]{2,1,0:T(8,128)(2,1)} collective-permute-done((bf16[3,512,1024]{2,1,0:T(8,128)(2,1)}, bf16[3,512,1024]{2,1,0:T(8,128)(2,1)}, u32[]{:S(2)}, u32[]{:S(2)}) %collective-permute-start.21) | collective-permute-done | bytes 3145760 | tf_op jit(solution)/shard_map/ppermute | solution.py:338
  289.6 3.8 %place.11.refs_4_ = bf16[8,512,1024]{2,1,0:T(8,128)(2,1)} custom-call(s32[3]{0:T(128)} %pad_add_fusion.refs_0_, bf16[3,512,1024]{2,1,0:T(8,128)(2,1)} %hand_on.25.refs_3_.refs_1_, bf16[3,512,1024]{2,1,0:T(8,128)(2,1)} %collective-permute-done.21.refs_2_, bf16[1,512,1024]{2,1,0:T(8,128)(2,1)} %hand_on.16.refs_1_.refs_3_, ...), custom_call_target="tpu_custom_call", output_to_operand_aliasing={{}: (5, {})} | custom-call | flops 999999995904 | bytes 1000000000 | tf_op jit(solution)/shard_map/place/pallas_call | solution.py:55
  303.4 6.2 %collective-permute-done.17.refs_2_ = bf16[1,512,1024]{2,1,0:T(8,128)(2,1)} collective-permute-done((bf16[1,512,1024]{2,1,0:T(8,128)(2,1)}, bf16[1,512,1024]{2,1,0:T(8,128)(2,1)}, u32[]{:S(2)}, u32[]{:S(2)}) %collective-permute-start.17) | collective-permute-done | bytes 1048608 | tf_op jit(solution)/shard_map/ppermute | solution.py:338
  (62 shorter events, 63.7 us)
Async XLA Ops:
  4.4 10.4 %collective-permute-start.1 = (bf16[2,512,1024]{2,1,0:T(8,128)(2,1)}, bf16[2,512,1024]{2,1,0:T(8,128)(2,1)}, u32[]{:S(2)}, u32[]{:S(2)}) collective-permute-start(bf16[2,512,1024]{2,1,0:T(8,128)(2,1)} %order_tiles.4.refs_11_.refs_3_), channel_id=1, source_target_pairs={{0,1},{1,0},{2,3},{3,2},{4,5},{5,4},{6,7},{7,6},{8,9},{9,8},{10,11... | collective-permute-start | bytes 6291464 | tf_op jit(solution)/shard_map/ppermute | solution.py:357
  8.2 26.2 %collective-permute-start.2 = (bf16[2,512,1024]{2,1,0:T(8,128)(2,1)}, bf16[2,512,1024]{2,1,0:T(8,128)(2,1)}, u32[]{:S(2)}, u32[]{:S(2)}) collective-permute-start(bf16[2,512,1024]{2,1,0:T(8,128)(2,1)} %order_tiles.5.refs_11_.refs_0_), channel_id=1, source_target_pairs={{0,1},{1,0},{2,3},{3,2},{4,5},{5,4},{6,7},{7,6},{8,9},{9,8},{10,11... | collective-permute-start | bytes 6291464 | tf_op jit(solution)/shard_map/ppermute | solution.py:357
  14.8 29.8 %collective-permute-start = (bf16[4,512,1024]{2,1,0:T(8,128)(2,1)}, bf16[4,512,1024]{2,1,0:T(8,128)(2,1)}, u32[]{:S(2)}, u32[]{:S(2)}) collective-permute-start(bf16[4,512,1024]{2,1,0:T(8,128)(2,1)} %order_tiles.6.refs_5_.refs_0_), channel_id=1, source_target_pairs={{0,1},{1,0},{2,3},{3,2},{4,5},{5,4},{6,7},{7,6},{8,9},{9,8},{10,11... | collective-permute-start | bytes 12582920 | tf_op jit(solution)/shard_map/ppermute | solution.py:357
  26.6 80.0 %collective-permute-start.7 = (bf16[1,512,1024]{2,1,0:T(8,128)(2,1)}, bf16[1,512,1024]{2,1,0:T(8,128)(2,1)}, u32[]{:S(2)}, u32[]{:S(2)}) collective-permute-start(bf16[1,512,1024]{2,1,0:T(8,128)(2,1)} %get-tuple-element.25), channel_id=1, source_target_pairs={{2,12},{6,8},{8,6},{12,2},{3,13},{7,9},{9,7},{13,3},{18,28},{22,24... | collective-permute-start | bytes 3145736 | tf_op jit(solution)/shard_map/ppermute | solution.py:338
  28.3 82.8 %collective-permute-start.6 = (bf16[1,512,1024]{2,1,0:T(8,128)(2,1)}, bf16[1,512,1024]{2,1,0:T(8,128)(2,1)}, u32[]{:S(2)}, u32[]{:S(2)}) collective-permute-start(bf16[1,512,1024]{2,1,0:T(8,128)(2,1)} %get-tuple-element.25), channel_id=1, source_target_pairs={{0,12},{4,8},{10,6},{14,2},{1,13},{5,9},{11,7},{15,3},{16,28},{20,... | collective-permute-start | bytes 3145736 | tf_op jit(solution)/shard_map/ppermute | solution.py:338
  34.4 44.7 %collective-permute-start.3 = (bf16[1,512,1024]{2,1,0:T(8,128)(2,1)}, bf16[1,512,1024]{2,1,0:T(8,128)(2,1)}, u32[]{:S(2)}, u32[]{:S(2)}) collective-permute-start(bf16[1,512,1024]{2,1,0:T(8,128)(2,1)} %get-tuple-element.19.refs_3_), channel_id=1, source_target_pairs={{2,0},{6,4},{8,10},{12,14},{0,2},{4,6},{10,8},{14,12},{3,1},{7,5},... | collective-permute-start | bytes 3145736 | tf_op jit(solution)/shard_map/ppermute | solution.py:338
  43.3 60.8 %collective-permute-start.8 = (bf16[1,512,1024]{2,1,0:T(8,128)(2,1)}, bf16[1,512,1024]{2,1,0:T(8,128)(2,1)}, u32[]{:S(2)}, u32[]{:S(2)}) collective-permute-start(bf16[1,512,1024]{2,1,0:T(8,128)(2,1)} %get-tuple-element.20.refs_3_.refs_0_), channel_id=1, source_target_pairs={{2,0},{6,4},{8,10},{12,14},{3,1},{7,5},{9,11},{13,15},{18,16},{22,... | collective-permute-start | bytes 3145736 | tf_op jit(solution)/shard_map/ppermute | solution.py:338
  81.6 64.7 %collective-permute-start.11 = (bf16[1,512,1024]{2,1,0:T(8,128)(2,1)}, bf16[1,512,1024]{2,1,0:T(8,128)(2,1)}, u32[]{:S(2)}, u32[]{:S(2)}) collective-permute-start(bf16[1,512,1024]{2,1,0:T(8,128)(2,1)} %add.12.refs_1_), channel_id=1, source_target_pairs={{0,4},{4,0},{10,14},{14,10},{2,12},{6,8},{8,6},{12,2},{1,5},{5,1},... | collective-permute-start | bytes 3145736 | tf_op jit(solution)/shard_map/ppermute | solution.py:338
  81.6 30.7 %collective-permute-start.5 = (bf16[1,512,1024]{2,1,0:T(8,128)(2,1)}, bf16[1,512,1024]{2,1,0:T(8,128)(2,1)}, u32[]{:S(2)}, u32[]{:S(2)}) collective-permute-start(bf16[1,512,1024]{2,1,0:T(8,128)(2,1)} %hand_on.14.refs_3_), channel_id=1, source_target_pairs={{2,0},{6,4},{8,10},{12,14},{0,2},{4,6},{10,8},{14,12},{3,1},{7,5},... | collective-permute-start | bytes 3145736 | tf_op jit(solution)/shard_map/ppermute | solution.py:338
  104.1 30.6 %collective-permute-start.4 = (bf16[8,512,1024]{2,1,0:T(8,128)(2,1)}, bf16[8,512,1024]{2,1,0:T(8,128)(2,1)}, u32[]{:S(2)}, u32[]{:S(2)}) collective-permute-start(bf16[8,512,1024]{2,1,0:T(8,128)(2,1)} %order_tiles.7.refs_2_.refs_0_.refs_1_), channel_id=1, source_target_pairs={{0,1},{1,0},{2,3},{3,2},{4,5},{5,4},{6,7},{7,6},{8,9},{9,8},{10,11... | collective-permute-start | bytes 25165832 | tf_op jit(solution)/shard_map/ppermute | solution.py:357
  106.7 49.2 %collective-permute-start.10 = (bf16[1,512,1024]{2,1,0:T(8,128)(2,1)}, bf16[1,512,1024]{2,1,0:T(8,128)(2,1)}, u32[]{:S(2)}, u32[]{:S(2)}) collective-permute-start(bf16[1,512,1024]{2,1,0:T(8,128)(2,1)} %add.13.refs_1_), channel_id=1, source_target_pairs={{0,8},{4,12},{10,2},{14,6},{1,9},{5,13},{11,3},{15,7},{16,24},{20,... | collective-permute-start | bytes 3145736 | tf_op jit(solution)/shard_map/ppermute | solution.py:338
  111.0 44.8 %collective-permute-start.9 = (bf16[1,512,1024]{2,1,0:T(8,128)(2,1)}, bf16[1,512,1024]{2,1,0:T(8,128)(2,1)}, u32[]{:S(2)}, u32[]{:S(2)}) collective-permute-start(bf16[1,512,1024]{2,1,0:T(8,128)(2,1)} %hand_on.15.refs_1_.refs_0_), channel_id=1, source_target_pairs={{2,0},{6,4},{8,10},{12,14},{3,1},{7,5},{9,11},{13,15},{18,16},{22,... | collective-permute-start | bytes 3145736 | tf_op jit(solution)/shard_map/ppermute | solution.py:338
  114.8 91.9 %collective-permute-start.14 = (bf16[1,512,1024]{2,1,0:T(8,128)(2,1)}, bf16[1,512,1024]{2,1,0:T(8,128)(2,1)}, u32[]{:S(2)}, u32[]{:S(2)}) collective-permute-start(bf16[1,512,1024]{2,1,0:T(8,128)(2,1)} %add.14.refs_1_), channel_id=1, source_target_pairs={{0,4},{4,0},{10,14},{14,10},{2,8},{6,12},{8,2},{12,6},{1,5},{5,1},... | collective-permute-start | bytes 3145736 | tf_op jit(solution)/shard_map/ppermute | solution.py:338
  134.7 45.1 %collective-permute-start.12 = (bf16[1,512,1024]{2,1,0:T(8,128)(2,1)}, bf16[1,512,1024]{2,1,0:T(8,128)(2,1)}, u32[]{:S(2)}, u32[]{:S(2)}) collective-permute-start(bf16[1,512,1024]{2,1,0:T(8,128)(2,1)} %hand_on.18.refs_3_), channel_id=1, source_target_pairs={{2,0},{6,4},{8,10},{12,14},{0,2},{4,6},{10,8},{14,12},{3,1},{7,5},... | collective-permute-start | bytes 3145736 | tf_op jit(solution)/shard_map/ppermute | solution.py:338
  158.4 48.3 %collective-permute-start.16 = (bf16[1,512,1024]{2,1,0:T(8,128)(2,1)}, bf16[1,512,1024]{2,1,0:T(8,128)(2,1)}, u32[]{:S(2)}, u32[]{:S(2)}) collective-permute-start(bf16[1,512,1024]{2,1,0:T(8,128)(2,1)} %add.15.refs_1_), channel_id=1, source_target_pairs={{0,12},{4,8},{10,6},{14,2},{1,13},{5,9},{11,7},{15,3},{16,28},{20,... | collective-permute-start | bytes 3145736 | tf_op jit(solution)/shard_map/ppermute | solution.py:338
  160.7 45.9 %collective-permute-start.15 = (bf16[1,512,1024]{2,1,0:T(8,128)(2,1)}, bf16[1,512,1024]{2,1,0:T(8,128)(2,1)}, u32[]{:S(2)}, u32[]{:S(2)}) collective-permute-start(bf16[1,512,1024]{2,1,0:T(8,128)(2,1)} %hand_on.21.refs_3_.refs_0_), channel_id=1, source_target_pairs={{2,0},{6,4},{8,10},{12,14},{3,1},{7,5},{9,11},{13,15},{18,16},{22,... | collective-permute-start | bytes 3145736 | tf_op jit(solution)/shard_map/ppermute | solution.py:338
  182.3 53.6 %collective-permute-start.19 = (bf16[1,512,1024]{2,1,0:T(8,128)(2,1)}, bf16[1,512,1024]{2,1,0:T(8,128)(2,1)}, u32[]{:S(2)}, u32[]{:S(2)}) collective-permute-start(bf16[1,512,1024]{2,1,0:T(8,128)(2,1)} %add.16.refs_1_), channel_id=1, source_target_pairs={{0,4},{4,0},{10,14},{14,10},{2,12},{6,8},{8,6},{12,2},{1,5},{5,1},... | collective-permute-start | bytes 3145736 | tf_op jit(solution)/shard_map/ppermute | solution.py:338
  185.1 35.8 %collective-permute-start.13 = (bf16[1,512,1024]{2,1,0:T(8,128)(2,1)}, bf16[1,512,1024]{2,1,0:T(8,128)(2,1)}, u32[]{:S(2)}, u32[]{:S(2)}) collective-permute-start(bf16[1,512,1024]{2,1,0:T(8,128)(2,1)} %hand_on.22.refs_4_), channel_id=1, source_target_pairs={{2,0},{6,4},{8,10},{12,14},{0,2},{4,6},{10,8},{14,12},{3,1},{7,5},... | collective-permute-start | bytes 3145736 | tf_op jit(solution)/shard_map/ppermute | solution.py:338
  209.1 47.3 %collective-permute-start.18 = (bf16[1,512,1024]{2,1,0:T(8,128)(2,1)}, bf16[1,512,1024]{2,1,0:T(8,128)(2,1)}, u32[]{:S(2)}, u32[]{:S(2)}) collective-permute-start(bf16[1,512,1024]{2,1,0:T(8,128)(2,1)} %add.17.refs_1_), channel_id=1, source_target_pairs={{0,8},{4,12},{10,2},{14,6},{1,9},{5,13},{11,3},{15,7},{16,24},{20,... | collective-permute-start | bytes 3145736 | tf_op jit(solution)/shard_map/ppermute | solution.py:338
  216.3 73.2 %collective-permute-start.21 = (bf16[3,512,1024]{2,1,0:T(8,128)(2,1)}, bf16[3,512,1024]{2,1,0:T(8,128)(2,1)}, u32[]{:S(2)}, u32[]{:S(2)}) collective-permute-start(bf16[3,512,1024]{2,1,0:T(8,128)(2,1)} %hand_on.25.refs_3_.refs_1_), channel_id=1, source_target_pairs={{2,0},{6,4},{8,10},{12,14},{3,1},{7,5},{9,11},{13,15},{18,16},{22,... | collective-permute-start | bytes 9437192 | tf_op jit(solution)/shard_map/ppermute | solution.py:338
  223.3 76.9 %collective-permute-start.20 = (bf16[1,512,1024]{2,1,0:T(8,128)(2,1)}, bf16[1,512,1024]{2,1,0:T(8,128)(2,1)}, u32[]{:S(2)}, u32[]{:S(2)}) collective-permute-start(bf16[1,512,1024]{2,1,0:T(8,128)(2,1)} %add.18.refs_1_), channel_id=1, source_target_pairs={{0,4},{4,0},{10,14},{14,10},{2,8},{6,12},{8,2},{12,6},{1,5},{5,1},... | collective-permute-start | bytes 3145736 | tf_op jit(solution)/shard_map/ppermute | solution.py:338
  234.5 75.1 %collective-permute-start.17 = (bf16[1,512,1024]{2,1,0:T(8,128)(2,1)}, bf16[1,512,1024]{2,1,0:T(8,128)(2,1)}, u32[]{:S(2)}, u32[]{:S(2)}) collective-permute-start(bf16[1,512,1024]{2,1,0:T(8,128)(2,1)} %hand_on.26.refs_4_.refs_1_), channel_id=1, source_target_pairs={{2,0},{6,4},{8,10},{12,14},{3,1},{7,5},{9,11},{13,15},{18,16},{22,... | collective-permute-start | bytes 3145736 | tf_op jit(solution)/shard_map/ppermute | solution.py:338

commit v4 on v3

--- a/solution.py
+++ b/solution.py
@@ -9,7 +9,7 @@
 F32 = jnp.float32
 MIB = 2**20
 
-SUM_HOME = [(0, 2), (1, 3), (2, 2)]
+SUM_HOME = [(0, 2), (2, 2), (1, 3)]
 SUM_AWAY = [(0, 3), (1, 2), (2, 3), (3, 2)]
 SUM_LAST = (3, 3)
 NEAR = [(0, 1), (1, 1), (2, 1), (3, 1)]
@@ -117,65 +117,31 @@
             scratch=[pltpu.VMEM((k_count, t_mask.shape[2], c_here), F32)],
         )
 
-    def contract_first(self, role, tiles, integrals, w_mask, tile_size):
-        mine, theirs = tiles
+    def mask_integrals(self, role, integrals, w_mask, tile_size):
         k_count, c_rows, b_cols = integrals.shape
-        count, rows, _ = mine.shape
         half = c_rows // 2
         half_tiles = half // tile_size
 
-        def kernel(role, mask_ref, in_ref, mine_ref, theirs_ref, *refs):
-            *out_refs, weights_ref, wide_ref, total_ref = refs
-            h, k = pl.program_id(0), pl.program_id(1)
+        def kernel(role, mask_ref, in_ref, out_ref, wide_ref):
             wide_ref[...] = widen(mask_ref[0], tile_size, 1)
             for j in range(half_tiles):
                 at = pl.ds(j * tile_size, tile_size)
-                scale = wide_ref[pl.ds((h ^ role[2]) * half_tiles + j, 1), :].astype(BF16)
-                weights_ref[0, at, :] = in_ref[0, at, :] * scale
-
-            def term(ref, block):
-                return jnp.dot(ref[block], weights_ref[0], preferred_element_type=F32)
-
-            for block in range(count):
-
-                @pl.when((h == 0) & (k == 0))
-                def _(block=block):
-                    total_ref[block] = term(mine_ref, block)
-
-                @pl.when((h == 0) & (k > 0))
-                def _(block=block):
-                    total_ref[block] += term(mine_ref, block)
-
-                @pl.when((h == 1) & (k < k_count - 1))
-                def _(block=block):
-                    total_ref[block] += term(theirs_ref, block)
-
-                @pl.when((h == 1) & (k == k_count - 1))
-                def _(block=block):
-                    out_refs[block][0] = (total_ref[block] + term(theirs_ref, block)).astype(BF16)
-
-        block = pl.BlockSpec((count, rows, half), lambda h, k, role: (0, 0, k))
-        return self.call(
-            kernel,
-            "contract_first",
-            (w_mask, integrals, mine, theirs),
-            [
-                *[jax.ShapeDtypeStruct((1, rows, b_cols), BF16)] * count,
-                jax.ShapeDtypeStruct((2, k_count * half, b_cols), BF16),
-            ],
+                scale = wide_ref[pl.ds((pl.program_id(0) ^ role[2]) * half_tiles + j, 1), :].astype(BF16)
+                out_ref[0, at, :] = in_ref[0, at, :] * scale
+
+        return self.call(
+            kernel,
+            "mask_integrals",
+            (w_mask, integrals),
+            jax.ShapeDtypeStruct((2, k_count * half, b_cols), BF16),
             (2, k_count),
             [
                 pl.BlockSpec((1, *w_mask.shape[1:]), lambda h, k, role: (k, 0, 0)),
                 pl.BlockSpec((1, half, b_cols), lambda h, k, role: (k, h ^ role[2], 0)),
-                block,
-                block,
             ],
-            [
-                *[pl.BlockSpec((1, rows, b_cols), lambda h, k, role: (0, 0, 0))] * count,
-                pl.BlockSpec((1, half, b_cols), lambda h, k, role: (h, k, 0)),
-            ],
+            pl.BlockSpec((1, half, b_cols), lambda h, k, role: (h, k, 0)),
             prefetch=(role,),
-            scratch=[pltpu.VMEM((w_mask.shape[1], b_cols), F32), pltpu.VMEM((count, rows, b_cols), F32)],
+            scratch=[pltpu.VMEM((w_mask.shape[1], b_cols), F32)],
         )
 
     def contract_apart(self, tiles, weights, first, count):
@@ -352,9 +318,14 @@
     near = [(device(w, True), device(w, True) % 2 + 2 * (w ^ 1)) for w in range(4)]
     chain = Chain()
 
+    def ordered_later(blocks):
+        return chain.order_tiles(role, owner_map, amplitudes, masks, tile_size, blocks)
+
+    def exchange(tiles):
+        return tiles, lax.ppermute(tiles, "sub", [(0, 1), (1, 0)])
+
     def ordered(blocks):
-        mine = chain.order_tiles(role, owner_map, amplitudes, masks, tile_size, blocks)
-        return mine, lax.ppermute(mine, "sub", [(0, 1), (1, 0)])
+        return exchange(ordered_later(blocks))
 
     def contract(tiles, first, count=1):
         return chain.contract(role, tiles, weights, first, count)
@@ -372,50 +343,64 @@
     give = [(away, home) for home, away in zip(NEAR, SUM_AWAY)]
     keep = list(zip(NEAR, SUM_AWAY))
 
+    def to_far(at):
+        return far(SUM_HOME[at][1], None)
+
+    def round_pairs(at):
+        return near + far(None, SUM_AWAY[at][1])
+
     tiles_a = ordered([give[0], same(SUM_LAST)])
+    weights = chain.mask_integrals(role, integrals, w_mask, tile_size)
     tiles_b = ordered([same(SUM_HOME[0]), keep[0]])
-    tiles_c = ordered([give[1], same(SUM_HOME[1]), keep[1], give[2]])
-    give_0, last, weights = chain.contract_first(role, tiles_a, integrals, w_mask, tile_size)
-    got_0 = move(give_0, swap)
-    last_away = move(last, far(None, SUM_LAST[1]))
+    got_0 = move(contract(tiles_a, 0), swap)
     home_0, keep_0 = chain.contract_apart(tiles_b, weights, 0, 2)
     home_0_in = move(home_0, inward)
+    last = contract(tiles_a, 1)
+    last_away = move(last, far(None, SUM_LAST[1]))
+    last_home = move(last, far(SUM_LAST[1], None))
+    tiles_c = ordered([give[1], same(SUM_HOME[1]), keep[1], give[2]])
+
+    round_0 = move(add((keep_0, 0), (got_0, 0)), round_pairs(0))
     give_1, home_1 = chain.contract_apart(tiles_c, weights, 0, 2)
-    last_home = move(last, far(SUM_LAST[1], None))
-
-    round_0 = move(add((keep_0, 0), (got_0, 0)), near + far(None, SUM_AWAY[0][1]))
-    got_1 = move(chain.hand_on(give_1), swap)
-    keep_1, give_2 = chain.contract_apart(tiles_c, weights, 2, 2)
-    tiles_d = ordered([same(SUM_HOME[2]), keep[2], give[3], keep[3], *[same(block) for block in OWN]])
-    far_0 = move(add((home_0, 0), (home_0_in, 0)), far(SUM_HOME[0][1], None))
+    got_1 = move(give_1, swap)
+    home_0_in = chain.hand_on(home_0_in)
     home_1 = chain.hand_on(home_1)
     home_1_in = move(home_1, inward)
+    keep_1, give_2 = chain.contract_apart(tiles_c, weights, 2, 2)
+    tiles_d = ordered_later(
+        [same(SUM_HOME[2]), keep[2], give[3], keep[3], *[same(block) for block in OWN]]
+    )
     last_away = chain.hand_on(last_away)
     last_home = chain.hand_on(last_home)
-
-    round_1 = move(add((keep_1, 0), (got_1, 0)), near + far(None, SUM_AWAY[1][1]))
+    far_0 = move(add((home_0, 0), (home_0_in, 0)), to_far(0))
+    tiles_d = exchange(chain.hand_on(tiles_d))
+
+    round_0 = chain.hand_on(round_0)
+    round_1 = move(add((keep_1, 0), (got_1, 0)), round_pairs(1))
     got_2 = move(chain.hand_on(give_2), swap)
     home_2, keep_2 = chain.contract_apart(tiles_d, weights, 0, 2)
-    round_0 = chain.hand_on(round_0)
-    far_0 = chain.hand_on(far_0)
-    far_1 = move(add((home_1, 0), (home_1_in, 0)), far(SUM_HOME[1][1], None))
+    home_1_in = chain.hand_on(home_1_in)
     home_2 = chain.hand_on(home_2)
     home_2_in = move(home_2, inward)
+    far_0 = chain.hand_on(far_0)
+    far_1 = move(add((home_1, 0), (home_1_in, 0)), to_far(1))
     give_3, keep_3 = chain.contract_apart(tiles_d, weights, 2, 2)
-
-    round_2 = move(add((keep_2, 0), (got_2, 0)), near + far(None, SUM_AWAY[2][1]))
+    own_012 = contract(tiles_d, 4, 3)
+
     got_3 = move(chain.hand_on(give_3), swap)
-    own_012 = contract(tiles_d, 4, 3)
-    own_3 = contract(tiles_d, 7)
     round_1 = chain.hand_on(round_1)
-    far_1 = chain.hand_on(far_1)
-    far_2 = move(add((home_2, 0), (home_2_in, 0)), far(SUM_HOME[2][1], None))
+    round_2 = move(add((keep_2, 0), (got_2, 0)), round_pairs(2))
+    home_2_in = chain.hand_on(home_2_in)
     own_012 = chain.hand_on(own_012)
     own_012_in = move(own_012, inward)
+    own_3 = contract(tiles_d, 7)
+    far_1 = chain.hand_on(far_1)
+    far_2 = move(add((home_2, 0), (home_2_in, 0)), to_far(2))
     out = place(None, NEAR[0], SUM_AWAY[0], [(round_0, 0)], [(round_0, 0)])
     out = place(out, NEAR[1], SUM_AWAY[1], [(round_1, 0)], [(round_1, 0)])
 
-    round_3 = move(add((keep_3, 0), (got_3, 0)), near + far(None, SUM_AWAY[3][1]))
+    round_2 = chain.hand_on(round_2)
+    round_3 = move(add((keep_3, 0), (got_3, 0)), round_pairs(3))
     own_3 = chain.hand_on(own_3)
     own_3_in = move(own_3, inward)
     out = place(out, NEAR[2], SUM_AWAY[2], [(round_2, 0)], [(round_2, 0)])

time: 317 us -> 305 us (0.962)
  starting transfers between devices: 68.2 us -> 55.9 us
  Pallas kernels: 143 us -> 151 us
  waiting for transfers between devices: 101 us -> 94.8 us
    ppermute x18, starting transfers between devices: 67.7 us -> 55.4 us  [move(): return lax.ppermute(x, both, pairs)]
    pallas_call x41 -> x47, Pallas kernels: 143 us -> 151 us  [call(): pl.pallas_call(body, out_shape=out_shape, grid_spec=pltpu.PrefetchScalarG...]
    ppermute x18, waiting for transfers between devices: 101 us -> 94.8 us  [move(): return lax.ppermute(x, both, pairs)]
  transfers between devices with their start and end apart: 22 -> 22, of which waited for: 6 -> 8; matrix products, arithmetic and copies ran while one was open for 0% -> 0% of each run, Pallas kernels for 44% -> 47%
where the time goes in v4:
time: 305 us; the launch traced here: 302 us
  Pallas kernels  151 us (50%)
  waiting for transfers between devices  94.8 us (31%)
  starting transfers between devices  55.9 us (18%)
    pallas_call x47, Pallas kernels, call(): pl.pallas_call(body, out_shape=out_shape, grid_spec=pltpu.PrefetchScalarG...  151 us
    ppermute x18, waiting for transfers between devices, move(): return lax.ppermute(x, both, pairs)  94.8 us
    ppermute x18, starting transfers between devices, move(): return lax.ppermute(x, both, pairs)  55.4 us
  transfers between devices with their start and end apart: 22, of which 8 were waited for; matrix products, arithmetic and copies ran while one was open for 0% of the time, Pallas kernels for 47%

profile of v4, /device:TPU:8, one launch (start us, length us, event | category | flops | bytes accessed | tf_op | source)
XLA Modules:
  0.0 302.1 jit_solution(10512727652060215212)
XLA Ops:
  4.3 5.8 %mask_integrals.1.refs_11_.refs_3_.refs_2_ = bf16[2,1024,1024]{2,1,0:T(8,128)(2,1)} custom-call(s32[3]{0:T(128)} %pad_add_fusion.refs_0_, s32[2,16,16]{2,1,0:T(8,128)} %refs_1_.6, bf16[2,1024,1024]{2,1,0:T(8,128)(2,1)} %refs_2_.1, bf16[2,512,1024]{2,1,0:T(8,128)(2,1)} %order_tiles.4.refs_3_.refs_1_), custom_call_target="tpu_custom_call" | custom-call | flops 999999995904 | bytes 1000000000 | tf_op jit(solution)/shard_map/mask_integrals/pallas_call | solution.py:55
  14.3 6.5 %contract.4.refs_3_ = bf16[1,512,1024]{2,1,0:T(8,128)(2,1)} custom-call(s32[3]{0:T(128)} %pad_add_fusion.refs_0_, bf16[2,512,1024]{2,1,0:T(8,128)(2,1)} %order_tiles.4.refs_3_.refs_1_, bf16[2,512,1024]{2,1,0:T(8,128)(2,1)} %collective-permute-done.refs_2_, bf16[2,1024,1024]{2,1,0:T(8,128)(2,1)} %mask_integrals.1.refs_11_.refs_3_.refs_2_, ...), custom_call_target="tpu_custom_call" | custom-call | flops 999999995904 | bytes 1000000000 | tf_op jit(solution)/shard_map/contract/pallas_call | solution.py:55
  22.4 8.9 %contract_apart.5 = (bf16[1,512,1024]{2,1,0:T(8,128)(2,1)}, bf16[1,512,1024]{2,1,0:T(8,128)(2,1)}) custom-call(bf16[2,512,1024]{2,1,0:T(8,128)(2,1)} %order_tiles.5.refs_4_.refs_0_, bf16[2,512,1024]{2,1,0:T(8,128)(2,1)} %collective-permute-done.1.refs_1_, bf16[2,1024,1024]{2,1,0:T(8,128)(2,1)} %mask_integrals.1.refs_11_.refs_3_.refs_2_, ...), custom_call_target="tpu_custom_call" | custom-call | flops 999999995904 | bytes 1000000000 | tf_op jit(solution)/shard_map/contract_apart/pallas_call | solution.py:55
  31.3 6.6 %contract.5.refs_11_ = bf16[1,512,1024]{2,1,0:T(8,128)(2,1)} custom-call(s32[3]{0:T(128)} %pad_add_fusion.refs_0_, bf16[2,512,1024]{2,1,0:T(8,128)(2,1)} %order_tiles.4.refs_3_.refs_1_, bf16[2,512,1024]{2,1,0:T(8,128)(2,1)} %collective-permute-done.refs_2_, bf16[2,1024,1024]{2,1,0:T(8,128)(2,1)} %mask_integrals.1.refs_11_.refs_3_.refs_2_, ...), custom_call_target="tpu_custom_call" | custom-call | flops 999999995904 | bytes 1000000000 | tf_op jit(solution)/shard_map/contract/pallas_call | solution.py:55
  39.5 5.2 %collective-permute-start.5 = (bf16[1,512,1024]{2,1,0:T(8,128)(2,1)}, bf16[1,512,1024]{2,1,0:T(8,128)(2,1)}, u32[]{:S(2)}, u32[]{:S(2)}) collective-permute-start(bf16[1,512,1024]{2,1,0:T(8,128)(2,1)} %contract.5.refs_11_), channel_id=1, source_target_pairs={{0,12},{4,8},{10,6},{14,2},{1,13},{5,9},{11,7},{15,3},{16,28},{20,... | collective-permute-start | bytes 3145736 | tf_op jit(solution)/shard_map/ppermute | solution.py:304
  46.0 6.1 %order_tiles.6.refs_2_.refs_0_ = bf16[4,512,1024]{2,1,0:T(8,128)(2,1)} custom-call(s32[3]{0:T(128)} %pad_add_fusion.refs_0_, s32[32]{0:T(128)} %refs_1_.9, s32[8,8,32]{2,1,0:T(8,128)} %bitcast.6, bf16[8,2048,512]{2,1,0:T(8,128)(2,1)} %refs_10_.7, bf16[8,2048,512]{2,1,0:T(8,128)(2,1)} %refs_10_.7, bf16[8,2048,512]{2,1,0:T(8,128)(2,1)} %refs_10_.7, ...), custom_call_target="tpu_custom_call" | custom-call | flops 999999995904 | bytes 1000000000 | tf_op jit(solution)/shard_map/order_tiles/pallas_call | solution.py:55
  54.6 16.0 %collective-permute-start.10 = (bf16[1,512,1024]{2,1,0:T(8,128)(2,1)}, bf16[1,512,1024]{2,1,0:T(8,128)(2,1)}, u32[]{:S(2)}, u32[]{:S(2)}) collective-permute-start(bf16[1,512,1024]{2,1,0:T(8,128)(2,1)} %add.12.refs_3_), channel_id=1, source_target_pairs={{0,4},{4,0},{10,14},{14,10},{2,12},{6,8},{8,6},{12,2},{1,5},{5,1},... | collective-permute-start | bytes 3145736 | tf_op jit(solution)/shard_map/ppermute | solution.py:304
  70.7 8.9 %contract_apart.6 = (bf16[1,512,1024]{2,1,0:T(8,128)(2,1)}, bf16[1,512,1024]{2,1,0:T(8,128)(2,1)}) custom-call(bf16[4,512,1024]{2,1,0:T(8,128)(2,1)} %order_tiles.6.refs_2_.refs_0_, bf16[4,512,1024]{2,1,0:T(8,128)(2,1)} %collective-permute-done.2.refs_1_, bf16[2,1024,1024]{2,1,0:T(8,128)(2,1)} %mask_integrals.1.refs_11_.refs_3_.refs_2_, ...), custom_call_target="tpu_custom_call" | custom-call | flops 999999995904 | bytes 1000000000 | tf_op jit(solution)/shard_map/contract_apart/pallas_call | solution.py:55
  80.9 8.9 %contract_apart.7 = (bf16[1,512,1024]{2,1,0:T(8,128)(2,1)}, bf16[1,512,1024]{2,1,0:T(8,128)(2,1)}) custom-call(bf16[4,512,1024]{2,1,0:T(8,128)(2,1)} %order_tiles.6.refs_2_.refs_0_, bf16[4,512,1024]{2,1,0:T(8,128)(2,1)} %collective-permute-done.2.refs_1_, bf16[2,1024,1024]{2,1,0:T(8,128)(2,1)} %mask_integrals.1.refs_11_.refs_3_.refs_2_, ...), custom_call_target="tpu_custom_call" | custom-call | flops 999999995904 | bytes 1000000000 | tf_op jit(solution)/shard_map/contract_apart/pallas_call | solution.py:55
  89.8 10.9 %order_tiles.7.refs_1_.refs_0_ = bf16[8,512,1024]{2,1,0:T(8,128)(2,1)} custom-call(s32[3]{0:T(128)} %pad_add_fusion.refs_0_, s32[32]{0:T(128)} %refs_1_.9, s32[8,8,32]{2,1,0:T(8,128)} %bitcast.7, bf16[8,2048,512]{2,1,0:T(8,128)(2,1)} %refs_10_.7, bf16[8,2048,512]{2,1,0:T(8,128)(2,1)} %refs_10_.7, bf16[8,2048,512]{2,1,0:T(8,128)(2,1)} %refs_10_.7, ...), custom_call_target="tpu_custom_call" | custom-call | flops 999999995904 | bytes 1000000000 | tf_op jit(solution)/shard_map/order_tiles/pallas_call | solution.py:55
  103.2 10.8 %collective-permute-start.11 = (bf16[1,512,1024]{2,1,0:T(8,128)(2,1)}, bf16[1,512,1024]{2,1,0:T(8,128)(2,1)}, u32[]{:S(2)}, u32[]{:S(2)}) collective-permute-start(bf16[1,512,1024]{2,1,0:T(8,128)(2,1)} %add.13.refs_1_), channel_id=1, source_target_pairs={{0,8},{4,12},{10,2},{14,6},{1,9},{5,13},{11,3},{15,7},{16,24},{20,... | collective-permute-start | bytes 3145736 | tf_op jit(solution)/shard_map/ppermute | solution.py:304
  115.2 21.2 %collective-permute-done.9.refs_1_ = bf16[1,512,1024]{2,1,0:T(8,128)(2,1)} collective-permute-done((bf16[1,512,1024]{2,1,0:T(8,128)(2,1)}, bf16[1,512,1024]{2,1,0:T(8,128)(2,1)}, u32[]{:S(2)}, u32[]{:S(2)}) %collective-permute-start.9) | collective-permute-done | bytes 1048608 | tf_op jit(solution)/shard_map/ppermute | solution.py:304
  141.3 9.0 %contract_apart.8 = (bf16[1,512,1024]{2,1,0:T(8,128)(2,1)}, bf16[1,512,1024]{2,1,0:T(8,128)(2,1)}) custom-call(bf16[8,512,1024]{2,1,0:T(8,128)(2,1)} %hand_on.22.refs_1_.refs_0_, bf16[8,512,1024]{2,1,0:T(8,128)(2,1)} %collective-permute-done.7.refs_1_.refs_2_, bf16[2,1024,1024]{2,1,0:T(8,128)(2,1)} %mask_integrals.1.refs_11_.refs_3_.refs_2_, ...), custom_call_target="tpu_custom_call" | custom-call | flops 999999995904 | bytes 1000000000 | tf_op jit(solution)/shard_map/contract_apart/pallas_call | solution.py:55
  151.6 5.1 %collective-permute-done.11.refs_0_ = bf16[1,512,1024]{2,1,0:T(8,128)(2,1)} collective-permute-done((bf16[1,512,1024]{2,1,0:T(8,128)(2,1)}, bf16[1,512,1024]{2,1,0:T(8,128)(2,1)}, u32[]{:S(2)}, u32[]{:S(2)}) %collective-permute-start.11) | collective-permute-done | bytes 1048608 | tf_op jit(solution)/shard_map/ppermute | solution.py:304
  159.1 6.4 %collective-permute-start.17 = (bf16[1,512,1024]{2,1,0:T(8,128)(2,1)}, bf16[1,512,1024]{2,1,0:T(8,128)(2,1)}, u32[]{:S(2)}, u32[]{:S(2)}) collective-permute-start(bf16[1,512,1024]{2,1,0:T(8,128)(2,1)} %add.15.refs_3_), channel_id=1, source_target_pairs={{0,8},{4,12},{10,2},{14,6},{1,9},{5,13},{11,3},{15,7},{16,24},{20,... | collective-permute-start | bytes 3145736 | tf_op jit(solution)/shard_map/ppermute | solution.py:304
  165.5 8.9 %contract_apart.9 = (bf16[1,512,1024]{2,1,0:T(8,128)(2,1)}, bf16[1,512,1024]{2,1,0:T(8,128)(2,1)}) custom-call(bf16[8,512,1024]{2,1,0:T(8,128)(2,1)} %hand_on.22.refs_1_.refs_0_, bf16[8,512,1024]{2,1,0:T(8,128)(2,1)} %collective-permute-done.7.refs_1_.refs_2_, bf16[2,1024,1024]{2,1,0:T(8,128)(2,1)} %mask_integrals.1.refs_11_.refs_3_.refs_2_, ...), custom_call_target="tpu_custom_call" | custom-call | flops 999999995904 | bytes 1000000000 | tf_op jit(solution)/shard_map/contract_apart/pallas_call | solution.py:55
  174.4 11.9 %contract.6.refs_1_.refs_0_ = bf16[3,512,1024]{2,1,0:T(8,128)(2,1)} custom-call(s32[3]{0:T(128)} %pad_add_fusion.refs_0_, bf16[8,512,1024]{2,1,0:T(8,128)(2,1)} %hand_on.22.refs_1_.refs_0_, bf16[8,512,1024]{2,1,0:T(8,128)(2,1)} %collective-permute-done.7.refs_1_.refs_2_, bf16[2,1024,1024]{2,1,0:T(8,128)(2,1)} %mask_integrals.1.refs_11_.refs_3_.refs_2_, ...), custom_call_target="tpu_custom_call" | custom-call | flops 999999995904 | bytes 1000000000 | tf_op jit(solution)/shard_map/contract/pallas_call | solution.py:55
  190.3 6.5 %contract.7.refs_1_.refs_0_ = bf16[1,512,1024]{2,1,0:T(8,128)(2,1)} custom-call(s32[3]{0:T(128)} %pad_add_fusion.refs_0_, bf16[8,512,1024]{2,1,0:T(8,128)(2,1)} %hand_on.22.refs_1_.refs_0_, bf16[8,512,1024]{2,1,0:T(8,128)(2,1)} %collective-permute-done.7.refs_1_.refs_2_, bf16[2,1024,1024]{2,1,0:T(8,128)(2,1)} %mask_integrals.1.refs_11_.refs_3_.refs_2_, ...), custom_call_target="tpu_custom_call" | custom-call | flops 999999995904 | bytes 1000000000 | tf_op jit(solution)/shard_map/contract/pallas_call | solution.py:55
  196.8 9.2 %collective-permute-done.17.refs_0_ = bf16[1,512,1024]{2,1,0:T(8,128)(2,1)} collective-permute-done((bf16[1,512,1024]{2,1,0:T(8,128)(2,1)}, bf16[1,512,1024]{2,1,0:T(8,128)(2,1)}, u32[]{:S(2)}, u32[]{:S(2)}) %collective-permute-start.17) | collective-permute-done | bytes 1048608 | tf_op jit(solution)/shard_map/ppermute | solution.py:304
  217.3 14.2 %collective-permute-done.16.refs_0_ = bf16[1,512,1024]{2,1,0:T(8,128)(2,1)} collective-permute-done((bf16[1,512,1024]{2,1,0:T(8,128)(2,1)}, bf16[1,512,1024]{2,1,0:T(8,128)(2,1)}, u32[]{:S(2)}, u32[]{:S(2)}) %collective-permute-start.16) | collective-permute-done | bytes 1048608 | tf_op jit(solution)/shard_map/ppermute | solution.py:304
  240.9 13.4 %collective-permute-done.19.refs_0_ = bf16[1,512,1024]{2,1,0:T(8,128)(2,1)} collective-permute-done((bf16[1,512,1024]{2,1,0:T(8,128)(2,1)}, bf16[1,512,1024]{2,1,0:T(8,128)(2,1)}, u32[]{:S(2)}, u32[]{:S(2)}) %collective-permute-start.19) | collective-permute-done | bytes 1048608 | tf_op jit(solution)/shard_map/ppermute | solution.py:304
  254.3 25.8 %collective-permute-done.21.refs_2_ = bf16[3,512,1024]{2,1,0:T(8,128)(2,1)} collective-permute-done((bf16[3,512,1024]{2,1,0:T(8,128)(2,1)}, bf16[3,512,1024]{2,1,0:T(8,128)(2,1)}, u32[]{:S(2)}, u32[]{:S(2)}) %collective-permute-start.21) | collective-permute-done | bytes 3145760 | tf_op jit(solution)/shard_map/ppermute | solution.py:304
  280.1 3.8 %place.11.refs_4_ = bf16[8,512,1024]{2,1,0:T(8,128)(2,1)} custom-call(s32[3]{0:T(128)} %pad_add_fusion.refs_0_, bf16[3,512,1024]{2,1,0:T(8,128)(2,1)} %hand_on.31.refs_4_.refs_1_, bf16[3,512,1024]{2,1,0:T(8,128)(2,1)} %collective-permute-done.21.refs_2_, bf16[1,512,1024]{2,1,0:T(8,128)(2,1)} %hand_on.20.refs_1_.refs_3_, ...), custom_call_target="tpu_custom_call", output_to_operand_aliasing={{}: (5, {})} | custom-call | flops 999999995904 | bytes 1000000000 | tf_op jit(solution)/shard_map/place/pallas_call | solution.py:55
  294.0 4.7 %collective-permute-done.18.refs_2_ = bf16[1,512,1024]{2,1,0:T(8,128)(2,1)} collective-permute-done((bf16[1,512,1024]{2,1,0:T(8,128)(2,1)}, bf16[1,512,1024]{2,1,0:T(8,128)(2,1)}, u32[]{:S(2)}, u32[]{:S(2)}) %collective-permute-start.18) | collective-permute-done | bytes 1048608 | tf_op jit(solution)/shard_map/ppermute | solution.py:304
  (68 shorter events, 67.3 us)
Async XLA Ops:
  4.3 10.0 %collective-permute-start = (bf16[2,512,1024]{2,1,0:T(8,128)(2,1)}, bf16[2,512,1024]{2,1,0:T(8,128)(2,1)}, u32[]{:S(2)}, u32[]{:S(2)}) collective-permute-start(bf16[2,512,1024]{2,1,0:T(8,128)(2,1)} %order_tiles.4.refs_3_.refs_1_), channel_id=1, source_target_pairs={{0,1},{1,0},{2,3},{3,2},{4,5},{5,4},{6,7},{7,6},{8,9},{9,8},{10,11... | collective-permute-start | bytes 6291464 | tf_op jit(solution)/shard_map/ppermute | solution.py:325
  13.8 8.5 %collective-permute-start.1 = (bf16[2,512,1024]{2,1,0:T(8,128)(2,1)}, bf16[2,512,1024]{2,1,0:T(8,128)(2,1)}, u32[]{:S(2)}, u32[]{:S(2)}) collective-permute-start(bf16[2,512,1024]{2,1,0:T(8,128)(2,1)} %order_tiles.5.refs_4_.refs_0_), channel_id=1, source_target_pairs={{0,1},{1,0},{2,3},{3,2},{4,5},{5,4},{6,7},{7,6},{8,9},{9,8},{10,11... | collective-permute-start | bytes 6291464 | tf_op jit(solution)/shard_map/ppermute | solution.py:325
  20.9 31.3 %collective-permute-start.3 = (bf16[1,512,1024]{2,1,0:T(8,128)(2,1)}, bf16[1,512,1024]{2,1,0:T(8,128)(2,1)}, u32[]{:S(2)}, u32[]{:S(2)}) collective-permute-start(bf16[1,512,1024]{2,1,0:T(8,128)(2,1)} %contract.4.refs_3_), channel_id=1, source_target_pairs={{2,0},{6,4},{8,10},{12,14},{0,2},{4,6},{10,8},{14,12},{3,1},{7,5},... | collective-permute-start | bytes 3145736 | tf_op jit(solution)/shard_map/ppermute | solution.py:304
  37.9 62.8 %collective-permute-start.6 = (bf16[1,512,1024]{2,1,0:T(8,128)(2,1)}, bf16[1,512,1024]{2,1,0:T(8,128)(2,1)}, u32[]{:S(2)}, u32[]{:S(2)}) collective-permute-start(bf16[1,512,1024]{2,1,0:T(8,128)(2,1)} %contract.5.refs_11_), channel_id=1, source_target_pairs={{2,12},{6,8},{8,6},{12,2},{3,13},{7,9},{9,7},{13,3},{18,28},{22,24... | collective-permute-start | bytes 3145736 | tf_op jit(solution)/shard_map/ppermute | solution.py:304
  39.5 61.2 %collective-permute-start.5 = (bf16[1,512,1024]{2,1,0:T(8,128)(2,1)}, bf16[1,512,1024]{2,1,0:T(8,128)(2,1)}, u32[]{:S(2)}, u32[]{:S(2)}) collective-permute-start(bf16[1,512,1024]{2,1,0:T(8,128)(2,1)} %contract.5.refs_11_), channel_id=1, source_target_pairs={{0,12},{4,8},{10,6},{14,2},{1,13},{5,9},{11,7},{15,3},{16,28},{20,... | collective-permute-start | bytes 3145736 | tf_op jit(solution)/shard_map/ppermute | solution.py:304
  44.7 34.9 %collective-permute-start.4 = (bf16[1,512,1024]{2,1,0:T(8,128)(2,1)}, bf16[1,512,1024]{2,1,0:T(8,128)(2,1)}, u32[]{:S(2)}, u32[]{:S(2)}) collective-permute-start(bf16[1,512,1024]{2,1,0:T(8,128)(2,1)} %get-tuple-element.15.refs_4_.refs_0_), channel_id=1, source_target_pairs={{2,0},{6,4},{8,10},{12,14},{3,1},{7,5},{9,11},{13,15},{18,16},{22,... | collective-permute-start | bytes 3145736 | tf_op jit(solution)/shard_map/ppermute | solution.py:304
  52.1 18.5 %collective-permute-start.2 = (bf16[4,512,1024]{2,1,0:T(8,128)(2,1)}, bf16[4,512,1024]{2,1,0:T(8,128)(2,1)}, u32[]{:S(2)}, u32[]{:S(2)}) collective-permute-start(bf16[4,512,1024]{2,1,0:T(8,128)(2,1)} %order_tiles.6.refs_2_.refs_0_), channel_id=1, source_target_pairs={{0,1},{1,0},{2,3},{3,2},{4,5},{5,4},{6,7},{7,6},{8,9},{9,8},{10,11... | collective-permute-start | bytes 12582920 | tf_op jit(solution)/shard_map/ppermute | solution.py:325
  54.6 60.6 %collective-permute-start.10 = (bf16[1,512,1024]{2,1,0:T(8,128)(2,1)}, bf16[1,512,1024]{2,1,0:T(8,128)(2,1)}, u32[]{:S(2)}, u32[]{:S(2)}) collective-permute-start(bf16[1,512,1024]{2,1,0:T(8,128)(2,1)} %add.12.refs_3_), channel_id=1, source_target_pairs={{0,4},{4,0},{10,14},{14,10},{2,12},{6,8},{8,6},{12,2},{1,5},{5,1},... | collective-permute-start | bytes 3145736 | tf_op jit(solution)/shard_map/ppermute | solution.py:304
  79.6 56.8 %collective-permute-start.9 = (bf16[1,512,1024]{2,1,0:T(8,128)(2,1)}, bf16[1,512,1024]{2,1,0:T(8,128)(2,1)}, u32[]{:S(2)}, u32[]{:S(2)}) collective-permute-start(bf16[1,512,1024]{2,1,0:T(8,128)(2,1)} %get-tuple-element.18.refs_1_), channel_id=1, source_target_pairs={{2,0},{6,4},{8,10},{12,14},{0,2},{4,6},{10,8},{14,12},{3,1},{7,5},... | collective-permute-start | bytes 3145736 | tf_op jit(solution)/shard_map/ppermute | solution.py:304
  79.6 70.7 %collective-permute-start.8 = (bf16[1,512,1024]{2,1,0:T(8,128)(2,1)}, bf16[1,512,1024]{2,1,0:T(8,128)(2,1)}, u32[]{:S(2)}, u32[]{:S(2)}) collective-permute-start(bf16[1,512,1024]{2,1,0:T(8,128)(2,1)} %hand_on.19.refs_3_.refs_0_), channel_id=1, source_target_pairs={{2,0},{6,4},{8,10},{12,14},{3,1},{7,5},{9,11},{13,15},{18,16},{22,... | collective-permute-start | bytes 3145736 | tf_op jit(solution)/shard_map/ppermute | solution.py:304
  103.2 53.4 %collective-permute-start.11 = (bf16[1,512,1024]{2,1,0:T(8,128)(2,1)}, bf16[1,512,1024]{2,1,0:T(8,128)(2,1)}, u32[]{:S(2)}, u32[]{:S(2)}) collective-permute-start(bf16[1,512,1024]{2,1,0:T(8,128)(2,1)} %add.13.refs_1_), channel_id=1, source_target_pairs={{0,8},{4,12},{10,2},{14,6},{1,9},{5,13},{11,3},{15,7},{16,24},{20,... | collective-permute-start | bytes 3145736 | tf_op jit(solution)/shard_map/ppermute | solution.py:304
  114.0 27.3 %collective-permute-start.7 = (bf16[8,512,1024]{2,1,0:T(8,128)(2,1)}, bf16[8,512,1024]{2,1,0:T(8,128)(2,1)}, u32[]{:S(2)}, u32[]{:S(2)}) collective-permute-start(bf16[8,512,1024]{2,1,0:T(8,128)(2,1)} %hand_on.22.refs_1_.refs_0_), channel_id=1, source_target_pairs={{0,1},{1,0},{2,3},{3,2},{4,5},{5,4},{6,7},{7,6},{8,9},{9,8},{10,11... | collective-permute-start | bytes 25165832 | tf_op jit(solution)/shard_map/ppermute | solution.py:325
  138.8 47.5 %collective-permute-start.14 = (bf16[1,512,1024]{2,1,0:T(8,128)(2,1)}, bf16[1,512,1024]{2,1,0:T(8,128)(2,1)}, u32[]{:S(2)}, u32[]{:S(2)}) collective-permute-start(bf16[1,512,1024]{2,1,0:T(8,128)(2,1)} %add.14.refs_1_), channel_id=1, source_target_pairs={{0,4},{4,0},{10,14},{14,10},{2,8},{6,12},{8,2},{12,6},{1,5},{5,1},... | collective-permute-start | bytes 3145736 | tf_op jit(solution)/shard_map/ppermute | solution.py:304
  138.8 47.5 %collective-permute-start.13 = (bf16[1,512,1024]{2,1,0:T(8,128)(2,1)}, bf16[1,512,1024]{2,1,0:T(8,128)(2,1)}, u32[]{:S(2)}, u32[]{:S(2)}) collective-permute-start(bf16[1,512,1024]{2,1,0:T(8,128)(2,1)} %hand_on.24.refs_3_), channel_id=1, source_target_pairs={{2,0},{6,4},{8,10},{12,14},{0,2},{4,6},{10,8},{14,12},{3,1},{7,5},... | collective-permute-start | bytes 3145736 | tf_op jit(solution)/shard_map/ppermute | solution.py:304
  150.3 38.5 %collective-permute-start.12 = (bf16[1,512,1024]{2,1,0:T(8,128)(2,1)}, bf16[1,512,1024]{2,1,0:T(8,128)(2,1)}, u32[]{:S(2)}, u32[]{:S(2)}) collective-permute-start(bf16[1,512,1024]{2,1,0:T(8,128)(2,1)} %hand_on.26.refs_1_.refs_0_), channel_id=1, source_target_pairs={{2,0},{6,4},{8,10},{12,14},{3,1},{7,5},{9,11},{13,15},{18,16},{22,... | collective-permute-start | bytes 3145736 | tf_op jit(solution)/shard_map/ppermute | solution.py:304
  159.1 46.8 %collective-permute-start.17 = (bf16[1,512,1024]{2,1,0:T(8,128)(2,1)}, bf16[1,512,1024]{2,1,0:T(8,128)(2,1)}, u32[]{:S(2)}, u32[]{:S(2)}) collective-permute-start(bf16[1,512,1024]{2,1,0:T(8,128)(2,1)} %add.15.refs_3_), channel_id=1, source_target_pairs={{0,8},{4,12},{10,2},{14,6},{1,9},{5,13},{11,3},{15,7},{16,24},{20,... | collective-permute-start | bytes 3145736 | tf_op jit(solution)/shard_map/ppermute | solution.py:304
  186.3 45.3 %collective-permute-start.15 = (bf16[1,512,1024]{2,1,0:T(8,128)(2,1)}, bf16[1,512,1024]{2,1,0:T(8,128)(2,1)}, u32[]{:S(2)}, u32[]{:S(2)}) collective-permute-start(bf16[1,512,1024]{2,1,0:T(8,128)(2,1)} %hand_on.28.refs_1_), channel_id=1, source_target_pairs={{2,0},{6,4},{8,10},{12,14},{0,2},{4,6},{10,8},{14,12},{3,1},{7,5},... | collective-permute-start | bytes 3145736 | tf_op jit(solution)/shard_map/ppermute | solution.py:304
  188.8 42.8 %collective-permute-start.16 = (bf16[1,512,1024]{2,1,0:T(8,128)(2,1)}, bf16[1,512,1024]{2,1,0:T(8,128)(2,1)}, u32[]{:S(2)}, u32[]{:S(2)}) collective-permute-start(bf16[1,512,1024]{2,1,0:T(8,128)(2,1)} %add.16.refs_1_), channel_id=1, source_target_pairs={{0,4},{4,0},{10,14},{14,10},{2,12},{6,8},{8,6},{12,2},{1,5},{5,1},... | collective-permute-start | bytes 3145736 | tf_op jit(solution)/shard_map/ppermute | solution.py:304
  188.8 91.3 %collective-permute-start.21 = (bf16[3,512,1024]{2,1,0:T(8,128)(2,1)}, bf16[3,512,1024]{2,1,0:T(8,128)(2,1)}, u32[]{:S(2)}, u32[]{:S(2)}) collective-permute-start(bf16[3,512,1024]{2,1,0:T(8,128)(2,1)} %hand_on.31.refs_4_.refs_1_), channel_id=1, source_target_pairs={{2,0},{6,4},{8,10},{12,14},{3,1},{7,5},{9,11},{13,15},{18,16},{22,... | collective-permute-start | bytes 9437192 | tf_op jit(solution)/shard_map/ppermute | solution.py:304
  208.4 45.9 %collective-permute-start.19 = (bf16[1,512,1024]{2,1,0:T(8,128)(2,1)}, bf16[1,512,1024]{2,1,0:T(8,128)(2,1)}, u32[]{:S(2)}, u32[]{:S(2)}) collective-permute-start(bf16[1,512,1024]{2,1,0:T(8,128)(2,1)} %add.17.refs_3_), channel_id=1, source_target_pairs={{0,12},{4,8},{10,6},{14,2},{1,13},{5,9},{11,7},{15,3},{16,28},{20,... | collective-permute-start | bytes 3145736 | tf_op jit(solution)/shard_map/ppermute | solution.py:304
  237.0 61.6 %collective-permute-start.18 = (bf16[1,512,1024]{2,1,0:T(8,128)(2,1)}, bf16[1,512,1024]{2,1,0:T(8,128)(2,1)}, u32[]{:S(2)}, u32[]{:S(2)}) collective-permute-start(bf16[1,512,1024]{2,1,0:T(8,128)(2,1)} %hand_on.34.refs_4_.refs_1_), channel_id=1, source_target_pairs={{2,0},{6,4},{8,10},{12,14},{3,1},{7,5},{9,11},{13,15},{18,16},{22,... | collective-permute-start | bytes 3145736 | tf_op jit(solution)/shard_map/ppermute | solution.py:304
  238.3 52.4 %collective-permute-start.20 = (bf16[1,512,1024]{2,1,0:T(8,128)(2,1)}, bf16[1,512,1024]{2,1,0:T(8,128)(2,1)}, u32[]{:S(2)}, u32[]{:S(2)}) collective-permute-start(bf16[1,512,1024]{2,1,0:T(8,128)(2,1)} %add.18.refs_1_), channel_id=1, source_target_pairs={{0,4},{4,0},{10,14},{14,10},{2,8},{6,12},{8,2},{12,6},{1,5},{5,1},... | collective-permute-start | bytes 3145736 | tf_op jit(solution)/shard_map/ppermute | solution.py:304

commit v5 on v4

--- a/solution.py
+++ b/solution.py
@@ -375,9 +375,9 @@
     far_0 = move(add((home_0, 0), (home_0_in, 0)), to_far(0))
     tiles_d = exchange(chain.hand_on(tiles_d))
 
+    got_2 = move(chain.hand_on(give_2), swap)
     round_0 = chain.hand_on(round_0)
     round_1 = move(add((keep_1, 0), (got_1, 0)), round_pairs(1))
-    got_2 = move(chain.hand_on(give_2), swap)
     home_2, keep_2 = chain.contract_apart(tiles_d, weights, 0, 2)
     home_1_in = chain.hand_on(home_1_in)
     home_2 = chain.hand_on(home_2)

time: 305 us -> 303 us (level)
  waiting for transfers between devices: 94.8 us -> 78.6 us
  starting transfers between devices: 55.9 us -> 71.9 us
    ppermute x18, waiting for transfers between devices: 94.8 us -> 78.6 us  [move(): return lax.ppermute(x, both, pairs)]
    ppermute x18, starting transfers between devices: 55.4 us -> 71.4 us  [move(): return lax.ppermute(x, both, pairs)]
  transfers between devices with their start and end apart: 22 -> 22, of which waited for: 8 -> 8; matrix products, arithmetic and copies ran while one was open for 0% -> 0% of each run, Pallas kernels for 47% -> 48%
where the time goes in v5:
time: 303 us; the launch traced here: 302 us
  Pallas kernels  151 us (50%)
  waiting for transfers between devices  78.6 us (26%)
  starting transfers between devices  71.9 us (24%)
    pallas_call x47, Pallas kernels, call(): pl.pallas_call(body, out_shape=out_shape, grid_spec=pltpu.PrefetchScalarG...  151 us
    ppermute x18, waiting for transfers between devices, move(): return lax.ppermute(x, both, pairs)  78.6 us
    ppermute x18, starting transfers between devices, move(): return lax.ppermute(x, both, pairs)  71.4 us
  transfers between devices with their start and end apart: 22, of which 8 were waited for; matrix products, arithmetic and copies ran while one was open for 0% of the time, Pallas kernels for 48%

profile of v5, /device:TPU:8, one launch (start us, length us, event | category | flops | bytes accessed | tf_op | source)
XLA Modules:
  0.0 301.9 jit_solution(9946194784606963044)
XLA Ops:
  4.3 5.8 %mask_integrals.1.refs_11_.refs_3_.refs_2_ = bf16[2,1024,1024]{2,1,0:T(8,128)(2,1)} custom-call(s32[3]{0:T(128)} %pad_add_fusion.refs_0_, s32[2,16,16]{2,1,0:T(8,128)} %refs_1_.6, bf16[2,1024,1024]{2,1,0:T(8,128)(2,1)} %refs_2_.1, bf16[2,512,1024]{2,1,0:T(8,128)(2,1)} %order_tiles.4.refs_3_.refs_1_), custom_call_target="tpu_custom_call" | custom-call | flops 999999995904 | bytes 1000000000 | tf_op jit(solution)/shard_map/mask_integrals/pallas_call | solution.py:55
  14.3 6.5 %contract.4.refs_3_ = bf16[1,512,1024]{2,1,0:T(8,128)(2,1)} custom-call(s32[3]{0:T(128)} %pad_add_fusion.refs_0_, bf16[2,512,1024]{2,1,0:T(8,128)(2,1)} %order_tiles.4.refs_3_.refs_1_, bf16[2,512,1024]{2,1,0:T(8,128)(2,1)} %collective-permute-done.refs_2_, bf16[2,1024,1024]{2,1,0:T(8,128)(2,1)} %mask_integrals.1.refs_11_.refs_3_.refs_2_, ...), custom_call_target="tpu_custom_call" | custom-call | flops 999999995904 | bytes 1000000000 | tf_op jit(solution)/shard_map/contract/pallas_call | solution.py:55
  22.4 8.9 %contract_apart.5 = (bf16[1,512,1024]{2,1,0:T(8,128)(2,1)}, bf16[1,512,1024]{2,1,0:T(8,128)(2,1)}) custom-call(bf16[2,512,1024]{2,1,0:T(8,128)(2,1)} %order_tiles.5.refs_4_.refs_0_, bf16[2,512,1024]{2,1,0:T(8,128)(2,1)} %collective-permute-done.1.refs_1_, bf16[2,1024,1024]{2,1,0:T(8,128)(2,1)} %mask_integrals.1.refs_11_.refs_3_.refs_2_, ...), custom_call_target="tpu_custom_call" | custom-call | flops 999999995904 | bytes 1000000000 | tf_op jit(solution)/shard_map/contract_apart/pallas_call | solution.py:55
  31.3 6.6 %contract.5.refs_11_ = bf16[1,512,1024]{2,1,0:T(8,128)(2,1)} custom-call(s32[3]{0:T(128)} %pad_add_fusion.refs_0_, bf16[2,512,1024]{2,1,0:T(8,128)(2,1)} %order_tiles.4.refs_3_.refs_1_, bf16[2,512,1024]{2,1,0:T(8,128)(2,1)} %collective-permute-done.refs_2_, bf16[2,1024,1024]{2,1,0:T(8,128)(2,1)} %mask_integrals.1.refs_11_.refs_3_.refs_2_, ...), custom_call_target="tpu_custom_call" | custom-call | flops 999999995904 | bytes 1000000000 | tf_op jit(solution)/shard_map/contract/pallas_call | solution.py:55
  39.6 5.2 %collective-permute-start.5 = (bf16[1,512,1024]{2,1,0:T(8,128)(2,1)}, bf16[1,512,1024]{2,1,0:T(8,128)(2,1)}, u32[]{:S(2)}, u32[]{:S(2)}) collective-permute-start(bf16[1,512,1024]{2,1,0:T(8,128)(2,1)} %contract.5.refs_11_), channel_id=1, source_target_pairs={{0,12},{4,8},{10,6},{14,2},{1,13},{5,9},{11,7},{15,3},{16,28},{20,... | collective-permute-start | bytes 3145736 | tf_op jit(solution)/shard_map/ppermute | solution.py:304
  46.1 6.1 %order_tiles.6.refs_2_.refs_0_ = bf16[4,512,1024]{2,1,0:T(8,128)(2,1)} custom-call(s32[3]{0:T(128)} %pad_add_fusion.refs_0_, s32[32]{0:T(128)} %refs_1_.9, s32[8,8,32]{2,1,0:T(8,128)} %bitcast.6, bf16[8,2048,512]{2,1,0:T(8,128)(2,1)} %refs_10_.7, bf16[8,2048,512]{2,1,0:T(8,128)(2,1)} %refs_10_.7, bf16[8,2048,512]{2,1,0:T(8,128)(2,1)} %refs_10_.7, ...), custom_call_target="tpu_custom_call" | custom-call | flops 999999995904 | bytes 1000000000 | tf_op jit(solution)/shard_map/order_tiles/pallas_call | solution.py:55
  54.7 15.9 %collective-permute-start.10 = (bf16[1,512,1024]{2,1,0:T(8,128)(2,1)}, bf16[1,512,1024]{2,1,0:T(8,128)(2,1)}, u32[]{:S(2)}, u32[]{:S(2)}) collective-permute-start(bf16[1,512,1024]{2,1,0:T(8,128)(2,1)} %add.12.refs_3_), channel_id=1, source_target_pairs={{0,4},{4,0},{10,14},{14,10},{2,12},{6,8},{8,6},{12,2},{1,5},{5,1},... | collective-permute-start | bytes 3145736 | tf_op jit(solution)/shard_map/ppermute | solution.py:304
  70.6 8.9 %contract_apart.6 = (bf16[1,512,1024]{2,1,0:T(8,128)(2,1)}, bf16[1,512,1024]{2,1,0:T(8,128)(2,1)}) custom-call(bf16[4,512,1024]{2,1,0:T(8,128)(2,1)} %order_tiles.6.refs_2_.refs_0_, bf16[4,512,1024]{2,1,0:T(8,128)(2,1)} %collective-permute-done.2.refs_1_, bf16[2,1024,1024]{2,1,0:T(8,128)(2,1)} %mask_integrals.1.refs_11_.refs_3_.refs_2_, ...), custom_call_target="tpu_custom_call" | custom-call | flops 999999995904 | bytes 1000000000 | tf_op jit(solution)/shard_map/contract_apart/pallas_call | solution.py:55
  80.9 9.0 %contract_apart.7 = (bf16[1,512,1024]{2,1,0:T(8,128)(2,1)}, bf16[1,512,1024]{2,1,0:T(8,128)(2,1)}) custom-call(bf16[4,512,1024]{2,1,0:T(8,128)(2,1)} %order_tiles.6.refs_2_.refs_0_, bf16[4,512,1024]{2,1,0:T(8,128)(2,1)} %collective-permute-done.2.refs_1_, bf16[2,1024,1024]{2,1,0:T(8,128)(2,1)} %mask_integrals.1.refs_11_.refs_3_.refs_2_, ...), custom_call_target="tpu_custom_call" | custom-call | flops 999999995904 | bytes 1000000000 | tf_op jit(solution)/shard_map/contract_apart/pallas_call | solution.py:55
  89.9 10.9 %order_tiles.7.refs_1_.refs_0_ = bf16[8,512,1024]{2,1,0:T(8,128)(2,1)} custom-call(s32[3]{0:T(128)} %pad_add_fusion.refs_0_, s32[32]{0:T(128)} %refs_1_.9, s32[8,8,32]{2,1,0:T(8,128)} %bitcast.7, bf16[8,2048,512]{2,1,0:T(8,128)(2,1)} %refs_10_.7, bf16[8,2048,512]{2,1,0:T(8,128)(2,1)} %refs_10_.7, bf16[8,2048,512]{2,1,0:T(8,128)(2,1)} %refs_10_.7, ...), custom_call_target="tpu_custom_call" | custom-call | flops 999999995904 | bytes 1000000000 | tf_op jit(solution)/shard_map/order_tiles/pallas_call | solution.py:55
  103.2 10.7 %collective-permute-start.11 = (bf16[1,512,1024]{2,1,0:T(8,128)(2,1)}, bf16[1,512,1024]{2,1,0:T(8,128)(2,1)}, u32[]{:S(2)}, u32[]{:S(2)}) collective-permute-start(bf16[1,512,1024]{2,1,0:T(8,128)(2,1)} %add.13.refs_1_), channel_id=1, source_target_pairs={{0,8},{4,12},{10,2},{14,6},{1,9},{5,13},{11,3},{15,7},{16,24},{20,... | collective-permute-start | bytes 3145736 | tf_op jit(solution)/shard_map/ppermute | solution.py:304
  115.2 18.7 %collective-permute-start.13 = (bf16[1,512,1024]{2,1,0:T(8,128)(2,1)}, bf16[1,512,1024]{2,1,0:T(8,128)(2,1)}, u32[]{:S(2)}, u32[]{:S(2)}) collective-permute-start(bf16[1,512,1024]{2,1,0:T(8,128)(2,1)} %hand_on.23.refs_1_), channel_id=1, source_target_pairs={{2,0},{6,4},{8,10},{12,14},{0,2},{4,6},{10,8},{14,12},{3,1},{7,5},... | collective-permute-start | bytes 3145736 | tf_op jit(solution)/shard_map/ppermute | solution.py:304
  133.9 4.4 %collective-permute-done.9.refs_1_ = bf16[1,512,1024]{2,1,0:T(8,128)(2,1)} collective-permute-done((bf16[1,512,1024]{2,1,0:T(8,128)(2,1)}, bf16[1,512,1024]{2,1,0:T(8,128)(2,1)}, u32[]{:S(2)}, u32[]{:S(2)}) %collective-permute-start.9) | collective-permute-done | bytes 1048608 | tf_op jit(solution)/shard_map/ppermute | solution.py:304
  140.8 8.9 %contract_apart.8 = (bf16[1,512,1024]{2,1,0:T(8,128)(2,1)}, bf16[1,512,1024]{2,1,0:T(8,128)(2,1)}) custom-call(bf16[8,512,1024]{2,1,0:T(8,128)(2,1)} %hand_on.22.refs_1_.refs_0_, bf16[8,512,1024]{2,1,0:T(8,128)(2,1)} %collective-permute-done.7.refs_1_.refs_2_, bf16[2,1024,1024]{2,1,0:T(8,128)(2,1)} %mask_integrals.1.refs_11_.refs_3_.refs_2_, ...), custom_call_target="tpu_custom_call" | custom-call | flops 999999995904 | bytes 1000000000 | tf_op jit(solution)/shard_map/contract_apart/pallas_call | solution.py:55
  151.0 5.6 %collective-permute-done.11.refs_0_ = bf16[1,512,1024]{2,1,0:T(8,128)(2,1)} collective-permute-done((bf16[1,512,1024]{2,1,0:T(8,128)(2,1)}, bf16[1,512,1024]{2,1,0:T(8,128)(2,1)}, u32[]{:S(2)}, u32[]{:S(2)}) %collective-permute-start.11) | collective-permute-done | bytes 1048608 | tf_op jit(solution)/shard_map/ppermute | solution.py:304
  159.1 6.2 %collective-permute-start.17 = (bf16[1,512,1024]{2,1,0:T(8,128)(2,1)}, bf16[1,512,1024]{2,1,0:T(8,128)(2,1)}, u32[]{:S(2)}, u32[]{:S(2)}) collective-permute-start(bf16[1,512,1024]{2,1,0:T(8,128)(2,1)} %add.15.refs_3_), channel_id=1, source_target_pairs={{0,8},{4,12},{10,2},{14,6},{1,9},{5,13},{11,3},{15,7},{16,24},{20,... | collective-permute-start | bytes 3145736 | tf_op jit(solution)/shard_map/ppermute | solution.py:304
  165.3 8.9 %contract_apart.9 = (bf16[1,512,1024]{2,1,0:T(8,128)(2,1)}, bf16[1,512,1024]{2,1,0:T(8,128)(2,1)}) custom-call(bf16[8,512,1024]{2,1,0:T(8,128)(2,1)} %hand_on.22.refs_1_.refs_0_, bf16[8,512,1024]{2,1,0:T(8,128)(2,1)} %collective-permute-done.7.refs_1_.refs_2_, bf16[2,1024,1024]{2,1,0:T(8,128)(2,1)} %mask_integrals.1.refs_11_.refs_3_.refs_2_, ...), custom_call_target="tpu_custom_call" | custom-call | flops 999999995904 | bytes 1000000000 | tf_op jit(solution)/shard_map/contract_apart/pallas_call | solution.py:55
  174.2 11.9 %contract.6.refs_1_.refs_0_ = bf16[3,512,1024]{2,1,0:T(8,128)(2,1)} custom-call(s32[3]{0:T(128)} %pad_add_fusion.refs_0_, bf16[8,512,1024]{2,1,0:T(8,128)(2,1)} %hand_on.22.refs_1_.refs_0_, bf16[8,512,1024]{2,1,0:T(8,128)(2,1)} %collective-permute-done.7.refs_1_.refs_2_, bf16[2,1024,1024]{2,1,0:T(8,128)(2,1)} %mask_integrals.1.refs_11_.refs_3_.refs_2_, ...), custom_call_target="tpu_custom_call" | custom-call | flops 999999995904 | bytes 1000000000 | tf_op jit(solution)/shard_map/contract/pallas_call | solution.py:55
  190.1 6.5 %contract.7.refs_1_.refs_0_ = bf16[1,512,1024]{2,1,0:T(8,128)(2,1)} custom-call(s32[3]{0:T(128)} %pad_add_fusion.refs_0_, bf16[8,512,1024]{2,1,0:T(8,128)(2,1)} %hand_on.22.refs_1_.refs_0_, bf16[8,512,1024]{2,1,0:T(8,128)(2,1)} %collective-permute-done.7.refs_1_.refs_2_, bf16[2,1024,1024]{2,1,0:T(8,128)(2,1)} %mask_integrals.1.refs_11_.refs_3_.refs_2_, ...), custom_call_target="tpu_custom_call" | custom-call | flops 999999995904 | bytes 1000000000 | tf_op jit(solution)/shard_map/contract/pallas_call | solution.py:55
  196.7 8.3 %collective-permute-done.17.refs_0_ = bf16[1,512,1024]{2,1,0:T(8,128)(2,1)} collective-permute-done((bf16[1,512,1024]{2,1,0:T(8,128)(2,1)}, bf16[1,512,1024]{2,1,0:T(8,128)(2,1)}, u32[]{:S(2)}, u32[]{:S(2)}) %collective-permute-start.17) | collective-permute-done | bytes 1048608 | tf_op jit(solution)/shard_map/ppermute | solution.py:304
  216.1 15.3 %collective-permute-done.16.refs_0_ = bf16[1,512,1024]{2,1,0:T(8,128)(2,1)} collective-permute-done((bf16[1,512,1024]{2,1,0:T(8,128)(2,1)}, bf16[1,512,1024]{2,1,0:T(8,128)(2,1)}, u32[]{:S(2)}, u32[]{:S(2)}) %collective-permute-start.16) | collective-permute-done | bytes 1048608 | tf_op jit(solution)/shard_map/ppermute | solution.py:304
  240.7 11.8 %collective-permute-done.19.refs_0_ = bf16[1,512,1024]{2,1,0:T(8,128)(2,1)} collective-permute-done((bf16[1,512,1024]{2,1,0:T(8,128)(2,1)}, bf16[1,512,1024]{2,1,0:T(8,128)(2,1)}, u32[]{:S(2)}, u32[]{:S(2)}) %collective-permute-start.19) | collective-permute-done | bytes 1048608 | tf_op jit(solution)/shard_map/ppermute | solution.py:304
  252.6 27.3 %collective-permute-done.21.refs_2_ = bf16[3,512,1024]{2,1,0:T(8,128)(2,1)} collective-permute-done((bf16[3,512,1024]{2,1,0:T(8,128)(2,1)}, bf16[3,512,1024]{2,1,0:T(8,128)(2,1)}, u32[]{:S(2)}, u32[]{:S(2)}) %collective-permute-start.21) | collective-permute-done | bytes 3145760 | tf_op jit(solution)/shard_map/ppermute | solution.py:304
  293.8 4.7 %collective-permute-done.18.refs_2_ = bf16[1,512,1024]{2,1,0:T(8,128)(2,1)} collective-permute-done((bf16[1,512,1024]{2,1,0:T(8,128)(2,1)}, bf16[1,512,1024]{2,1,0:T(8,128)(2,1)}, u32[]{:S(2)}, u32[]{:S(2)}) %collective-permute-start.18) | collective-permute-done | bytes 1048608 | tf_op jit(solution)/shard_map/ppermute | solution.py:304
  (68 shorter events, 68.7 us)
Async XLA Ops:
  4.3 10.0 %collective-permute-start = (bf16[2,512,1024]{2,1,0:T(8,128)(2,1)}, bf16[2,512,1024]{2,1,0:T(8,128)(2,1)}, u32[]{:S(2)}, u32[]{:S(2)}) collective-permute-start(bf16[2,512,1024]{2,1,0:T(8,128)(2,1)} %order_tiles.4.refs_3_.refs_1_), channel_id=1, source_target_pairs={{0,1},{1,0},{2,3},{3,2},{4,5},{5,4},{6,7},{7,6},{8,9},{9,8},{10,11... | collective-permute-start | bytes 6291464 | tf_op jit(solution)/shard_map/ppermute | solution.py:325
  13.8 8.5 %collective-permute-start.1 = (bf16[2,512,1024]{2,1,0:T(8,128)(2,1)}, bf16[2,512,1024]{2,1,0:T(8,128)(2,1)}, u32[]{:S(2)}, u32[]{:S(2)}) collective-permute-start(bf16[2,512,1024]{2,1,0:T(8,128)(2,1)} %order_tiles.5.refs_4_.refs_0_), channel_id=1, source_target_pairs={{0,1},{1,0},{2,3},{3,2},{4,5},{5,4},{6,7},{7,6},{8,9},{9,8},{10,11... | collective-permute-start | bytes 6291464 | tf_op jit(solution)/shard_map/ppermute | solution.py:325
  20.9 31.4 %collective-permute-start.3 = (bf16[1,512,1024]{2,1,0:T(8,128)(2,1)}, bf16[1,512,1024]{2,1,0:T(8,128)(2,1)}, u32[]{:S(2)}, u32[]{:S(2)}) collective-permute-start(bf16[1,512,1024]{2,1,0:T(8,128)(2,1)} %contract.4.refs_3_), channel_id=1, source_target_pairs={{2,0},{6,4},{8,10},{12,14},{0,2},{4,6},{10,8},{14,12},{3,1},{7,5},... | collective-permute-start | bytes 3145736 | tf_op jit(solution)/shard_map/ppermute | solution.py:304
  37.9 62.8 %collective-permute-start.6 = (bf16[1,512,1024]{2,1,0:T(8,128)(2,1)}, bf16[1,512,1024]{2,1,0:T(8,128)(2,1)}, u32[]{:S(2)}, u32[]{:S(2)}) collective-permute-start(bf16[1,512,1024]{2,1,0:T(8,128)(2,1)} %contract.5.refs_11_), channel_id=1, source_target_pairs={{2,12},{6,8},{8,6},{12,2},{3,13},{7,9},{9,7},{13,3},{18,28},{22,24... | collective-permute-start | bytes 3145736 | tf_op jit(solution)/shard_map/ppermute | solution.py:304
  39.6 61.1 %collective-permute-start.5 = (bf16[1,512,1024]{2,1,0:T(8,128)(2,1)}, bf16[1,512,1024]{2,1,0:T(8,128)(2,1)}, u32[]{:S(2)}, u32[]{:S(2)}) collective-permute-start(bf16[1,512,1024]{2,1,0:T(8,128)(2,1)} %contract.5.refs_11_), channel_id=1, source_target_pairs={{0,12},{4,8},{10,6},{14,2},{1,13},{5,9},{11,7},{15,3},{16,28},{20,... | collective-permute-start | bytes 3145736 | tf_op jit(solution)/shard_map/ppermute | solution.py:304
  44.8 34.8 %collective-permute-start.4 = (bf16[1,512,1024]{2,1,0:T(8,128)(2,1)}, bf16[1,512,1024]{2,1,0:T(8,128)(2,1)}, u32[]{:S(2)}, u32[]{:S(2)}) collective-permute-start(bf16[1,512,1024]{2,1,0:T(8,128)(2,1)} %get-tuple-element.15.refs_4_.refs_0_), channel_id=1, source_target_pairs={{2,0},{6,4},{8,10},{12,14},{3,1},{7,5},{9,11},{13,15},{18,16},{22,... | collective-permute-start | bytes 3145736 | tf_op jit(solution)/shard_map/ppermute | solution.py:304
  52.2 18.4 %collective-permute-start.2 = (bf16[4,512,1024]{2,1,0:T(8,128)(2,1)}, bf16[4,512,1024]{2,1,0:T(8,128)(2,1)}, u32[]{:S(2)}, u32[]{:S(2)}) collective-permute-start(bf16[4,512,1024]{2,1,0:T(8,128)(2,1)} %order_tiles.6.refs_2_.refs_0_), channel_id=1, source_target_pairs={{0,1},{1,0},{2,3},{3,2},{4,5},{5,4},{6,7},{7,6},{8,9},{9,8},{10,11... | collective-permute-start | bytes 12582920 | tf_op jit(solution)/shard_map/ppermute | solution.py:325
  54.7 60.5 %collective-permute-start.10 = (bf16[1,512,1024]{2,1,0:T(8,128)(2,1)}, bf16[1,512,1024]{2,1,0:T(8,128)(2,1)}, u32[]{:S(2)}, u32[]{:S(2)}) collective-permute-start(bf16[1,512,1024]{2,1,0:T(8,128)(2,1)} %add.12.refs_3_), channel_id=1, source_target_pairs={{0,4},{4,0},{10,14},{14,10},{2,12},{6,8},{8,6},{12,2},{1,5},{5,1},... | collective-permute-start | bytes 3145736 | tf_op jit(solution)/shard_map/ppermute | solution.py:304
  79.6 58.7 %collective-permute-start.9 = (bf16[1,512,1024]{2,1,0:T(8,128)(2,1)}, bf16[1,512,1024]{2,1,0:T(8,128)(2,1)}, u32[]{:S(2)}, u32[]{:S(2)}) collective-permute-start(bf16[1,512,1024]{2,1,0:T(8,128)(2,1)} %get-tuple-element.18.refs_1_), channel_id=1, source_target_pairs={{2,0},{6,4},{8,10},{12,14},{0,2},{4,6},{10,8},{14,12},{3,1},{7,5},... | collective-permute-start | bytes 3145736 | tf_op jit(solution)/shard_map/ppermute | solution.py:304
  79.6 70.1 %collective-permute-start.8 = (bf16[1,512,1024]{2,1,0:T(8,128)(2,1)}, bf16[1,512,1024]{2,1,0:T(8,128)(2,1)}, u32[]{:S(2)}, u32[]{:S(2)}) collective-permute-start(bf16[1,512,1024]{2,1,0:T(8,128)(2,1)} %hand_on.19.refs_3_.refs_0_), channel_id=1, source_target_pairs={{2,0},{6,4},{8,10},{12,14},{3,1},{7,5},{9,11},{13,15},{18,16},{22,... | collective-permute-start | bytes 3145736 | tf_op jit(solution)/shard_map/ppermute | solution.py:304
  103.2 53.4 %collective-permute-start.11 = (bf16[1,512,1024]{2,1,0:T(8,128)(2,1)}, bf16[1,512,1024]{2,1,0:T(8,128)(2,1)}, u32[]{:S(2)}, u32[]{:S(2)}) collective-permute-start(bf16[1,512,1024]{2,1,0:T(8,128)(2,1)} %add.13.refs_1_), channel_id=1, source_target_pairs={{0,8},{4,12},{10,2},{14,6},{1,9},{5,13},{11,3},{15,7},{16,24},{20,... | collective-permute-start | bytes 3145736 | tf_op jit(solution)/shard_map/ppermute | solution.py:304
  113.9 26.9 %collective-permute-start.7 = (bf16[8,512,1024]{2,1,0:T(8,128)(2,1)}, bf16[8,512,1024]{2,1,0:T(8,128)(2,1)}, u32[]{:S(2)}, u32[]{:S(2)}) collective-permute-start(bf16[8,512,1024]{2,1,0:T(8,128)(2,1)} %hand_on.22.refs_1_.refs_0_), channel_id=1, source_target_pairs={{0,1},{1,0},{2,3},{3,2},{4,5},{5,4},{6,7},{7,6},{8,9},{9,8},{10,11... | collective-permute-start | bytes 25165832 | tf_op jit(solution)/shard_map/ppermute | solution.py:325
  115.2 70.9 %collective-permute-start.13 = (bf16[1,512,1024]{2,1,0:T(8,128)(2,1)}, bf16[1,512,1024]{2,1,0:T(8,128)(2,1)}, u32[]{:S(2)}, u32[]{:S(2)}) collective-permute-start(bf16[1,512,1024]{2,1,0:T(8,128)(2,1)} %hand_on.23.refs_1_), channel_id=1, source_target_pairs={{2,0},{6,4},{8,10},{12,14},{0,2},{4,6},{10,8},{14,12},{3,1},{7,5},... | collective-permute-start | bytes 3145736 | tf_op jit(solution)/shard_map/ppermute | solution.py:304
  140.8 45.3 %collective-permute-start.14 = (bf16[1,512,1024]{2,1,0:T(8,128)(2,1)}, bf16[1,512,1024]{2,1,0:T(8,128)(2,1)}, u32[]{:S(2)}, u32[]{:S(2)}) collective-permute-start(bf16[1,512,1024]{2,1,0:T(8,128)(2,1)} %add.14.refs_3_), channel_id=1, source_target_pairs={{0,4},{4,0},{10,14},{14,10},{2,8},{6,12},{8,2},{12,6},{1,5},{5,1},... | collective-permute-start | bytes 3145736 | tf_op jit(solution)/shard_map/ppermute | solution.py:304
  149.7 38.9 %collective-permute-start.12 = (bf16[1,512,1024]{2,1,0:T(8,128)(2,1)}, bf16[1,512,1024]{2,1,0:T(8,128)(2,1)}, u32[]{:S(2)}, u32[]{:S(2)}) collective-permute-start(bf16[1,512,1024]{2,1,0:T(8,128)(2,1)} %hand_on.26.refs_1_.refs_0_), channel_id=1, source_target_pairs={{2,0},{6,4},{8,10},{12,14},{3,1},{7,5},{9,11},{13,15},{18,16},{22,... | collective-permute-start | bytes 3145736 | tf_op jit(solution)/shard_map/ppermute | solution.py:304
  159.1 45.9 %collective-permute-start.17 = (bf16[1,512,1024]{2,1,0:T(8,128)(2,1)}, bf16[1,512,1024]{2,1,0:T(8,128)(2,1)}, u32[]{:S(2)}, u32[]{:S(2)}) collective-permute-start(bf16[1,512,1024]{2,1,0:T(8,128)(2,1)} %add.15.refs_3_), channel_id=1, source_target_pairs={{0,8},{4,12},{10,2},{14,6},{1,9},{5,13},{11,3},{15,7},{16,24},{20,... | collective-permute-start | bytes 3145736 | tf_op jit(solution)/shard_map/ppermute | solution.py:304
  186.1 45.3 %collective-permute-start.15 = (bf16[1,512,1024]{2,1,0:T(8,128)(2,1)}, bf16[1,512,1024]{2,1,0:T(8,128)(2,1)}, u32[]{:S(2)}, u32[]{:S(2)}) collective-permute-start(bf16[1,512,1024]{2,1,0:T(8,128)(2,1)} %hand_on.28.refs_1_), channel_id=1, source_target_pairs={{2,0},{6,4},{8,10},{12,14},{0,2},{4,6},{10,8},{14,12},{3,1},{7,5},... | collective-permute-start | bytes 3145736 | tf_op jit(solution)/shard_map/ppermute | solution.py:304
  188.6 42.8 %collective-permute-start.16 = (bf16[1,512,1024]{2,1,0:T(8,128)(2,1)}, bf16[1,512,1024]{2,1,0:T(8,128)(2,1)}, u32[]{:S(2)}, u32[]{:S(2)}) collective-permute-start(bf16[1,512,1024]{2,1,0:T(8,128)(2,1)} %add.16.refs_1_), channel_id=1, source_target_pairs={{0,4},{4,0},{10,14},{14,10},{2,12},{6,8},{8,6},{12,2},{1,5},{5,1},... | collective-permute-start | bytes 3145736 | tf_op jit(solution)/shard_map/ppermute | solution.py:304
  188.7 91.2 %collective-permute-start.21 = (bf16[3,512,1024]{2,1,0:T(8,128)(2,1)}, bf16[3,512,1024]{2,1,0:T(8,128)(2,1)}, u32[]{:S(2)}, u32[]{:S(2)}) collective-permute-start(bf16[3,512,1024]{2,1,0:T(8,128)(2,1)} %hand_on.31.refs_4_.refs_1_), channel_id=1, source_target_pairs={{2,0},{6,4},{8,10},{12,14},{3,1},{7,5},{9,11},{13,15},{18,16},{22,... | collective-permute-start | bytes 9437192 | tf_op jit(solution)/shard_map/ppermute | solution.py:304
  207.4 45.2 %collective-permute-start.19 = (bf16[1,512,1024]{2,1,0:T(8,128)(2,1)}, bf16[1,512,1024]{2,1,0:T(8,128)(2,1)}, u32[]{:S(2)}, u32[]{:S(2)}) collective-permute-start(bf16[1,512,1024]{2,1,0:T(8,128)(2,1)} %add.17.refs_3_), channel_id=1, source_target_pairs={{0,12},{4,8},{10,6},{14,2},{1,13},{5,9},{11,7},{15,3},{16,28},{20,... | collective-permute-start | bytes 3145736 | tf_op jit(solution)/shard_map/ppermute | solution.py:304
  236.9 61.6 %collective-permute-start.18 = (bf16[1,512,1024]{2,1,0:T(8,128)(2,1)}, bf16[1,512,1024]{2,1,0:T(8,128)(2,1)}, u32[]{:S(2)}, u32[]{:S(2)}) collective-permute-start(bf16[1,512,1024]{2,1,0:T(8,128)(2,1)} %hand_on.34.refs_4_.refs_1_), channel_id=1, source_target_pairs={{2,0},{6,4},{8,10},{12,14},{3,1},{7,5},{9,11},{13,15},{18,16},{22,... | collective-permute-start | bytes 3145736 | tf_op jit(solution)/shard_map/ppermute | solution.py:304
  238.2 52.4 %collective-permute-start.20 = (bf16[1,512,1024]{2,1,0:T(8,128)(2,1)}, bf16[1,512,1024]{2,1,0:T(8,128)(2,1)}, u32[]{:S(2)}, u32[]{:S(2)}) collective-permute-start(bf16[1,512,1024]{2,1,0:T(8,128)(2,1)} %add.18.refs_1_), channel_id=1, source_target_pairs={{0,4},{4,0},{10,14},{14,10},{2,8},{6,12},{8,2},{12,6},{1,5},{5,1},... | collective-permute-start | bytes 3145736 | tf_op jit(solution)/shard_map/ppermute | solution.py:304
